TPU v7x, 32 devices: a whole 2x2x4 slice. The times are simulated.
32 devices in a mesh: batch: 8 (over z, y), expert: 4 (over x, core).
Axes of the slice: x: 2, y: 2, z: 4, core: 2. Of those that a mesh axis runs over, the one named last changes fastest.
Arguments:
- tokens: bfloat16 [4096, 768], P(('batch', 'expert')), may hold values from -6 to 6
- cond: bfloat16 [32, 768], P(('batch', 'expert')), may hold values from -6 to 6
- lengths: int32 [32], P(('batch', 'expert')), may hold values from 32 to 128, as said below
- routes: int32 [4096, 2], P(('batch', 'expert')), may hold values from 0 to 3, all different within a row
- gate_weights: float32 [4096, 2], P(('batch', 'expert')), may hold values from 0.2 to 1
- ada_weight: bfloat16 [768, 4608], P(('batch', 'expert')), may hold values from -0.21875 to 0.21875
- ada_bias: bfloat16 [4608], P(('batch', 'expert')), may hold values from -3 to 3
- qkv_weight: bfloat16 [768, 2304], P(('batch', 'expert')), may hold values from -0.21875 to 0.21875
- out_weight: bfloat16 [768, 768], P(('batch', 'expert')), may hold values from -0.875 to 0.875
- shared_up: bfloat16 [768, 3072], P(('batch', 'expert')), may hold values from -0.21875 to 0.21875
- shared_down: bfloat16 [3072, 768], P(('batch', 'expert')), may hold values from -0.109375 to 0.109375
- expert_up: bfloat16 [4, 768, 3072], P('expert', 'batch'), may hold values from -0.21875 to 0.21875
- expert_down: bfloat16 [4, 3072, 768], P('expert', 'batch'), may hold values from -0.109375 to 0.109375
- cotangent: bfloat16 [4096, 768], P(('batch', 'expert')), may hold values from -6 to 6
Outputs:
- block_out: float32 [4096, 768], P(('batch', 'expert'))
- grad_tokens: float32 [4096, 768], P(('batch', 'expert'))
- grad_cond: float32 [32, 768], P(('batch', 'expert'))
- grad_gate_weights: float32 [4096, 2], P(('batch', 'expert'))
- grad_ada_weight: float32 [768, 4608], P('batch', 'expert')
- grad_ada_bias: float32 [4608], replicated
- grad_qkv_weight: float32 [768, 2304], P('batch', 'expert')
- grad_out_weight: float32 [768, 768], P('batch', 'expert')
- grad_shared_up: float32 [768, 3072], P('batch', 'expert')
- grad_shared_down: float32 [3072, 768], P('batch', 'expert')
- grad_expert_up: float32 [4, 768, 3072], P('expert', 'batch')
- grad_expert_down: float32 [4, 3072, 768], P('expert', 'batch')
- expert_load: float32 [4], replicated
Inputs may be any that keep to these rules, and one draw needn't show every extreme that they name: `lengths`: every item holds 128 or 32 valid patches at its start; both occur in every draw. `routes`: the two experts of a patch slot differ.
All inputs are finite; a program needn't handle non-finite values.
Results may differ from a plain program's by a relative error of at most 0.017.
The roundings to bfloat16 on the way count: a program that leaves them out, or rounds other values in their place, can miss the bound.
Values may be sent and summed in bfloat16 or wider, within the bound.
No kernel may reach another device: no remote copies, remote signals or barrier semaphores. Data moves between devices by JAX's collectives and lax.ppermute only.
A program may use at most 128 MiB of HBM per device.

v0:
```python
import functools

import jax
import jax.numpy as jnp
import numpy as np
from jax import lax
from jax.experimental import pallas as pl
from jax.experimental.pallas import tpu as pltpu
from jax.sharding import PartitionSpec as P

HEADS = 12
HEAD_DIM = 64
AXES = ("batch", "expert")
LOW = jnp.bfloat16
WIDE = jnp.float32
LANES = 128
EXTRA = 16
CURVE = 0.7978845608028654
CUBIC = 0.044715


def dot(left, right):
    return lax.dot_general(left, right, (((1,), (0,)), ((), ())), preferred_element_type=WIDE)


def dot_nt(left, right):
    return lax.dot_general(left, right, (((1,), (1,)), ((), ())), preferred_element_type=WIDE)


def dot_tn(left, right):
    return lax.dot_general(left, right, (((0,), (0,)), ((), ())), preferred_element_type=WIDE)


def up_to(value, step):
    return -(-value // step) * step


def call(body, outs, args, scratch=(), smem=(), limit=48):
    specs = [pl.BlockSpec(memory_space=pltpu.SMEM) if at in smem else pl.BlockSpec() for at in range(len(args))]
    return pl.pallas_call(
        body,
        out_shape=[jax.ShapeDtypeStruct(shape, kind) for shape, kind in outs],
        in_specs=specs,
        out_specs=[pl.BlockSpec()] * len(outs),
        scratch_shapes=[pltpu.VMEM(shape, kind) for shape, kind in scratch],
        compiler_params=pltpu.CompilerParams(vmem_limit_bytes=limit * 1024 * 1024),
    )(*args)


def sweep(body, steps, ins, outs, scratch=(), limit=56):
    return pl.pallas_call(
        body,
        out_shape=[jax.ShapeDtypeStruct(shape, kind) for shape, kind, _, _ in outs],
        grid=(steps,),
        in_specs=[
            pl.BlockSpec(memory_space=pltpu.SMEM) if block is None else pl.BlockSpec(block, index)
            for _, block, index in ins
        ],
        out_specs=[pl.BlockSpec(block, index) for _, _, block, index in outs],
        scratch_shapes=[pltpu.VMEM(shape, kind) for shape, kind in scratch],
        compiler_params=pltpu.CompilerParams(vmem_limit_bytes=limit * 1024 * 1024),
    )(*[array for array, _, _ in ins])


def pad_lanes(values, width):
    return jnp.pad(values, ((0, 0),) * (values.ndim - 1) + ((0, width - values.shape[-1]),))


def tie(values, *others):
    return lax.optimization_barrier((values, *others))[0]


def together(*values):
    leaves, tree = jax.tree.flatten(values)
    return jax.tree.unflatten(tree, lax.optimization_barrier(tuple(leaves)))


def grown(values, got):
    return jnp.concatenate([values, got], axis=0)


def added(low, got):
    half = ((low.shape[0] // 2,) + low.shape[1:], low.dtype)
    return call(add_body, [half, half], (low, got))


def bits_of(count):
    found = []
    step = 1
    while step < count:
        found.append(step)
        step *= 2
    assert step == count
    return found


def swap(values, mask):
    total = lax.axis_size("batch") * lax.axis_size("expert")
    return lax.ppermute(values, AXES, [(at, at ^ mask) for at in range(total)])


def spread(values, masks, waits=()):
    waits = dict(waits)
    for at, mask in enumerate(masks):
        if at in waits:
            values = tie(values, *waits[at])
        values = jnp.concatenate([values, swap(values, mask)], axis=0)
    return values


def order(masks):
    found = [0]
    for mask in masks:
        found = found + [at ^ mask for at in found]
    return found


def add_body(low, got, keep, send):
    half = keep.shape[0]
    keep[...] = (low[:half].astype(WIDE) + got[:half].astype(WIDE)).astype(keep.dtype)
    send[...] = (low[half:].astype(WIDE) + got[half:].astype(WIDE)).astype(send.dtype)


def fold(lows, highs, orders, waits=()):
    waits = dict(waits)
    lows, highs, sent = list(lows), list(highs), []
    for at in range(len(orders[0]) - 1):
        sent.append(list(highs))
        got = [swap(high, links[-1 - at]) for high, links in zip(highs, orders)]
        if at in waits:
            got = tie(tuple(got), *waits[at])
        for part, other in enumerate(got):
            half = ((other.shape[0] // 2,) + other.shape[1:], other.dtype)
            lows[part], highs[part] = call(add_body, [half, half], (lows[part], other))
    sent.append(list(highs))
    got = [swap(high, links[0]) for high, links in zip(highs, orders)]
    return [half[0] for pair in zip(lows, got) for half in pair], sent


def center_of(values):
    center = values - jnp.mean(values, axis=-1, keepdims=True)
    scale = lax.rsqrt(jnp.mean(center * center, axis=-1, keepdims=True) + 1e-06)
    return center * scale, scale


def norm_back(grad, unit, scale):
    return scale * (
        grad
        - jnp.mean(grad, axis=-1, keepdims=True)
        - unit * jnp.mean(grad * unit, axis=-1, keepdims=True)
    )


def route_body(experts, capacity, groups, routes, gates, lengths, cond, weight, kept, sent):
    count, width = routes.shape[1], cond.shape[1]
    lane = lax.broadcasted_iota(jnp.int32, (8, count), 1)
    row = lax.broadcasted_iota(jnp.int32, (8, count), 0)
    length = lengths[0]
    live = lane < length
    first = (row == routes[0:1]) & live
    second = (row == routes[1:2]) & live
    hits = first.astype(WIDE) + second.astype(WIDE)
    above = (
        lax.broadcasted_iota(jnp.int32, (count, count), 0)
        < lax.broadcasted_iota(jnp.int32, (count, count), 1)
    ).astype(LOW)
    room = (dot(hits.astype(LOW), above) < capacity).astype(WIDE)
    first = first.astype(WIDE) * room
    second = second.astype(WIDE) * room
    weight[...] = first * gates[0:1] + second * gates[1:2]
    kept[0] = first
    kept[1] = second
    rows = width // groups
    tally = jnp.sum(hits, axis=1, keepdims=True)
    spot = lax.broadcasted_iota(jnp.int32, (8, LANES), 1)
    line = lax.broadcasted_iota(jnp.int32, (8, LANES), 0)
    tally = jnp.sum(jnp.where(spot == line + rows, tally, 0.0), axis=0, keepdims=True)
    spot = spot[:1]
    tally = jnp.where(spot == rows + experts, length.astype(WIDE), tally)
    value = cond[...].astype(WIDE)
    value = value / (1.0 + jnp.exp(-value))
    for group in range(groups):
        start = group * rows // LANES * LANES
        part = value[:, start : start + LANES]
        shift = group * rows - start
        if shift:
            tail = value[:, start + LANES : start + 2 * LANES] if start + 2 * LANES <= width else part
            part = jnp.where(
                spot < LANES - shift, pltpu.roll(part, LANES - shift, 1), pltpu.roll(tail, LANES - shift, 1)
            )
        part = jnp.where(spot < rows, part, tally).astype(LOW)
        for expert in range(experts):
            sent[group * experts + expert] = jnp.broadcast_to(part, sent.shape[1:])


def place_of(me, rows, piece, width):
    natural = (rows[0:1] ^ me) * piece + rows[1:2]
    return (lax.broadcasted_iota(jnp.int32, (width, width), 0) == natural).astype(LOW)


def terms_body(where, got, weight, bias, shared, out, loads):
    me, expert = where[0], where[1]
    total, _, _ = got.shape
    piece, wide = weight.shape
    rows = got[:, 0, :]
    pick = (
        lax.broadcasted_iota(jnp.int32, (LANES, piece), 0)
        == lax.broadcasted_iota(jnp.int32, (LANES, piece), 1) + expert * piece
    ).astype(LOW)
    share = bias.shape[1]
    spot = (
        lax.broadcasted_iota(jnp.int32, (share, wide), 1)
        == lax.broadcasted_iota(jnp.int32, (share, wide), 0) + me * share
    ).astype(LOW)
    terms = dot(dot(rows, pick).astype(LOW), weight[...]) + dot(bias[...], spot)
    terms = terms.astype(LOW)
    first = up_to(piece, 8)
    for at in range(wide // LANES):
        out[:, first + at, :] = terms[:, at * LANES : (at + 1) * LANES]
    cols = shared.shape[1] // total
    for at in range(total):
        out[at, :piece, :cols] = shared[:, at * cols : (at + 1) * cols]
    load = jnp.sum(rows.astype(WIDE), axis=0, keepdims=True)
    loads[...] = load


def shift_body(piece, terms, weight, modulation, lines):
    total = modulation.shape[1] // LANES
    first = up_to(piece, 8)
    sums = jnp.sum(terms[:, first : first + total, :].astype(WIDE), axis=0)
    for at in range(total):
        modulation[:, at * LANES : (at + 1) * LANES] = sums[at : at + 1]
    gate = total // 6
    lines[:, :8] = jnp.zeros((lines.shape[0], 8, LANES), WIDE)
    lines[:, :gate] = jnp.broadcast_to(sums[5 * gate :], (lines.shape[0], gate, LANES))
    lines[:, 8:] = jnp.broadcast_to(weight[...], (lines.shape[0], 8, LANES))


def head_pair(values, pair):
    both = values[:, pair * LANES : (pair + 1) * LANES]
    lane = lax.broadcasted_iota(jnp.int32, both.shape, 1)
    zero = jnp.zeros_like(both)
    return jnp.concatenate(
        [jnp.where(lane < HEAD_DIM, both, zero), jnp.where(lane < HEAD_DIM, zero, both)], axis=0
    )


def scores_of(queries, stacked, pair, length):
    count = queries.shape[0]
    raw = dot_nt(queries[:, pair * LANES : (pair + 1) * LANES], stacked) * HEAD_DIM ** (-0.5)
    lane = lax.broadcasted_iota(jnp.int32, raw.shape, 1)
    return jnp.where((lane & (count - 1)) < length, raw, -1e30)


def times(left, low, high, cols):
    half = low.shape[0]
    return dot(left[:, :half], low[:, cols]) + dot(left[:, half:], high[:, cols])


def times_back(left, low, high, cols):
    return jnp.concatenate([dot_nt(left, low[:, cols]), dot_nt(left, high[:, cols])], axis=1)


def forward_body(
    piece, where, tokens, modulation, lengths, rows0, rows1, low0, high0, low1, high1,
    both, joined, totals, attn_out, middle_out, *parts,
):
    count, width = tokens.shape
    length = lengths[0]
    mod = modulation[...]
    tok = tokens[...].astype(WIDE)
    unit, _ = center_of(tok)
    first = (unit * (1.0 + mod[:, width : 2 * width]) + mod[:, :width]).astype(LOW)
    both[:, :width] = first
    start = 0
    for rows, low, high in ((rows0, low0, high0), (rows1, low1, high1)):
        moved = dot(first, place_of(where[0], rows, piece, width)).astype(LOW)
        size = min(low.shape[1], 3 * width - start)
        joined[:, start : start + size] = times(moved, low, high, slice(0, size)).astype(LOW)
        start += size
    queries, keys, values = joined[:, :width], joined[:, width : 2 * width], joined[:, 2 * width :]
    lane = lax.broadcasted_iota(jnp.int32, (count, LANES), 1)
    sums = jnp.zeros((count, LANES), WIDE)
    for pair in range(HEADS // 2):
        scores = scores_of(queries, head_pair(keys, pair), pair, length)
        probs = []
        for one in range(2):
            mine = scores[:, one * count : (one + 1) * count]
            top = jnp.max(mine, axis=-1, keepdims=True)
            total = top + jnp.log(jnp.sum(jnp.exp(mine - top), axis=-1, keepdims=True))
            sums = jnp.where(lane == 2 * pair + one, total, sums)
            probs.append(jnp.exp(mine - total).astype(LOW))
        both[:, width + pair * LANES : width + (pair + 1) * LANES] = dot(
            jnp.concatenate(probs, axis=1), head_pair(values, pair)
        ).astype(LOW)
    totals[...] = sums
    moved = dot(both[:, width:], place_of(where[0], rows1, piece, width)).astype(LOW)
    attn = times(moved, low1, high1, slice(width, 2 * width))
    attn_out[...] = attn
    middle = tok + mod[:, 2 * width : 3 * width] * attn
    middle_out[...] = middle
    unit, _ = center_of(middle)
    second = (unit * (1.0 + mod[:, 4 * width : 5 * width]) + mod[:, 3 * width : 4 * width]).astype(LOW)
    start = 0
    for part in parts:
        part[...] = second[:, start : start + part.shape[1]]
        start += part.shape[1]


def backward_body(
    piece, where, tokens, cotangent, modulation, lengths, rows0, rows1, low0, high0, low1, high1,
    joined, totals, attn_in, middle_in, near0, far0, near1, far1,
    grad_tokens, sent, lines, d_rows, d_cols, d_mod,
):
    count, width = tokens.shape
    length = lengths[0]
    mod = modulation[...]
    start = 0
    for low, high in ((near0, far0), (near1, far1)):
        size = low.shape[1]
        total = low[...].astype(WIDE) + high[...].astype(WIDE)
        d_rows[:, start : start + size] = total[:count]
        d_mod[:, 5 * width + start : 5 * width + start + size] = total[count : count + 1]
        start += size
    d_second = d_rows[...]
    attn = attn_in[...]
    unit, scale = center_of(middle_in[...])
    d_mod[:, 3 * width : 4 * width] = jnp.sum(d_second, axis=0, keepdims=True)
    d_mod[:, 4 * width : 5 * width] = jnp.sum(d_second * unit, axis=0, keepdims=True)
    d_middle = cotangent[...].astype(WIDE) + norm_back(
        d_second * (1.0 + mod[:, 4 * width : 5 * width]), unit, scale
    )
    d_mod[:, 2 * width : 3 * width] = jnp.sum(d_middle * attn, axis=0, keepdims=True)
    d_attn = (mod[:, 2 * width : 3 * width] * d_middle).astype(LOW)
    d_cols[:, 3 * width :] = d_attn
    d_attended = dot_nt(
        times_back(d_attn, low1, high1, slice(width, 2 * width)).astype(LOW), place_of(where[0], rows1, piece, width)
    ).astype(LOW)
    queries, keys, values = joined[:, :width], joined[:, width : 2 * width], joined[:, 2 * width :]
    sums = totals[...]
    lane = lax.broadcasted_iota(jnp.int32, (count, LANES), 1)
    factor = HEAD_DIM ** (-0.5)
    for pair in range(HEADS // 2):
        at = slice(pair * LANES, (pair + 1) * LANES)
        k_pair, v_pair = head_pair(keys, pair), head_pair(values, pair)
        scores = scores_of(queries, k_pair, pair, length)
        d_probs = dot_nt(d_attended[:, at], v_pair)
        probs_low, d_scores_low = [], []
        for one in range(2):
            half = slice(one * count, (one + 1) * count)
            total = jnp.sum(jnp.where(lane == 2 * pair + one, sums, 0.0), axis=1, keepdims=True)
            probs = jnp.exp(scores[:, half] - total)
            back = d_probs[:, half]
            d_scores = probs * (back - jnp.sum(probs * back, axis=-1, keepdims=True))
            probs_low.append(probs.astype(LOW))
            d_scores_low.append(d_scores.astype(LOW))
        d_scores_both = jnp.concatenate(d_scores_low, axis=1)
        d_cols[:, at] = (dot(d_scores_both, k_pair) * factor).astype(LOW)
        q_pair, d_pair = queries[:, at], d_attended[:, at]
        d_k = dot_tn(d_scores_both, q_pair) * factor
        d_v = dot_tn(jnp.concatenate(probs_low, axis=1), d_pair)
        d_k = jnp.where(lane < HEAD_DIM, d_k[:count], d_k[count:])
        d_v = jnp.where(lane < HEAD_DIM, d_v[:count], d_v[count:])
        d_cols[:, width + pair * LANES : width + (pair + 1) * LANES] = d_k.astype(LOW)
        d_cols[:, 2 * width + pair * LANES : 2 * width + (pair + 1) * LANES] = d_v.astype(LOW)
    d_first = jnp.zeros((count, width), WIDE)
    start = 0
    for rows, low, high in ((rows0, low0, high0), (rows1, low1, high1)):
        size = min(low.shape[1], 3 * width - start)
        part = times_back(d_cols[:, start : start + size], low, high, slice(0, size))
        start += size
        place = place_of(where[0], rows, piece, width)
        top = part.astype(LOW)
        rest = (part - top.astype(WIDE)).astype(LOW)
        d_first += dot_nt(top, place) + dot_nt(rest, place)
    unit, scale = center_of(tokens[...].astype(WIDE))
    d_mod[:, :width] = jnp.sum(d_first, axis=0, keepdims=True)
    d_mod[:, width : 2 * width] = jnp.sum(d_first * unit, axis=0, keepdims=True)
    grad_tokens[...] = d_middle + norm_back(
        d_first * (1.0 + mod[:, width : 2 * width]), unit, scale
    )
    for at in range(lines.shape[1]):
        line = d_mod[:, at * LANES : (at + 1) * LANES].astype(LOW)
        lines[:, at, :] = jnp.broadcast_to(line, (lines.shape[0], LANES))
    experts = sent.shape[0]
    cols, out_cols = 3 * width // experts, width // experts
    for expert in range(experts):
        to = expert ^ where[1]
        sent[to, :, :cols] = d_cols[:, expert * cols : (expert + 1) * cols]
        sent[to, :, cols:] = d_cols[:, 3 * width + expert * out_cols : 3 * width + (expert + 1) * out_cols]


def join_rows(lows, highs, rows):
    start = 0
    half = rows.shape[0] // 2
    for low, high in zip(lows, highs):
        share = low.shape[-1]
        for at, part in enumerate((low, high)):
            rows[at * half : (at + 1) * half, start : start + share] = part[...].reshape(half, share)
        start += share


def item_of(where, links, at, block):
    core, outer, inner = links
    item = where[0] ^ (core[0] * at) ^ (inner[0] * block)
    for bit, mask in enumerate(outer):
        item = item ^ ((pl.program_id(0) >> bit & 1) * mask)
    return item


def d_act_body(links, where, low, high, lines, down, d_act, rows):
    count, width = low.shape[-2:]
    for at, part in enumerate((low, high)):
        for block in range(2):
            item = item_of(where, links, at, block)
            here = slice((2 * at + block) * count, (2 * at + block + 1) * count)
            for line in range(width // LANES):
                cols = slice(line * LANES, (line + 1) * LANES)
                rows[0, here, cols] = (
                    part[block, :, cols].astype(WIDE) * lines[item, line : line + 1]
                ).astype(LOW)
    d_act[0] = dot_nt(rows[0], down[...]).astype(LOW)


def hidden_body(links, routed, where, *refs):
    lows, highs, cots, (lines, d_act, up, down) = refs[:2], refs[2:4], refs[4:6], refs[6:10]
    back_lows, back_highs, branches, (d_pre, act, rows) = refs[10:12], refs[12:14], refs[14:16], refs[16:]
    join_rows(lows, highs, rows)
    count = rows.shape[0] // 4
    width = up.shape[0]
    expert = where[1]
    flat = lax.broadcasted_iota(jnp.int32, (count, count), 0) == lax.broadcasted_iota(jnp.int32, (count, count), 1)
    spare = lax.broadcasted_iota(jnp.int32, (EXTRA, width), 0)
    blocks = [(at, block) for at in range(2) for block in range(2)]
    weights = []
    for at, block in blocks:
        line = lines[item_of(where, links, at, block), pl.ds(8 + expert, 1)]
        weights.append(jnp.sum(jnp.where(flat, line, 0.0), axis=1, keepdims=True))
    weight = jnp.concatenate(weights, axis=0)
    pre = dot(rows[...], up[...])
    square = pre * pre
    bend = jnp.tanh(pre * (CURVE + (CURVE * CUBIC) * square))
    gate = 0.5 + 0.5 * bend
    hidden = pre * gate
    slope = gate + hidden * (1.0 - bend) * (CURVE + (3.0 * CURVE * CUBIC) * square)
    d_hidden = d_act[0].astype(WIDE)
    d_full = d_hidden * slope
    d_low = jnp.concatenate([d_full[:, :routed] * weight, d_full[:, routed:]], axis=1).astype(LOW)
    d_pre[0] = d_low
    act_low = jnp.concatenate([hidden[:, :routed] * weight, hidden[:, routed:]], axis=1).astype(LOW)
    act[0] = act_low
    pair = jnp.sum(hidden[:, :routed] * d_hidden[:, :routed], axis=1, keepdims=True)
    back = dot_nt(d_low, up[...]).astype(LOW)
    out = dot(act_low, down[...])
    for number, (at, block) in enumerate(blocks):
        one = slice(number * count, (number + 1) * count)
        body, extra = slice(0, count), slice(count, count + EXTRA)
        d_gate = jnp.sum(out[one] * cots[at][block].astype(WIDE), axis=0, keepdims=True)
        d_gate = jnp.where(spare == 0, d_gate, 0.0).astype(LOW)
        start = 0
        for ref in (back_lows, back_highs)[at]:
            size = ref.shape[-1]
            ref[block, body] = back[one, start : start + size]
            ref[block, extra] = d_gate[:, start : start + size]
            start += size
        ref = branches[at]
        ref[block, body] = out[one].astype(LOW)
        line = jnp.sum(jnp.where(flat, pair[one], 0.0), axis=0, keepdims=True)
        ref[block, extra] = jnp.zeros((EXTRA, width), LOW)
        ref[block, extra, :count] = jnp.where(spare[:, :count] == expert, line, 0.0).astype(LOW)


def grads_body(write, where, *refs):
    second, d_mlp, d_pre, act = refs[:4], refs[4], refs[5], refs[6]
    outs, (rows, up_sum, down_sum) = refs[7:-3], refs[-3:]
    step = pl.program_id(0)

    @pl.when(step == 0)
    def _():
        up_sum[...] = jnp.zeros(up_sum.shape, WIDE)
        down_sum[...] = jnp.zeros(down_sum.shape, WIDE)

    join_rows(second[:2], second[2:], rows)
    up_sum[...] += dot_tn(rows[...], d_pre[0])
    down_sum[...] += dot_tn(act[0], d_mlp[0])

    @pl.when(step == pl.num_programs(0) - 1)
    def _():
        write(where, up_sum, down_sum, outs)


def write_whole(where, up_sum, down_sum, outs):
    outs[0][...] = up_sum[...]
    outs[1][...] = down_sum[...]


def place_and_twin(where):
    return where[2] // 2, where[2] % 2


def rows_at(number, size):
    return pl.ds(pl.multiple_of(number * size, 16), size)


def lanes_at(number, size):
    return pl.ds(pl.multiple_of(number * size, LANES), size)


def up_sent_body(where, weight, near, away):
    place, _ = place_and_twin(where)
    for at in range(4):
        (near if at < 2 else away)[at % 2] = weight[:, lanes_at(place ^ at, near.shape[2])]


def up_join_body(where, own, shared, other, shared_other, full):
    place, twin = place_and_twin(where)
    rows, cols = own.shape[1], own.shape[2]
    for at, mask in enumerate((0, 2, 1, 3)):
        full[rows_at(2 * (place ^ mask) + twin, rows), :cols] = own[at]
        full[rows_at(2 * (place ^ mask) + 1 - twin, rows), :cols] = other[at]
    size = shared.shape[1]
    blank = jnp.zeros((full.shape[0], LANES - size), LOW)
    for at, piece in enumerate((shared, shared_other)):
        start = cols + at * LANES
        full[:, start : start + size] = piece[...]
        full[:, start + size : start + LANES] = blank


def down_join_body(where, own, other, full):
    _, twin = place_and_twin(where)
    rows = (full.shape[0] - 2 * LANES) // 2
    size = own.shape[0] - rows
    blank = jnp.zeros((LANES - size, full.shape[1]), LOW)
    for at, piece in enumerate((own, other)):
        full[rows_at(twin if at == 0 else 1 - twin, rows)] = piece[:rows]
        start = 2 * rows + at * LANES
        full[start : start + size] = piece[rows:]
        full[start + size : start + LANES] = blank


def write_twins(where, up_sum, down_sum, outs):
    keep_up, send_up, keep_down, send_down = outs
    place, twin = place_and_twin(where)
    rows, units = keep_up.shape[1], 2 * (down_sum.shape[0] - 2 * LANES) // 2
    size = (keep_up.shape[2] - units) // 2
    mine, other = slice(units, units + size), slice(units + LANES, units + LANES + size)
    for out, at_twin, order_ in ((keep_up, twin, (mine, other)), (send_up, 1 - twin, (other, mine))):
        for at in range(out.shape[0]):
            here = rows_at(2 * (place ^ at) + at_twin, rows)
            out[at, :, :units] = up_sum[here, :units].astype(LOW)
            for number, cols in enumerate(order_):
                start = units + number * size
                out[at, :, start : start + size] = up_sum[here, cols].astype(LOW)
    half = units // 2
    for out, at_twin, rows_ in ((keep_down, twin, mine), (send_down, 1 - twin, other)):
        out[:half] = down_sum[rows_at(at_twin, half)].astype(out.dtype)
        out[half:] = down_sum[rows_].astype(out.dtype)


def twins_body(keep_up, got_up, keep_down, got_down, grad_down, shared_down, *ups):
    for at, out in enumerate(ups):
        out[...] = (keep_up[at].astype(WIDE) + got_up[at].astype(WIDE)).astype(LOW)
    half = grad_down.shape[0]
    grad_down[...] = keep_down[:half] + got_down[:half].astype(WIDE)
    shared_down[...] = (keep_down[half:] + got_down[half:].astype(WIDE)).astype(LOW)


def up_rows_body(where, up0, up1, up2, up3, shared_down, grad_up, sent):
    place, twin = place_and_twin(where)
    expert = where[1]
    units = grad_up.shape[1] // 4
    size = (up0.shape[1] - units) // 2
    cols = sent.shape[2] - 2 * size
    for at, piece in enumerate((up0, up1, up2, up3)):
        grad_up[:, lanes_at(place ^ at, units)] = piece[:, :units].astype(WIDE)
        mine, other = piece[:, units : units + size], piece[:, units + size :]
        sent[(place ^ at) ^ expert, :, :size] = jnp.where(twin == 0, mine, other)
        sent[(place ^ at) ^ expert, :, size : 2 * size] = jnp.where(twin == 0, other, mine)
    for to in range(4):
        sent[to ^ expert, :, 2 * size :] = shared_down[:, to * cols : (to + 1) * cols]


def shared_rows_body(where, got0, got1, got2, got3, grad_up, grad_down, held):
    expert = where[1]
    for at, got in enumerate((got0, got1, got2, got3)):
        held[at ^ expert] = got[...]
    size = grad_up.shape[1] // 8
    for source in range(4):
        for twin in range(2):
            start = (4 * twin + source) * size
            grad_up[:, start : start + size] = held[source, :, twin * size : (twin + 1) * size].astype(WIDE)
        grad_down[source * size : (source + 1) * size] = held[source, :, 2 * size :].astype(WIDE)


def attn_terms_body(masks, where, both, cols0, cols1, cols2, cols3, low0, low1, high0, high1, term):
    expert, group = where[1], where[2]
    width = both.shape[2] // 2
    cut = 3 * width // 4
    rows = low0.shape[1]
    for at, cols in enumerate((cols0, cols1, cols2, cols3)):
        inputs = both[expert ^ at]
        parts = (dot_tn(inputs[:, :width], cols[:, :cut]), dot_tn(inputs[:, width:], cols[:, cut:]))
        for start, part in ((0, parts[0]), (cut, parts[1])):
            here = slice(start, start + part.shape[1])
            if at:
                term[:, here] += part
            else:
                term[:, here] = part
    half = width // 2
    for number, (low, high) in enumerate(((low0, high0), (low1, high1))):
        for at, mask in enumerate(masks[number]):
            ref = low if at < 4 else high
            ref[at % 4] = term[rows_at(group ^ mask, rows), number * half : (number + 1) * half].astype(LOW)


def attn_out_body(near0, far0, near1, far1, grad_qkv, grad_out, total):
    half = near0.shape[1]
    for at, (near, far) in enumerate(((near0, far0), (near1, far1))):
        total[:, at * half : (at + 1) * half] = near[...].astype(WIDE) + far[...].astype(WIDE)
    cut = grad_qkv.shape[1]
    grad_qkv[...] = total[:, :cut]
    grad_out[...] = total[:, cut:]


def finish_body(modulation, middle, kept, low, high, block_out, grad_gates, total):
    count, width = middle.shape
    total[...] = low[...].astype(WIDE) + high[...].astype(WIDE)
    block_out[...] = middle[...] + modulation[:, 5 * width :] * total[:count]
    pairs = total[count : count + 8, :count]
    for choice in range(2):
        grad_gates[choice : choice + 1] = jnp.sum(kept[choice] * pairs, axis=0, keepdims=True)


def ada_body(experts, where, got, cond, weight, grad_weight, grad_bias, sent, d_mod):
    expert = where[1]
    total, lines, _ = got.shape
    for at in range(lines):
        d_mod[:, at * LANES : (at + 1) * LANES] = got[:, at, :]
    grad_bias[...] = jnp.sum(d_mod[...].astype(WIDE), axis=0, keepdims=True)
    cols = grad_weight.shape[1]
    mine = d_mod[:, pl.ds(pl.multiple_of(expert * cols, LANES), cols)]
    grad_weight[...] = dot_tn(cond[:, 0, :], mine)[: grad_weight.shape[0]]
    piece = weight.shape[0]
    back = dot_nt(d_mod[...], weight[...])
    sent[...] = jnp.zeros(sent.shape, WIDE)
    sent[:, 0, :piece] = back


def attn_grads_body(both, d_cols, out):
    experts, count, cols = d_cols.shape
    width = both.shape[2] // 2
    groups, rows, _ = out.shape
    flat = d_cols[...].reshape(experts * count, cols)
    inputs = both[...].reshape(experts * count, 2 * width)
    cut = 3 * cols // 4
    out[...] = jnp.concatenate(
        [dot_tn(inputs[:, :width], flat[:, :cut]), dot_tn(inputs[:, width:], flat[:, cut:])], axis=1
    ).astype(LOW).reshape(groups, rows, cols)


def attn_sum_body(got, grad_qkv, grad_out):
    total = jnp.sum(got[...].astype(WIDE), axis=0)
    cut = grad_qkv.shape[1]
    grad_qkv[...] = total[:, :cut]
    grad_out[...] = total[:, cut:]


def up_out_body(units, got, grad_up):
    for group in range(got.shape[0]):
        grad_up[:, group * units : (group + 1) * units] = got[group, :, :units].astype(WIDE)


def gather_far(pieces, masks):
    found = [pieces]
    for mask in masks:
        found = found + [[swap(piece, mask) for piece in held] for held in found]
    return found


def shards(
    tokens,
    cond,
    lengths,
    routes,
    gate_weights,
    ada_weight,
    ada_bias,
    qkv_weight,
    out_weight,
    shared_up,
    shared_down,
    expert_up,
    expert_down,
    cotangent,
):
    count, width = tokens.shape
    experts = lax.axis_size("expert")
    groups = lax.axis_size("batch")
    total = experts * groups
    me = lax.axis_index(AXES)
    my_expert = lax.axis_index("expert")
    my_group = lax.axis_index("batch")
    where = jnp.stack([me, my_expert, my_group]).astype(jnp.int32)
    capacity = 5 * 2 * count // (4 * experts)
    piece = ada_weight.shape[0]
    group_rows = width // groups
    shared_units = shared_down.shape[0]
    units = expert_down.shape[1]
    shares = [width // 2, width // 2]
    tall = (count, width)
    lines = 6 * width // LANES

    expert_masks = bits_of(experts)
    group_masks = [experts * step for step in bits_of(groups)]
    away = list(reversed(group_masks[1:3]))
    far = group_masks[:1] + group_masks[3:]
    core, across = expert_masks[:1], expert_masks[1:]
    team_links = [away + across, across + away]
    inner, outer = away[:1], across + away[1:]
    links = (core, outer, inner)
    steps = 2 ** len(outer)
    weight_links = [far[1:] + away + far[:1] + across, far[1:] + away + across + far[:1]]
    paired = groups == 8 and experts == 4
    away_masks = order(sorted(away))

    pair_weight, kept, sent = call(
        functools.partial(route_body, experts, capacity, groups),
        [((8, count), WIDE), ((2, 8, count), WIDE), ((total, 16, LANES), LOW)],
        (routes.T, gate_weights.T, lengths, cond),
        smem=(2,),
    )
    cond_all = lax.all_to_all(sent, AXES, split_axis=0, concat_axis=0, tiled=True)

    attn_w = jnp.concatenate([qkv_weight, out_weight], axis=1)[None]
    cot = cotangent[None]
    first_links = far[1:] + away
    for at, mask in enumerate(first_links):
        attn_got = swap(attn_w, mask)
        if at == len(far) - 1:
            cot_got = swap(cot, away[0])
            attn_got, cot_got, cond_all = together(attn_got, cot_got, cond_all)
            cot = grown(cot, cot_got)
            terms, loads = call(
                terms_body,
                [((total, up_to(up_to(piece, 8) + lines, 8), LANES), LOW), ((1, LANES), WIDE)],
                (where, cond_all, ada_weight, ada_bias[None], shared_up),
                smem=(0,),
            )
            terms_got = lax.all_to_all(terms, AXES, split_axis=0, concat_axis=0, tiled=True)
        attn_w = grown(attn_w, attn_got)
        if at == len(first_links) - 1:
            cot_links = away[:1] + across[:1]
            cot_got = swap(cot, across[0])
            attn_w, cot_got, terms = together(attn_w, cot_got, terms)
            cot = grown(cot, cot_got)
    cot_links = away[:1] + across + away[1:]
    for mask in across[1:]:
        cot = grown(cot, swap(cot, mask))
    tallies = loads[0, group_rows : group_rows + experts + 1]
    expert_load = tallies[:experts] * experts / (2.0 * tallies[experts])
    attn_parts = [attn_w[:, :, : 2 * width], attn_w[:, :, 2 * width :]]
    last_links = [far[:1] + across, across + far[:1]]
    weight_links = [first_links + masks for masks in last_links]
    if paired:
        place_units = expert_up.shape[2] // 4
        up_near, up_away = call(
            up_sent_body, [((2, group_rows, place_units), LOW)] * 2, (where, expert_up[0]), smem=(0,)
        )
        down_own = jnp.concatenate([expert_down[0], shared_down], axis=0)
        down_other = swap(down_own, far[0])
    for at in range(len(last_links[0])):
        got = [swap(part, masks[at]) for part, masks in zip(attn_parts, last_links)]
        if at == 0:
            cot_got = swap(cot, away[1])
            if paired:
                up_got = swap(up_away, away[0])
                got, up_got = together(got, up_got)
        elif at == len(last_links[0]) - 1:
            got, cot_got = together(got, cot_got)
            cot_low = grown(cot, cot_got)
            if paired:
                got, down_other = together(got, down_other)
        attn_parts = [grown(*pair) for pair in zip(attn_parts, got)]
    modulation, own_lines = call(
        functools.partial(shift_body, piece),
        [((1, 6 * width), WIDE), ((total, 16, LANES), WIDE)],
        (terms_got, pair_weight),
    )
    attn_far = [swap(part, core[0]) for part in attn_parts]
    cot_high = swap(cot_low, core[0])
    weights = []
    row_places = []
    for low, high, masks in zip(attn_parts, attn_far, weight_links):
        weights += [low.reshape(-1, 2 * width), high.reshape(-1, 2 * width)]
        found = np.repeat(np.array(order(masks + core), np.int32), piece)
        row_places.append(jnp.asarray(np.stack([found, np.tile(np.arange(piece, dtype=np.int32), total)])))

    both, joined, totals, attn, middle, *seconds = call(
        functools.partial(forward_body, piece),
        [
            ((count, 2 * width), LOW),
            ((count, 3 * width), LOW),
            ((count, LANES), WIDE),
            (tall, WIDE),
            (tall, WIDE),
            *[((count, share), LOW) for share in shares],
        ],
        (where, tokens, modulation, lengths, *row_places, *weights),
        smem=(0, 3),
    )

    part_shared_up = terms_got[:, :piece, :shared_units].reshape(width, shared_units)
    shared_slot = up_to(shared_units, LANES)
    second_low = [part[None] for part in seconds]
    for at in range(len(away + across)):
        got = [swap(part, masks[at]) for part, masks in zip(second_low, team_links)]
        if at == 0:
            item_lines = lax.all_to_all(tie(own_lines, *seconds), AXES, split_axis=0, concat_axis=0, tiled=True)
            if paired:
                up_mine = jnp.stack([up_near[0], up_got[0]])
                up_sent = jnp.stack([up_near[1], up_got[1]])
                up_last = swap(up_sent, away[1])
                got, up_last = together(got, up_last)
                up_own = jnp.concatenate([up_mine, up_last], axis=0)
                up_other = swap(up_own, far[0])
                shared_up_other = swap(part_shared_up, far[0])
        elif at == 1:
            got, item_lines = together(got, item_lines)
            if paired:
                routed, hidden = 2 * units, 2 * units + 2 * shared_slot
                (down_cat,) = call(
                    down_join_body, [((hidden, width), LOW)], (where, down_own, down_other), smem=(0,)
                )
        second_got = got
        if at < len(away + across) - 1:
            second_low = [grown(*pair) for pair in zip(second_low, got)]
    if paired:
        (up_cat,) = call(
            up_join_body,
            [((width, hidden), LOW)],
            (where, up_own, part_shared_up, up_other, shared_up_other),
            smem=(0,),
        )
    else:
        part_up = lax.all_to_all(expert_up[0], "batch", split_axis=1, concat_axis=0, tiled=True)
        held = gather_far([part_up, part_shared_up, expert_down[0], shared_down], far)
        slot = up_to(units, LANES)
        routed, hidden = len(held) * slot, len(held) * (slot + shared_slot)
        up_cat = jnp.concatenate(
            [pad_lanes(h[0], slot) for h in held] + [pad_lanes(h[1], shared_slot) for h in held], axis=1
        )
        down_cat = jnp.concatenate(
            [pad_lanes(h[2].T, slot).T for h in held] + [pad_lanes(h[3].T, shared_slot).T for h in held], axis=0
        )

    half = 2 * count

    def whole(array):
        return array, array.shape, lambda step: (0,) * array.ndim

    def block_at(masks, rows, lanes):
        bits = list(reversed(masks))
        block = tuple(2 if mask in inner else None for mask in bits) + (rows, lanes)

        def index(step):
            spot = {mask: step // 2**at % 2 for at, mask in enumerate(outer)}
            return tuple(spot.get(mask, 0) for mask in bits) + (0, 0)

        return block, index

    def block_in(array, masks):
        laid = array.reshape((2,) * len(masks) + array.shape[1:])
        return laid, *block_at(masks, *array.shape[1:])

    def block_out_of(rows, lanes, masks):
        return (2,) * len(masks) + (rows, lanes), LOW, *block_at(masks, rows, lanes)

    def rows_of(array):
        return array, (1,) + array.shape[1:], lambda step: (step, 0, 0)

    def rows_out(lanes):
        return (steps, 2 * half, lanes), LOW, (1, 2 * half, lanes), lambda step: (step, 0, 0)

    def sum_out(shape, kind):
        return shape, kind, shape, lambda step: (0,) * len(shape)

    def flat(part):
        return part.reshape((-1,) + part.shape[-2:])

    scalars = (where, None, None)

    cots = [block_in(cot_low, cot_links), block_in(cot_high, cot_links)]
    d_act, d_mlp = sweep(
        functools.partial(d_act_body, links),
        steps,
        [scalars, *cots, whole(item_lines), whole(down_cat)],
        [rows_out(hidden), rows_out(width)],
    )
    second_got, d_act, up_cat = together(second_got, d_act, up_cat)
    second_low = [grown(*pair) for pair in zip(second_low, second_got)]
    second_high = [swap(part, core[0]) for part in second_low]
    second_in = [block_in(part, masks) for parts in (second_low, second_high) for part, masks in zip(parts, team_links)]

    tall_rows = count + EXTRA
    back = [block_out_of(tall_rows, share, masks) for share, masks in zip(shares, team_links)]
    side = block_out_of(tall_rows, width, away + across)
    *parts, d_pre, act = sweep(
        functools.partial(hidden_body, links, routed),
        steps,
        [scalars, *second_in, *cots, whole(item_lines), rows_of(d_act), whole(up_cat), whole(down_cat)],
        [*back, *back, side, side, rows_out(hidden), rows_out(hidden)],
        scratch=[((2 * half, width), LOW)],
    )
    parts = [flat(part) for part in parts]
    if paired:
        up_lanes = place_units + 2 * shared_units
        sum_outs = [
            sum_out((4, group_rows, up_lanes), LOW),
            sum_out((4, group_rows, up_lanes), LOW),
            sum_out((units + shared_units, width), WIDE),
            sum_out((units + shared_units, width), LOW),
        ]
    else:
        sum_outs = [sum_out((width, hidden), WIDE), sum_out((hidden, width), WIDE)]
    grads = sweep(
        functools.partial(grads_body, write_twins if paired else write_whole),
        steps,
        [scalars, *second_in, rows_of(d_mlp), rows_of(d_pre), rows_of(act)],
        sum_outs,
        scratch=[((2 * half, width), LOW), ((width, hidden), WIDE), ((hidden, width), WIDE)],
    )

    lows, highs, orders = list(parts[:2]), list(parts[2:4]), [masks + core for masks in team_links]
    out_low, out_high, out_order = parts[4], parts[5], away + across + core
    sums_at = len(orders[0]) - 1
    for at in range(sums_at + 1):
        got = [swap(high, masks[-1 - at]) for high, masks in zip(highs, orders)]
        if at in (0, 2):
            out_got = swap(out_high, out_order[-1 - at // 2])
        if at == 1:
            got, grads, out_got = together(got, list(grads), out_got)
            if paired:
                twin_up, twin_down = swap(grads[1], far[0]), swap(grads[3], far[0])
        elif at < sums_at or not paired:
            got = together(*got)
        else:
            got, twin_up, twin_down = together(got, twin_up, twin_down)
        if at < sums_at:
            pairs = [added(low, other) for low, other in zip(lows, got)]
            lows, highs = [pair[0] for pair in pairs], [pair[1] for pair in pairs]
        if at == 1:
            out_low, out_high = added(out_low, out_got)
    folded = [half_[0] for pair in zip(lows, got) for half_ in pair]
    grad_tokens, d_cols, d_mod_sent = call(
        functools.partial(backward_body, piece),
        [(tall, WIDE), ((experts, count, 4 * width // experts), LOW), ((total, lines, LANES), LOW)],
        (
            where, tokens, cotangent, modulation, lengths, *row_places, *weights,
            joined, totals, attn, middle, *folded,
        ),
        scratch=[(tall, WIDE), ((count, 4 * width), LOW), ((1, 6 * width), WIDE)],
        smem=(0, 4),
    )

    both_group = lax.all_gather(tie(both, *second_high), "expert", axis=0)
    d_mod_all = lax.all_to_all(d_mod_sent, AXES, split_axis=0, concat_axis=0, tiled=True)
    if paired:
        cols_got = [d_cols[at] if not at else swap(d_cols[at], at) for at in range(4)]
        cols_got, out_got = together(cols_got, out_got)
        sum_links = [away + far, away[:1] + far + away[1:]]
        sum_masks = [[mask // experts for mask in order(masks)] for masks in sum_links]
        term_half = ((4, group_rows, width // 2), LOW)
        attn_sent = call(
            functools.partial(attn_terms_body, sum_masks),
            [term_half] * 4,
            (where, both_group, *cols_got),
            scratch=[((width, width), WIDE)],
            smem=(0,),
        )
        out_low, out_high = added(out_low, out_got)
        out_got = swap(out_high, out_order[-3])
        term_lows, term_highs = attn_sent[:2], attn_sent[2:]
        for at in range(3):
            got = [swap(high, masks[-1 - at]) for high, masks in zip(term_highs, sum_links)]
            if at == 1:
                got, out_got = together(got, out_got)
                out_low, out_high = added(out_low, out_got)
                out_got = swap(out_high, out_order[-4])
            else:
                got = together(*got)
            if at < 2:
                pairs = [added(low, other) for low, other in zip(term_lows, got)]
                term_lows, term_highs = [pair[0] for pair in pairs], [pair[1] for pair in pairs]
        grad_qkv, grad_out = call(
            attn_out_body,
            [((group_rows, 3 * width // experts), WIDE), ((group_rows, width // experts), WIDE)],
            [half_[0] for pair in zip(term_lows, got) for half_ in pair],
            scratch=[((group_rows, width), WIDE)],
        )
    else:
        natural = jnp.arange(experts, dtype=jnp.int32) ^ my_expert
        d_cols = jnp.take(d_cols, natural, axis=0)
        d_cols = lax.all_to_all(d_cols, "expert", split_axis=0, concat_axis=0, tiled=True)
        (attn_terms,) = call(
            attn_grads_body, [((groups, group_rows, 4 * width // experts), LOW)], (both_group, d_cols)
        )
        attn_terms = lax.all_to_all(attn_terms, "batch", split_axis=0, concat_axis=0, tiled=True)
        grad_qkv, grad_out = call(
            attn_sum_body,
            [((group_rows, 3 * width // experts), WIDE), ((group_rows, width // experts), WIDE)],
            (attn_terms,),
        )
        for mask in reversed(out_order[:-2]):
            out_low, out_high = added(out_low, out_got)
            out_got = swap(out_high, mask)

    block_out, grad_gate_weights = call(
        finish_body,
        [(tall, WIDE), ((2, count), WIDE)],
        (modulation, middle, kept, out_low[0], out_got[0]),
        scratch=[((tall_rows, width), WIDE)],
    )

    if paired:
        grad_expert_down, shared_own, *up_own = call(
            twins_body,
            [
                ((units, width), WIDE),
                ((shared_units, width), LOW),
                *[((group_rows, up_lanes), LOW)] * 4,
            ],
            (grads[0], twin_up, grads[2], twin_down),
        )
        up_got = [piece if not mask else swap(piece, mask) for piece, mask in zip(up_own, away_masks)]
        grad_expert_up, crossed = call(
            up_rows_body,
            [
                ((group_rows, groups * units), WIDE),
                ((4, group_rows, 2 * shared_units + width // experts), LOW),
            ],
            (where, *up_got, shared_own),
            smem=(0,),
        )
        crossed = [crossed[at] if not at else swap(crossed[at], at) for at in range(4)]
        grad_shared_up, grad_shared_down = call(
            shared_rows_body,
            [((group_rows, width), WIDE), ((experts * shared_units, width // experts), WIDE)],
            (where, *crossed),
            scratch=[((4, group_rows, 2 * shared_units + width // experts), LOW)],
            smem=(0,),
        )
    else:
        grad_up, grad_down = grads
        replicas = hidden // (slot + shared_slot)
        sums = []
        for taken, size, first in ((grad_up.T, units, 0), (grad_up.T, shared_units, routed), (grad_down, units, 0), (grad_down, shared_units, routed)):
            room = up_to(size, LANES)
            held = [taken[first + at * room : first + at * room + size] for at in range(replicas)]
            for mask in reversed(far):
                some = len(held) // 2
                held = [
                    low + swap(high.astype(LOW), mask).astype(WIDE) for low, high in zip(held[:some], held[some:])
                ]
            sums.append(held[0])
        grad_expert_down = sums[2]
        up_rows = jnp.concatenate([sums[0].T, sums[1].T], axis=1).astype(LOW).reshape(groups, group_rows, -1)
        up_rows = lax.all_to_all(up_rows, "batch", split_axis=0, concat_axis=0, tiled=True)
        grad_shared_down = lax.all_to_all(
            sums[3].astype(LOW), "expert", split_axis=1, concat_axis=0, tiled=True
        ).astype(WIDE)
        (grad_expert_up,) = call(
            functools.partial(up_out_body, units), [((group_rows, groups * units), WIDE)], (up_rows,)
        )
        shared_rows = up_rows[:, :, units:].reshape(experts, groups // experts, group_rows, shared_units)
        shared_rows = lax.all_to_all(shared_rows, "expert", split_axis=0, concat_axis=0, tiled=True)
        grad_shared_up = shared_rows.transpose(2, 1, 0, 3).reshape(group_rows, groups * shared_units).astype(WIDE)

    grad_ada_weight, grad_ada_bias, sent = call(
        functools.partial(ada_body, experts),
        [((group_rows, 6 * width // experts), WIDE), ((1, 6 * width), WIDE), ((total, 8, LANES), WIDE)],
        (where, d_mod_all, cond_all, ada_weight),
        scratch=[((total, 6 * width), LOW)],
        smem=(0,),
    )
    d_cond_act = lax.all_to_all(sent, AXES, split_axis=0, concat_axis=0, tiled=True)
    d_cond_act = d_cond_act[:, 0, :piece].reshape(1, width)
    _, silu_back = jax.vjp(jax.nn.silu, cond.astype(WIDE))
    grad_cond = silu_back(d_cond_act)[0]

    return (
        block_out,
        grad_tokens,
        grad_cond,
        grad_gate_weights.T,
        grad_ada_weight,
        grad_ada_bias[0],
        grad_qkv,
        grad_out,
        grad_shared_up,
        grad_shared_down,
        grad_expert_up[None],
        grad_expert_down[None],
        expert_load,
    )


def solution(mesh):
    rows = P(AXES, None)
    line = P(AXES)
    tiles = P("batch", "expert")
    split = P("expert", "batch", None)
    in_specs = (rows, rows, line, rows, rows, rows, line, rows, rows, rows, rows, split, split, rows)
    out_specs = (rows, rows, rows, rows, tiles, P(), tiles, tiles, tiles, tiles, split, split, P())
    return jax.shard_map(shards, mesh=mesh, in_specs=in_specs, out_specs=out_specs, check_vma=False)
```

profile of v0, /device:TPU:0, one launch (start us, length us, event | category | flops | bytes accessed | tf_op | source)
XLA Modules:
  0.0 348.1 jit_solution(526330507749397595)
XLA Ops:
  7.2 4.1 %collective-permute-start.1 = (bf16[1,128,768]{2,1,0:T(8,128)(2,1)}, bf16[1,128,768]{2,1,0:T(8,128)(2,1)S(1)}, u32[]{:S(2)}, u32[]{:S(2)}) collective-permute-start(bf16[1,128,768]{2,1,0:T(8,128)(2,1)} %bitcast.68), channel_id=1, source_target_pairs={{0,16},{1,17},{2,18},{3,19},{4,20},{5,21},{6,22},{7,23},{8,24},{9,... | collective-permute-start | bytes 589832 | tf_op jit(solution)/shard_map/ppermute | solution.py:99
  15.4 3.8 %all-to-all-start = ((bf16[32,16,128]{2,1,0:T(8,128)(2,1)}), bf16[32,16,128]{2,1,0:T(8,128)(2,1)S(1)}, u32[]{:S(2)}, u32[]{:S(2)}) async-start(bf16[32,16,128]{2,1,0:T(8,128)(2,1)} %get-tuple-element.146), calls=%async_computation | async-start | bytes 262144 | tf_op jit(solution)/shard_map/all_to_all | solution.py:732
  20.1 2.7 collective-permute-start
  22.9 9.2 %collective-permute-done = bf16[1,24,3072]{2,1,0:T(8,128)(2,1)S(1)} collective-permute-done((bf16[1,24,3072]{2,1,0:T(8,128)(2,1)S(1)}, bf16[1,24,3072]{2,1,0:T(8,128)(2,1)S(1)}, u32[]{:S(2)}, u32[]{:S(2)}) %collective-permute-start) | collective-permute-done | bytes 147488 | tf_op jit(solution)/shard_map/ppermute | solution.py:99
  33.2 1.5 collective-permute-start.3
  36.2 2.2 collective-permute-start.6
  38.4 1.8 shard_map.256
  40.2 2.7 collective-permute-done.2
  44.0 1.6 collective-permute-start.4
  47.9 1.8 collective-permute-start.9
  49.7 2.2 collective-permute-done.6
  51.9 2.2 collective-permute-done.4
  54.1 1.6 collective-permute-start.7
  55.7 1.6 collective-permute-start.8
  57.3 11.3 %collective-permute-done.9 = bf16[4,128,768]{2,1,0:T(8,128)(2,1)S(1)} collective-permute-done((bf16[4,128,768]{2,1,0:T(8,128)(2,1)S(1)}, bf16[4,128,768]{2,1,0:T(8,128)(2,1)S(1)}, u32[]{:S(2)}, u32[]{:S(2)}) %collective-permute-start.9) | collective-permute-done | bytes 786464 | tf_op jit(solution)/shard_map/ppermute | solution.py:99
  68.6 11.6 %collective-permute-done.8 = bf16[8,24,1536]{2,1,0:T(8,128)(2,1)S(1)} collective-permute-done((bf16[8,24,1536]{2,1,0:T(8,128)(2,1)S(1)}, bf16[8,24,1536]{2,1,0:T(8,128)(2,1)S(1)}, u32[]{:S(2)}, u32[]{:S(2)}) %collective-permute-start.8) | collective-permute-done | bytes 589856 | tf_op jit(solution)/shard_map/ppermute | solution.py:99
  82.0 4.7 %all-to-all-start.1 = ((bf16[32,64,128]{2,1,0:T(8,128)(2,1)}), bf16[32,64,128]{2,1,0:T(8,128)(2,1)}, u32[]{:S(2)}, u32[]{:S(2)}) async-start(bf16[32,64,128]{2,1,0:T(8,128)(2,1)} %copy-done.32), calls=%async_computation.1 | async-start | bytes 1048576 | tf_op jit(solution)/shard_map/all_to_all | solution.py:749
  86.8 1.7 fusion.3
  88.4 2.7 pad_maximum_fusion
  92.7 1.7 collective-permute-start.15
  94.4 7.9 %all-to-all-done.1.terms = bf16[32,64,128]{2,1,0:T(8,128)(2,1)} async-done(((bf16[32,64,128]{2,1,0:T(8,128)(2,1)}), bf16[32,64,128]{2,1,0:T(8,128)(2,1)}, u32[]{:S(2)}, u32[]{:S(2)}) %all-to-all-start.1) | async-done | bytes 524320 | tf_op jit(solution)/shard_map/all_to_all | solution.py:749
  105.8 5.2 %shard_map.259 = (bf16[128,1536]{1,0:T(8,128)(2,1)S(1)}, bf16[128,2304]{1,0:T(8,128)(2,1)S(1)}, f32[128,128]{1,0:T(8,128)S(1)}, f32[128,768]{1,0:T(8,128)S(1)}, ...) custom-call(s32[3]{0:T(128)S(1)} %pad_add_fusion.where, ...), custom_call_target="tpu_custom_call" | custom-call | tf_op jit(solution)/shard_map/pallas_call | solution.py:40
  116.5 3.8 %all-to-all-start.2 = ((f32[32,16,128]{2,1,0:T(8,128)}), f32[32,16,128]{2,1,0:T(8,128)S(1)}, u32[]{:S(2)}, u32[]{:S(2)}) async-start(f32[32,16,128]{2,1,0:T(8,128)} %copy-done.44), calls=%async_computation.2 | async-start | bytes 524288 | tf_op jit(solution)/shard_map/all_to_all | solution.py:818
  120.6 1.9 collective-permute-done.13
  124.5 2.3 collective-permute-start.17
  126.8 2.0 pad_maximum_fusion.10.own
  130.3 5.6 %collective-permute-done.16 = bf16[2,128,384]{2,1,0:T(8,128)(2,1)S(1)} collective-permute-done((bf16[2,128,384]{2,1,0:T(8,128)(2,1)S(1)}, bf16[2,128,384]{2,1,0:T(8,128)(2,1)S(1)}, u32[]{:S(2)}, u32[]{:S(2)}) %collective-permute-start.16) | collective-permute-done | bytes 196640 | tf_op jit(solution)/shard_map/ppermute | solution.py:99
  136.6 1.7 collective-permute-done.17
  139.5 1.5 collective-permute-start.18
  143.3 1.6 collective-permute-start.22
  146.8 7.6 %shard_map.261 = (bf16[4,512,1024]{2,1,0:T(8,128)(2,1)}, bf16[4,512,768]{2,1,0:T(8,128)(2,1)}) custom-call(s32[3]{0:T(128)} %copy-done.55, bf16[2,2,2,128,768]{4,3,2,1,0:T(8,128)(2,1)} %bitcast.15.low.refs_4_, bf16[2,2,2,128,768]{4,3,2,1,0:T(8,128)(2,1)} %bitcast.16.high.refs_5_, f32[32,16,128]{2,1,0:T(8,128)} %copy-done.79, bf16[1024,768]{1,0:T(8,128)(2,1)} %copy-done), custom_call_target="tpu_custom_call" | custom-call | tf_op jit(solution)/shard_map/pallas_call | solution.py:51
  154.4 1.6 shard_map.262.refs_8_
  159.3 1.8 collective-permute-done.23
  163.1 18.8 %shard_map.263 = (bf16[2,2,2,144,384]{4,3,2,1,0:T(8,128)(2,1)}, bf16[2,2,2,144,384]{4,3,2,1,0:T(8,128)(2,1)}, bf16[2,2,2,144,384]{4,3,2,1,0:T(8,128)(2,1)}, bf16...) custom-call(s32[3]{0:T(128)} %copy-done.55, ...), custom_call_target="tpu_custom_call" | custom-call | tf_op jit(solution)/shard_map/pallas_call | solution.py:51
  182.7 4.6 %collective-permute-done.25.got = bf16[8,144,384]{2,1,0:T(8,128)(2,1)} collective-permute-done((bf16[8,144,384]{2,1,0:T(8,128)(2,1)}, bf16[8,144,384]{2,1,0:T(8,128)(2,1)}, u32[]{:S(2)}, u32[]{:S(2)}) %collective-permute-start.25) | collective-permute-done | bytes 884768 | tf_op jit(solution)/shard_map/ppermute | solution.py:99
  194.0 1.9 collective-permute-start.28
  195.8 12.8 %shard_map.266 = (bf16[4,96,960]{2,1,0:T(8,128)(2,1)}, bf16[4,96,960]{2,1,0:T(8,128)(2,1)}, f32[480,768]{1,0:T(8,128)}, bf16[480,768]{1,0:T(8,128)(2,1)}) custom-call(s32[3]{0:T(128)} %copy-done.55, bf16[2,2,2,128,384]{4,3,2,1,0:T(8,128)(2,1)} %bitcast.92, bf16[2,2,2,128,384]{4,3,2,1,0:T(8,128)(2,1)} %bitcast.94, bf16[2,2,2,128,384]{4,3,2,1,0:T(8,128)(2,1)} %bitcast.96, ...), custom_call_target="tpu_custom_call" | custom-call | tf_op jit(solution)/shard_map/pallas_call | solution.py:51
  211.5 2.8 shard_map.267
  216.3 2.4 collective-permute-start.31
  218.6 7.7 %collective-permute-done.30.got = bf16[2,144,384]{2,1,0:T(8,128)(2,1)S(1)} collective-permute-done((bf16[2,144,384]{2,1,0:T(8,128)(2,1)S(1)}, bf16[2,144,384]{2,1,0:T(8,128)(2,1)S(1)}, u32[]{:S(2)}, u32[]{:S(2)}) %collective-permute-start.30) | collective-permute-done | bytes 221216 | tf_op jit(solution)/shard_map/ppermute | solution.py:99
  226.4 1.6 collective-permute-done.31.got
  228.3 1.7 collective-permute-start.33
  230.0 3.8 %collective-permute-done.32 = bf16[1,144,384]{2,1,0:T(8,128)(2,1)S(1)} collective-permute-done((bf16[1,144,384]{2,1,0:T(8,128)(2,1)S(1)}, bf16[1,144,384]{2,1,0:T(8,128)(2,1)S(1)}, u32[]{:S(2)}, u32[]{:S(2)}) %collective-permute-start.32) | collective-permute-done | bytes 110624 | tf_op jit(solution)/shard_map/ppermute | solution.py:99
  233.7 3.9 %collective-permute-done.33 = bf16[1,144,384]{2,1,0:T(8,128)(2,1)S(1)} collective-permute-done((bf16[1,144,384]{2,1,0:T(8,128)(2,1)S(1)}, bf16[1,144,384]{2,1,0:T(8,128)(2,1)S(1)}, u32[]{:S(2)}, u32[]{:S(2)}) %collective-permute-start.33) | collective-permute-done | bytes 110624 | tf_op jit(solution)/shard_map/ppermute | solution.py:99
  237.7 6.9 %collective-permute-done.35.got_down = bf16[480,768]{1,0:T(8,128)(2,1)S(1)} collective-permute-done((bf16[480,768]{1,0:T(8,128)(2,1)}, bf16[480,768]{1,0:T(8,128)(2,1)S(1)}, u32[]{:S(2)}, u32[]{:S(2)}) %collective-permute-start.35) | collective-permute-done | bytes 737312 | tf_op jit(solution)/shard_map/ppermute | solution.py:99
  244.6 9.0 %shard_map.272 = (f32[128,768]{1,0:T(8,128)}, bf16[4,128,768]{2,1,0:T(8,128)(2,1)S(1)}, bf16[32,36,128]{2,1,0:T(8,128)(2,1)S(1)}) custom-call(s32[3]{0:T(128)S(1)} %copy-done.57, bf16[128,768]{1,0:T(8,128)(2,1)S(1)} %copy-done.21, bf16[128,768]{1,0:T(8,128)(2,1)S(1)} %copy-done.4, f32[1,4608]{1,0:T(1,128)S(1)} %copy-done.50, s32[1]{0:T(128)S(6)} %copy.31.lengths, ...), custom_call_target="tpu_custom_call" | custom-call | tf_op jit(solution)/shard_map/pallas_call | solution.py:40
  254.4 4.1 %all-to-all-start.3 = ((bf16[32,36,128]{2,1,0:T(8,128)(2,1)}), bf16[32,36,128]{2,1,0:T(8,128)(2,1)S(1)}, u32[]{:S(2)}, u32[]{:S(2)}) async-start(bf16[32,36,128]{2,1,0:T(8,128)(2,1)} %copy-done.42), calls=%async_computation.3 | async-start | bytes 655360 | tf_op jit(solution)/shard_map/all_to_all | solution.py:966
  258.9 1.7 collective-permute-start.37
  266.8 1.7 collective-permute-start.48
  269.5 3.4 collective-permute-done.38.cols3
  274.2 2.6 shard_map.274
  276.9 1.8 collective-permute-start.40
  281.2 2.0 shard_map.273
  283.9 2.2 collective-permute-start.49
  286.8 1.5 collective-permute-start.50
  289.6 11.5 %collective-permute-done.49.up2 = bf16[96,960]{1,0:T(8,128)(2,1)S(1)} collective-permute-done((bf16[96,960]{1,0:T(8,128)(2,1)S(1)}, bf16[96,960]{1,0:T(8,128)(2,1)S(1)}, u32[]{:S(2)}, u32[]{:S(2)}) %collective-permute-start.49) | collective-permute-done | bytes 184352 | tf_op jit(solution)/shard_map/ppermute | solution.py:99
  301.1 6.3 %collective-permute-done.50.up3 = bf16[96,960]{1,0:T(8,128)(2,1)S(1)} collective-permute-done((bf16[96,960]{1,0:T(8,128)(2,1)S(1)}, bf16[96,960]{1,0:T(8,128)(2,1)S(1)}, u32[]{:S(2)}, u32[]{:S(2)}) %collective-permute-start.50) | collective-permute-done | bytes 184352 | tf_op jit(solution)/shard_map/ppermute | solution.py:99
  308.3 1.8 shard_map.284
  311.0 2.1 shard_map.279
  313.1 3.5 all-to-all-start.4
  316.9 1.7 collective-permute-start.52
  318.7 2.6 collective-permute-start.46
  326.8 2.6 collective-permute-start.45
  331.0 9.4 %collective-permute-done.45 = bf16[1,144,768]{2,1,0:T(8,128)(2,1)S(1)} collective-permute-done((bf16[1,144,768]{2,1,0:T(8,128)(2,1)S(1)}, bf16[1,144,768]{2,1,0:T(8,128)(2,1)S(1)}, u32[]{:S(2)}, u32[]{:S(2)}) %collective-permute-start.45) | collective-permute-done | bytes 221216 | tf_op jit(solution)/shard_map/ppermute | solution.py:99
  (306 shorter events, 74.3 us)
Async XLA Ops:
  7.2 24.9 %collective-permute-start.1 = (bf16[1,128,768]{2,1,0:T(8,128)(2,1)}, bf16[1,128,768]{2,1,0:T(8,128)(2,1)S(1)}, u32[]{:S(2)}, u32[]{:S(2)}) collective-permute-start(bf16[1,128,768]{2,1,0:T(8,128)(2,1)} %bitcast.68), channel_id=1, source_target_pairs={{0,16},{1,17},{2,18},{3,19},{4,20},{5,21},{6,22},{7,23},{8,24},{9,... | collective-permute-start | bytes 589832 | tf_op jit(solution)/shard_map/ppermute | solution.py:99
  15.4 16.7 %all-to-all-start = ((bf16[32,16,128]{2,1,0:T(8,128)(2,1)}), bf16[32,16,128]{2,1,0:T(8,128)(2,1)S(1)}, u32[]{:S(2)}, u32[]{:S(2)}) async-start(bf16[32,16,128]{2,1,0:T(8,128)(2,1)} %get-tuple-element.146), calls=%async_computation | async-start | bytes 262144 | tf_op jit(solution)/shard_map/all_to_all | solution.py:732
  20.1 12.0 %collective-permute-start = (bf16[1,24,3072]{2,1,0:T(8,128)(2,1)S(1)}, bf16[1,24,3072]{2,1,0:T(8,128)(2,1)S(1)}, u32[]{:S(2)}, u32[]{:S(2)}) collective-permute-start(bf16[1,24,3072]{2,1,0:T(8,128)(2,1)S(1)} %maximum_bitcast_fusion), channel_id=1, source_target_pairs={{0,16},{1,17},{2,18},{3,19},{4,20},{5,21},{6,22},{7,23},{8,24},{9,... | collective-permute-start | bytes 442376 | tf_op jit(solution)/shard_map/ppermute | solution.py:99
  32.2 10.7 %collective-permute-start.2 = (bf16[2,24,3072]{2,1,0:T(8,128)(2,1)S(1)}, bf16[2,24,3072]{2,1,0:T(8,128)(2,1)S(1)}, u32[]{:S(2)}, u32[]{:S(2)}) collective-permute-start(bf16[2,24,3072]{2,1,0:T(8,128)(2,1)S(1)} %pad_maximum_fusion.14), channel_id=1, source_target_pairs={{0,8},{1,9},{2,10},{3,11},{4,12},{5,13},{6,14},{7,15},{8,0},{9,1},... | collective-permute-start | bytes 884744 | tf_op jit(solution)/shard_map/ppermute | solution.py:99
  33.2 10.8 %collective-permute-start.3 = (bf16[2,128,768]{2,1,0:T(8,128)(2,1)S(1)}, bf16[2,128,768]{2,1,0:T(8,128)(2,1)S(1)}, u32[]{:S(2)}, u32[]{:S(2)}) collective-permute-start(bf16[2,128,768]{2,1,0:T(8,128)(2,1)S(1)} %pad_maximum_fusion.11), channel_id=1, source_target_pairs={{0,2},{1,3},{2,0},{3,1},{4,6},{5,7},{6,4},{7,5},{8,10},{9,11},{10,... | collective-permute-start | bytes 1179656 | tf_op jit(solution)/shard_map/ppermute | solution.py:99
  34.8 110.0 %copy-start.55 = (s32[3]{0:T(128)}, s32[3]{0:T(128)S(1)}, u32[]{:S(2)}) copy-start(s32[3]{0:T(128)S(1)} %pad_add_fusion.where) | copy-start | bytes 40
  36.2 15.7 %collective-permute-start.6 = (bf16[2,96,768]{2,1,0:T(8,128)(2,1)S(1)}, bf16[2,96,768]{2,1,0:T(8,128)(2,1)S(1)}, u32[]{:S(2)}, u32[]{:S(2)}) collective-permute-start(bf16[2,96,768]{2,1,0:T(8,128)(2,1)S(1)} %get-tuple-element.154), channel_id=1, source_target_pairs={{0,16},{1,17},{2,18},{3,19},{4,20},{5,21},{6,22},{7,23},{8,24},{9,... | collective-permute-start | bytes 884744 | tf_op jit(solution)/shard_map/ppermute | solution.py:99
  44.0 10.0 %collective-permute-start.4 = (bf16[4,24,1536]{2,1,0:T(8,128)(2,1)S(1)}, bf16[4,24,1536]{2,1,0:T(8,128)(2,1)S(1)}, u32[]{:S(2)}, u32[]{:S(2)}) collective-permute-start(bf16[4,24,1536]{2,1,0:T(8,128)(2,1)S(1)} %get-tuple-element.310), channel_id=1, source_target_pairs={{0,4},{1,5},{2,6},{3,7},{4,0},{5,1},{6,2},{7,3},{8,12},{9,13},{10,... | collective-permute-start | bytes 884744 | tf_op jit(solution)/shard_map/ppermute | solution.py:99
  45.6 8.4 %collective-permute-start.5 = (bf16[4,24,1536]{2,1,0:T(8,128)(2,1)S(1)}, bf16[4,24,1536]{2,1,0:T(8,128)(2,1)S(1)}, u32[]{:S(2)}, u32[]{:S(2)}) collective-permute-start(bf16[4,24,1536]{2,1,0:T(8,128)(2,1)S(1)} %get-tuple-element.309), channel_id=1, source_target_pairs={{0,2},{1,3},{2,0},{3,1},{4,6},{5,7},{6,4},{7,5},{8,10},{9,11},{10,... | collective-permute-start | bytes 884744 | tf_op jit(solution)/shard_map/ppermute | solution.py:99
  47.2 33.1 %collective-permute-start.10 = (bf16[480,768]{1,0:T(8,128)(2,1)S(1)}, bf16[480,768]{1,0:T(8,128)(2,1)S(1)}, u32[]{:S(2)}, u32[]{:S(2)}) collective-permute-start(bf16[480,768]{1,0:T(8,128)(2,1)S(1)} %pad_maximum_fusion.6.own), channel_id=1, source_target_pairs={{0,4},{1,5},{2,6},{3,7},{4,0},{5,1},{6,2},{7,3},{8,12},{9,13},{10,... | collective-permute-start | bytes 2211848 | tf_op jit(solution)/shard_map/ppermute | solution.py:99
  47.9 20.7 %collective-permute-start.9 = (bf16[4,128,768]{2,1,0:T(8,128)(2,1)S(1)}, bf16[4,128,768]{2,1,0:T(8,128)(2,1)S(1)}, u32[]{:S(2)}, u32[]{:S(2)}) collective-permute-start(bf16[4,128,768]{2,1,0:T(8,128)(2,1)S(1)} %pad_maximum_fusion.3), channel_id=1, source_target_pairs={{0,8},{1,9},{2,10},{3,11},{4,12},{5,13},{6,14},{7,15},{8,0},{9,1},... | collective-permute-start | bytes 2359304 | tf_op jit(solution)/shard_map/ppermute | solution.py:99
  54.1 14.5 %collective-permute-start.7 = (bf16[8,24,1536]{2,1,0:T(8,128)(2,1)S(1)}, bf16[8,24,1536]{2,1,0:T(8,128)(2,1)S(1)}, u32[]{:S(2)}, u32[]{:S(2)}) collective-permute-start(bf16[8,24,1536]{2,1,0:T(8,128)(2,1)S(1)} %pad_maximum_fusion.8), channel_id=1, source_target_pairs={{0,2},{1,3},{2,0},{3,1},{4,6},{5,7},{6,4},{7,5},{8,10},{9,11},{10,... | collective-permute-start | bytes 1769480 | tf_op jit(solution)/shard_map/ppermute | solution.py:99
  55.7 24.5 %collective-permute-start.8 = (bf16[8,24,1536]{2,1,0:T(8,128)(2,1)S(1)}, bf16[8,24,1536]{2,1,0:T(8,128)(2,1)S(1)}, u32[]{:S(2)}, u32[]{:S(2)}) collective-permute-start(bf16[8,24,1536]{2,1,0:T(8,128)(2,1)S(1)} %pad_maximum_fusion.9), channel_id=1, source_target_pairs={{0,4},{1,5},{2,6},{3,7},{4,0},{5,1},{6,2},{7,3},{8,12},{9,13},{10,... | collective-permute-start | bytes 1769480 | tf_op jit(solution)/shard_map/ppermute | solution.py:99
  81.3 22.9 %collective-permute-start.11 = (bf16[16,24,1536]{2,1,0:T(8,128)(2,1)S(1)}, bf16[16,24,1536]{2,1,0:T(8,128)(2,1)S(1)}, u32[]{:S(2)}, u32[]{:S(2)}) collective-permute-start(bf16[16,24,1536]{2,1,0:T(8,128)(2,1)S(1)} %pad_maximum_fusion.1), channel_id=1, source_target_pairs={{0,1},{1,0},{2,3},{3,2},{4,5},{5,4},{6,7},{7,6},{8,9},{9,8},{10,11... | collective-permute-start | bytes 3538952 | tf_op jit(solution)/shard_map/ppermute | solution.py:99
  81.5 22.7 %collective-permute-start.12 = (bf16[16,24,1536]{2,1,0:T(8,128)(2,1)S(1)}, bf16[16,24,1536]{2,1,0:T(8,128)(2,1)}, u32[]{:S(2)}, u32[]{:S(2)}) collective-permute-start(bf16[16,24,1536]{2,1,0:T(8,128)(2,1)S(1)} %pad_maximum_fusion.2), channel_id=1, source_target_pairs={{0,1},{1,0},{2,3},{3,2},{4,5},{5,4},{6,7},{7,6},{8,9},{9,8},{10,11... | collective-permute-start | bytes 3538952 | tf_op jit(solution)/shard_map/ppermute | solution.py:99
  82.0 20.3 %all-to-all-start.1 = ((bf16[32,64,128]{2,1,0:T(8,128)(2,1)}), bf16[32,64,128]{2,1,0:T(8,128)(2,1)}, u32[]{:S(2)}, u32[]{:S(2)}) async-start(bf16[32,64,128]{2,1,0:T(8,128)(2,1)} %copy-done.32), calls=%async_computation.1 | async-start | bytes 1048576 | tf_op jit(solution)/shard_map/all_to_all | solution.py:749
  91.1 55.6 %collective-permute-start.20 = (bf16[8,128,768]{2,1,0:T(8,128)(2,1)}, bf16[8,128,768]{2,1,0:T(8,128)(2,1)}, u32[]{:S(2)}, u32[]{:S(2)}) collective-permute-start(bf16[8,128,768]{2,1,0:T(8,128)(2,1)} %pad_maximum_fusion), channel_id=1, source_target_pairs={{0,1},{1,0},{2,3},{3,2},{4,5},{5,4},{6,7},{7,6},{8,9},{9,8},{10,11... | collective-permute-start | bytes 4718600 | tf_op jit(solution)/shard_map/ppermute | solution.py:99
  92.7 27.8 %collective-permute-start.15 = (bf16[2,96,768]{2,1,0:T(8,128)(2,1)}, bf16[2,96,768]{2,1,0:T(8,128)(2,1)}, u32[]{:S(2)}, u32[]{:S(2)}) collective-permute-start(bf16[2,96,768]{2,1,0:T(8,128)(2,1)} %pad_maximum_fusion.15), channel_id=1, source_target_pairs={{0,8},{1,9},{2,10},{3,11},{4,12},{5,13},{6,14},{7,15},{8,0},{9,1},... | collective-permute-start | bytes 884744 | tf_op jit(solution)/shard_map/ppermute | solution.py:99
  114.7 7.8 %collective-permute-start.13 = (bf16[1,128,384]{2,1,0:T(8,128)(2,1)}, bf16[1,128,384]{2,1,0:T(8,128)(2,1)S(1)}, u32[]{:S(2)}, u32[]{:S(2)}) collective-permute-start(bf16[1,128,384]{2,1,0:T(8,128)(2,1)} %bitcast.13), channel_id=1, source_target_pairs={{0,16},{1,17},{2,18},{3,19},{4,20},{5,21},{6,22},{7,23},{8,24},{9,... | collective-permute-start | bytes 294920 | tf_op jit(solution)/shard_map/ppermute | solution.py:99
  115.1 7.4 %collective-permute-start.14 = (bf16[1,128,384]{2,1,0:T(8,128)(2,1)}, bf16[1,128,384]{2,1,0:T(8,128)(2,1)S(1)}, u32[]{:S(2)}, u32[]{:S(2)}) collective-permute-start(bf16[1,128,384]{2,1,0:T(8,128)(2,1)} %bitcast.14), channel_id=1, source_target_pairs={{0,2},{1,3},{2,0},{3,1},{4,6},{5,7},{6,4},{7,5},{8,10},{9,11},{10,... | collective-permute-start | bytes 294920 | tf_op jit(solution)/shard_map/ppermute | solution.py:99
  116.5 21.7 %all-to-all-start.2 = ((f32[32,16,128]{2,1,0:T(8,128)}), f32[32,16,128]{2,1,0:T(8,128)S(1)}, u32[]{:S(2)}, u32[]{:S(2)}) async-start(f32[32,16,128]{2,1,0:T(8,128)} %copy-done.44), calls=%async_computation.2 | async-start | bytes 524288 | tf_op jit(solution)/shard_map/all_to_all | solution.py:818
  120.4 152.5 %all-gather.3.cloned.1.call-start = ((), (), s32[]{:S(2)}) async-start(), calls=%async_computation.5 | async-start | bytes 1966080 | tf_op jit(solution)/shard_map/all_gather | solution.py:965
  123.5 12.5 %collective-permute-start.16 = (bf16[2,128,384]{2,1,0:T(8,128)(2,1)S(1)}, bf16[2,128,384]{2,1,0:T(8,128)(2,1)S(1)}, u32[]{:S(2)}, u32[]{:S(2)}) collective-permute-start(bf16[2,128,384]{2,1,0:T(8,128)(2,1)S(1)} %pad_maximum_fusion.16), channel_id=1, source_target_pairs={{0,8},{1,9},{2,10},{3,11},{4,12},{5,13},{6,14},{7,15},{8,0},{9,1},... | collective-permute-start | bytes 589832 | tf_op jit(solution)/shard_map/ppermute | solution.py:99
  124.5 13.8 %collective-permute-start.17 = (bf16[2,128,384]{2,1,0:T(8,128)(2,1)S(1)}, bf16[2,128,384]{2,1,0:T(8,128)(2,1)}, u32[]{:S(2)}, u32[]{:S(2)}) collective-permute-start(bf16[2,128,384]{2,1,0:T(8,128)(2,1)S(1)} %pad_maximum_fusion.17), channel_id=1, source_target_pairs={{0,16},{1,17},{2,18},{3,19},{4,20},{5,21},{6,22},{7,23},{8,24},{9,... | collective-permute-start | bytes 589832 | tf_op jit(solution)/shard_map/ppermute | solution.py:99
  128.8 25.6 %collective-permute-start.21 = (bf16[4,96,768]{2,1,0:T(8,128)(2,1)}, bf16[4,96,768]{2,1,0:T(8,128)(2,1)}, u32[]{:S(2)}, u32[]{:S(2)}) collective-permute-start(bf16[4,96,768]{2,1,0:T(8,128)(2,1)} %pad_maximum_fusion.10.own), channel_id=1, source_target_pairs={{0,4},{1,5},{2,6},{3,7},{4,0},{5,1},{6,2},{7,3},{8,12},{9,13},{10,... | collective-permute-start | bytes 1769480 | tf_op jit(solution)/shard_map/ppermute | solution.py:99
  139.5 16.6 %collective-permute-start.18 = (bf16[4,128,384]{2,1,0:T(8,128)(2,1)S(1)}, bf16[4,128,384]{2,1,0:T(8,128)(2,1)S(1)}, u32[]{:S(2)}, u32[]{:S(2)}) collective-permute-start(bf16[4,128,384]{2,1,0:T(8,128)(2,1)S(1)} %pad_maximum_fusion.12), channel_id=1, source_target_pairs={{0,2},{1,3},{2,0},{3,1},{4,6},{5,7},{6,4},{7,5},{8,10},{9,11},{10,... | collective-permute-start | bytes 1179656 | tf_op jit(solution)/shard_map/ppermute | solution.py:99
  142.1 14.0 %collective-permute-start.19 = (bf16[4,128,384]{2,1,0:T(8,128)(2,1)S(1)}, bf16[4,128,384]{2,1,0:T(8,128)(2,1)}, u32[]{:S(2)}, u32[]{:S(2)}) collective-permute-start(bf16[4,128,384]{2,1,0:T(8,128)(2,1)S(1)} %pad_maximum_fusion.13), channel_id=1, source_target_pairs={{0,8},{1,9},{2,10},{3,11},{4,12},{5,13},{6,14},{7,15},{8,0},{9,1},... | collective-permute-start | bytes 1179656 | tf_op jit(solution)/shard_map/ppermute | solution.py:99
  143.3 11.1 %collective-permute-start.22 = (bf16[768,96]{1,0:T(8,128)(2,1)S(1)}, bf16[768,96]{1,0:T(8,128)(2,1)S(1)}, u32[]{:S(2)}, u32[]{:S(2)}) collective-permute-start(bf16[768,96]{1,0:T(8,128)(2,1)S(1)} %bitcast.76), channel_id=1, source_target_pairs={{0,4},{1,5},{2,6},{3,7},{4,0},{5,1},{6,2},{7,3},{8,12},{9,13},{10,... | collective-permute-start | bytes 442376 | tf_op jit(solution)/shard_map/ppermute | solution.py:99
  158.7 2.4 collective-permute-start.23
  158.8 3.4 collective-permute-start.24
  181.9 27.5 %collective-permute-start.29 = (bf16[8,144,768]{2,1,0:T(8,128)(2,1)}, bf16[8,144,768]{2,1,0:T(8,128)(2,1)}, u32[]{:S(2)}, u32[]{:S(2)}) collective-permute-start(bf16[8,144,768]{2,1,0:T(8,128)(2,1)} %bitcast.100), channel_id=1, source_target_pairs={{0,1},{1,0},{2,3},{3,2},{4,5},{5,4},{6,7},{7,6},{8,9},{9,8},{10,11... | collective-permute-start | bytes 5308424 | tf_op jit(solution)/shard_map/ppermute | solution.py:99
  182.1 5.2 %collective-permute-start.25 = (bf16[8,144,384]{2,1,0:T(8,128)(2,1)}, bf16[8,144,384]{2,1,0:T(8,128)(2,1)}, u32[]{:S(2)}, u32[]{:S(2)}) collective-permute-start(bf16[8,144,384]{2,1,0:T(8,128)(2,1)} %bitcast.104), channel_id=1, source_target_pairs={{0,1},{1,0},{2,3},{3,2},{4,5},{5,4},{6,7},{7,6},{8,9},{9,8},{10,11... | collective-permute-start | bytes 2654216 | tf_op jit(solution)/shard_map/ppermute | solution.py:99
  182.5 6.1 %collective-permute-start.26 = (bf16[8,144,384]{2,1,0:T(8,128)(2,1)}, bf16[8,144,384]{2,1,0:T(8,128)(2,1)}, u32[]{:S(2)}, u32[]{:S(2)}) collective-permute-start(bf16[8,144,384]{2,1,0:T(8,128)(2,1)} %bitcast.103), channel_id=1, source_target_pairs={{0,1},{1,0},{2,3},{3,2},{4,5},{5,4},{6,7},{7,6},{8,9},{9,8},{10,11... | collective-permute-start | bytes 2654216 | tf_op jit(solution)/shard_map/ppermute | solution.py:99
  191.1 17.5 %collective-permute-start.27 = (bf16[4,144,384]{2,1,0:T(8,128)(2,1)S(1)}, bf16[4,144,384]{2,1,0:T(8,128)(2,1)S(1)}, u32[]{:S(2)}, u32[]{:S(2)}) collective-permute-start(bf16[4,144,384]{2,1,0:T(8,128)(2,1)S(1)} %get-tuple-element.188), channel_id=1, source_target_pairs={{0,2},{1,3},{2,0},{3,1},{4,6},{5,7},{6,4},{7,5},{8,10},{9,11},{10,... | collective-permute-start | bytes 1327112 | tf_op jit(solution)/shard_map/ppermute | solution.py:99
  194.0 15.5 %collective-permute-start.28 = (bf16[4,144,384]{2,1,0:T(8,128)(2,1)S(1)}, bf16[4,144,384]{2,1,0:T(8,128)(2,1)S(1)}, u32[]{:S(2)}, u32[]{:S(2)}) collective-permute-start(bf16[4,144,384]{2,1,0:T(8,128)(2,1)S(1)} %get-tuple-element.191), channel_id=1, source_target_pairs={{0,8},{1,9},{2,10},{3,11},{4,12},{5,13},{6,14},{7,15},{8,0},{9,1},... | collective-permute-start | bytes 1327112 | tf_op jit(solution)/shard_map/ppermute | solution.py:99
  209.4 28.2 %collective-permute-start.34 = (bf16[4,96,960]{2,1,0:T(8,128)(2,1)}, bf16[4,96,960]{2,1,0:T(8,128)(2,1)S(1)}, u32[]{:S(2)}, u32[]{:S(2)}) collective-permute-start(bf16[4,96,960]{2,1,0:T(8,128)(2,1)} %get-tuple-element.218), channel_id=1, source_target_pairs={{0,4},{1,5},{2,6},{3,7},{4,0},{5,1},{6,2},{7,3},{8,12},{9,13},{10,... | collective-permute-start | bytes 2211848 | tf_op jit(solution)/shard_map/ppermute | solution.py:99
  210.3 34.2 %collective-permute-start.35 = (bf16[480,768]{1,0:T(8,128)(2,1)}, bf16[480,768]{1,0:T(8,128)(2,1)S(1)}, u32[]{:S(2)}, u32[]{:S(2)}) collective-permute-start(bf16[480,768]{1,0:T(8,128)(2,1)} %get-tuple-element.219), channel_id=1, source_target_pairs={{0,4},{1,5},{2,6},{3,7},{4,0},{5,1},{6,2},{7,3},{8,12},{9,13},{10,... | collective-permute-start | bytes 2211848 | tf_op jit(solution)/shard_map/ppermute | solution.py:99
  214.3 39.4 %copy-start.14 = (bf16[4,144,768]{2,1,0:T(8,128)(2,1)}, bf16[4,144,768]{2,1,0:T(8,128)(2,1)S(1)}, u32[]{:S(2)}) copy-start(bf16[4,144,768]{2,1,0:T(8,128)(2,1)S(1)} %get-tuple-element.201.low) | copy-start | bytes 2654212
  214.3 54.2 %collective-permute-start.39 = (bf16[4,144,768]{2,1,0:T(8,128)(2,1)}, bf16[4,144,768]{2,1,0:T(8,128)(2,1)}, u32[]{:S(2)}, u32[]{:S(2)}) collective-permute-start(bf16[4,144,768]{2,1,0:T(8,128)(2,1)} %get-tuple-element.224), channel_id=1, source_target_pairs={{0,2},{1,3},{2,0},{3,1},{4,6},{5,7},{6,4},{7,5},{8,10},{9,11},{10,... | collective-permute-start | bytes 2654216 | tf_op jit(solution)/shard_map/ppermute | solution.py:99
  215.9 10.5 %collective-permute-start.30 = (bf16[2,144,384]{2,1,0:T(8,128)(2,1)S(1)}, bf16[2,144,384]{2,1,0:T(8,128)(2,1)S(1)}, u32[]{:S(2)}, u32[]{:S(2)}) collective-permute-start(bf16[2,144,384]{2,1,0:T(8,128)(2,1)S(1)} %get-tuple-element.208), channel_id=1, source_target_pairs={{0,8},{1,9},{2,10},{3,11},{4,12},{5,13},{6,14},{7,15},{8,0},{9,1},... | collective-permute-start | bytes 663560 | tf_op jit(solution)/shard_map/ppermute | solution.py:99
  216.3 11.7 %collective-permute-start.31 = (bf16[2,144,384]{2,1,0:T(8,128)(2,1)S(1)}, bf16[2,144,384]{2,1,0:T(8,128)(2,1)S(1)}, u32[]{:S(2)}, u32[]{:S(2)}) collective-permute-start(bf16[2,144,384]{2,1,0:T(8,128)(2,1)S(1)} %get-tuple-element.211), channel_id=1, source_target_pairs={{0,16},{1,17},{2,18},{3,19},{4,20},{5,21},{6,22},{7,23},{8,24},{9,... | collective-permute-start | bytes 663560 | tf_op jit(solution)/shard_map/ppermute | solution.py:99
  228.0 5.7 %collective-permute-start.32 = (bf16[1,144,384]{2,1,0:T(8,128)(2,1)S(1)}, bf16[1,144,384]{2,1,0:T(8,128)(2,1)S(1)}, u32[]{:S(2)}, u32[]{:S(2)}) collective-permute-start(bf16[1,144,384]{2,1,0:T(8,128)(2,1)S(1)} %get-tuple-element.214), channel_id=1, source_target_pairs={{0,16},{1,17},{2,18},{3,19},{4,20},{5,21},{6,22},{7,23},{8,24},{9,... | collective-permute-start | bytes 331784 | tf_op jit(solution)/shard_map/ppermute | solution.py:99
  228.3 9.3 %collective-permute-start.33 = (bf16[1,144,384]{2,1,0:T(8,128)(2,1)S(1)}, bf16[1,144,384]{2,1,0:T(8,128)(2,1)S(1)}, u32[]{:S(2)}, u32[]{:S(2)}) collective-permute-start(bf16[1,144,384]{2,1,0:T(8,128)(2,1)S(1)} %get-tuple-element.217), channel_id=1, source_target_pairs={{0,2},{1,3},{2,0},{3,1},{4,6},{5,7},{6,4},{7,5},{8,10},{9,11},{10,... | collective-permute-start | bytes 331784 | tf_op jit(solution)/shard_map/ppermute | solution.py:99
  254.4 56.6 %all-to-all-start.3 = ((bf16[32,36,128]{2,1,0:T(8,128)(2,1)}), bf16[32,36,128]{2,1,0:T(8,128)(2,1)S(1)}, u32[]{:S(2)}, u32[]{:S(2)}) async-start(bf16[32,36,128]{2,1,0:T(8,128)(2,1)} %copy-done.42), calls=%async_computation.3 | async-start | bytes 655360 | tf_op jit(solution)/shard_map/all_to_all | solution.py:966
  258.6 10.0 %collective-permute-start.36 = (bf16[128,768]{1,0:T(8,128)(2,1)S(1)}, bf16[128,768]{1,0:T(8,128)(2,1)S(1)}, u32[]{:S(2)}, u32[]{:S(2)}) collective-permute-start(bf16[128,768]{1,0:T(8,128)(2,1)S(1)} %get-tuple-element.307), channel_id=1, source_target_pairs={{0,1},{1,0},{2,3},{3,2},{4,5},{5,4},{6,7},{7,6},{8,9},{9,8},{10,11... | collective-permute-start | bytes 589832 | tf_op jit(solution)/shard_map/ppermute | solution.py:99
  258.9 10.6 %collective-permute-start.37 = (bf16[128,768]{1,0:T(8,128)(2,1)S(1)}, bf16[128,768]{1,0:T(8,128)(2,1)S(1)}, u32[]{:S(2)}, u32[]{:S(2)}) collective-permute-start(bf16[128,768]{1,0:T(8,128)(2,1)S(1)} %get-tuple-element.306), channel_id=1, source_target_pairs={{0,2},{1,3},{2,0},{3,1},{4,6},{5,7},{6,4},{7,5},{8,10},{9,11},{10,... | collective-permute-start | bytes 589832 | tf_op jit(solution)/shard_map/ppermute | solution.py:99
  260.6 12.2 %collective-permute-start.38 = (bf16[128,768]{1,0:T(8,128)(2,1)S(1)}, bf16[128,768]{1,0:T(8,128)(2,1)S(1)}, u32[]{:S(2)}, u32[]{:S(2)}) collective-permute-start(bf16[128,768]{1,0:T(8,128)(2,1)S(1)} %get-tuple-element.305), channel_id=1, source_target_pairs={{0,3},{1,2},{2,1},{3,0},{4,7},{5,6},{6,5},{7,4},{8,11},{9,10},{10,... | collective-permute-start | bytes 589832 | tf_op jit(solution)/shard_map/ppermute | solution.py:99
  266.8 19.3 %collective-permute-start.48 = (bf16[96,960]{1,0:T(8,128)(2,1)}, bf16[96,960]{1,0:T(8,128)(2,1)S(1)}, u32[]{:S(2)}, u32[]{:S(2)}) collective-permute-start(bf16[96,960]{1,0:T(8,128)(2,1)} %get-tuple-element.269), channel_id=1, source_target_pairs={{0,8},{1,9},{2,10},{3,11},{4,12},{5,13},{6,14},{7,15},{8,0},{9,1},... | collective-permute-start | bytes 552968 | tf_op jit(solution)/shard_map/ppermute | solution.py:99
  274.2 33.2 %copy-start.46 = (bf16[96,960]{1,0:T(8,128)(2,1)S(1)}, bf16[96,960]{1,0:T(8,128)(2,1)}, u32[]{:S(2)}) copy-start(bf16[96,960]{1,0:T(8,128)(2,1)} %copy-done.45) | copy-start | bytes 552964
  274.2 33.2 %copy-start.54 = (bf16[96,768]{1,0:T(8,128)(2,1)S(1)}, bf16[96,768]{1,0:T(8,128)(2,1)}, u32[]{:S(2)}) copy-start(bf16[96,768]{1,0:T(8,128)(2,1)} %copy-done.53) | copy-start | bytes 442372
  276.9 33.2 %collective-permute-start.40 = (bf16[4,96,384]{2,1,0:T(8,128)(2,1)S(1)}, bf16[4,96,384]{2,1,0:T(8,128)(2,1)S(1)}, u32[]{:S(2)}, u32[]{:S(2)}) collective-permute-start(bf16[4,96,384]{2,1,0:T(8,128)(2,1)S(1)} %get-tuple-element.234), channel_id=1, source_target_pairs={{0,4},{1,5},{2,6},{3,7},{4,0},{5,1},{6,2},{7,3},{8,12},{9,13},{10,... | collective-permute-start | bytes 884744 | tf_op jit(solution)/shard_map/ppermute | solution.py:99
  278.7 31.4 %collective-permute-start.41 = (bf16[4,96,384]{2,1,0:T(8,128)(2,1)S(1)}, bf16[4,96,384]{2,1,0:T(8,128)(2,1)S(1)}, u32[]{:S(2)}, u32[]{:S(2)}) collective-permute-start(bf16[4,96,384]{2,1,0:T(8,128)(2,1)S(1)} %get-tuple-element.235), channel_id=1, source_target_pairs={{0,8},{1,9},{2,10},{3,11},{4,12},{5,13},{6,14},{7,15},{8,0},{9,1},... | collective-permute-start | bytes 884744 | tf_op jit(solution)/shard_map/ppermute | solution.py:99
  283.2 35.4 %collective-permute-start.44 = (bf16[2,144,768]{2,1,0:T(8,128)(2,1)}, bf16[2,144,768]{2,1,0:T(8,128)(2,1)S(1)}, u32[]{:S(2)}, u32[]{:S(2)}) collective-permute-start(bf16[2,144,768]{2,1,0:T(8,128)(2,1)} %get-tuple-element.241), channel_id=1, source_target_pairs={{0,8},{1,9},{2,10},{3,11},{4,12},{5,13},{6,14},{7,15},{8,0},{9,1},... | collective-permute-start | bytes 1327112 | tf_op jit(solution)/shard_map/ppermute | solution.py:99
  283.9 17.1 %collective-permute-start.49 = (bf16[96,960]{1,0:T(8,128)(2,1)S(1)}, bf16[96,960]{1,0:T(8,128)(2,1)S(1)}, u32[]{:S(2)}, u32[]{:S(2)}) collective-permute-start(bf16[96,960]{1,0:T(8,128)(2,1)S(1)} %copy-done.72), channel_id=1, source_target_pairs={{0,16},{1,17},{2,18},{3,19},{4,20},{5,21},{6,22},{7,23},{8,24},{9,... | collective-permute-start | bytes 552968 | tf_op jit(solution)/shard_map/ppermute | solution.py:99
  286.8 20.6 %collective-permute-start.50 = (bf16[96,960]{1,0:T(8,128)(2,1)S(1)}, bf16[96,960]{1,0:T(8,128)(2,1)S(1)}, u32[]{:S(2)}, u32[]{:S(2)}) collective-permute-start(bf16[96,960]{1,0:T(8,128)(2,1)S(1)} %copy-done.70), channel_id=1, source_target_pairs={{0,24},{1,25},{2,26},{3,27},{4,28},{5,29},{6,30},{7,31},{8,16},{9,... | collective-permute-start | bytes 552968 | tf_op jit(solution)/shard_map/ppermute | solution.py:99
  310.2 8.4 %collective-permute-start.42 = (bf16[2,96,384]{2,1,0:T(8,128)(2,1)S(1)}, bf16[2,96,384]{2,1,0:T(8,128)(2,1)S(1)}, u32[]{:S(2)}, u32[]{:S(2)}) collective-permute-start(bf16[2,96,384]{2,1,0:T(8,128)(2,1)S(1)} %get-tuple-element.237), channel_id=1, source_target_pairs={{0,8},{1,9},{2,10},{3,11},{4,12},{5,13},{6,14},{7,15},{8,0},{9,1},... | collective-permute-start | bytes 442376 | tf_op jit(solution)/shard_map/ppermute | solution.py:99
  310.3 8.3 %collective-permute-start.43 = (bf16[2,96,384]{2,1,0:T(8,128)(2,1)S(1)}, bf16[2,96,384]{2,1,0:T(8,128)(2,1)S(1)}, u32[]{:S(2)}, u32[]{:S(2)}) collective-permute-start(bf16[2,96,384]{2,1,0:T(8,128)(2,1)S(1)} %get-tuple-element.240), channel_id=1, source_target_pairs={{0,4},{1,5},{2,6},{3,7},{4,0},{5,1},{6,2},{7,3},{8,12},{9,13},{10,... | collective-permute-start | bytes 442376 | tf_op jit(solution)/shard_map/ppermute | solution.py:99
  313.1 17.2 %all-to-all-start.4 = ((f32[32,8,128]{2,1,0:T(8,128)}), f32[32,8,128]{2,1,0:T(8,128)S(1)}, u32[]{:S(2)}, u32[]{:S(2)}) async-start(f32[32,8,128]{2,1,0:T(8,128)} %get-tuple-element.248), calls=%async_computation.4 | async-start | bytes 262144 | tf_op jit(solution)/shard_map/all_to_all | solution.py:1085
  316.6 5.8 %collective-permute-start.51 = (bf16[96,384]{1,0:T(8,128)(2,1)S(1)}, bf16[96,384]{1,0:T(8,128)(2,1)S(1)}, u32[]{:S(2)}, u32[]{:S(2)}) collective-permute-start(bf16[96,384]{1,0:T(8,128)(2,1)S(1)} %get-tuple-element.313), channel_id=1, source_target_pairs={{0,1},{1,0},{2,3},{3,2},{4,5},{5,4},{6,7},{7,6},{8,9},{9,8},{10,11... | collective-permute-start | bytes 221192 | tf_op jit(solution)/shard_map/ppermute | solution.py:99
  316.9 5.8 %collective-permute-start.52 = (bf16[96,384]{1,0:T(8,128)(2,1)S(1)}, bf16[96,384]{1,0:T(8,128)(2,1)S(1)}, u32[]{:S(2)}, u32[]{:S(2)}) collective-permute-start(bf16[96,384]{1,0:T(8,128)(2,1)S(1)} %get-tuple-element.312), channel_id=1, source_target_pairs={{0,2},{1,3},{2,0},{3,1},{4,6},{5,7},{6,4},{7,5},{8,10},{9,11},{10,... | collective-permute-start | bytes 221192 | tf_op jit(solution)/shard_map/ppermute | solution.py:99
  318.6 5.1 %collective-permute-start.53 = (bf16[96,384]{1,0:T(8,128)(2,1)S(1)}, bf16[96,384]{1,0:T(8,128)(2,1)S(1)}, u32[]{:S(2)}, u32[]{:S(2)}) collective-permute-start(bf16[96,384]{1,0:T(8,128)(2,1)S(1)} %get-tuple-element.311), channel_id=1, source_target_pairs={{0,3},{1,2},{2,1},{3,0},{4,7},{5,6},{6,5},{7,4},{8,11},{9,10},{10,... | collective-permute-start | bytes 221192 | tf_op jit(solution)/shard_map/ppermute | solution.py:99
  318.7 10.7 %collective-permute-start.46 = (bf16[1,96,384]{2,1,0:T(8,128)(2,1)S(1)}, bf16[1,96,384]{2,1,0:T(8,128)(2,1)S(1)}, u32[]{:S(2)}, u32[]{:S(2)}) collective-permute-start(bf16[1,96,384]{2,1,0:T(8,128)(2,1)S(1)} %get-tuple-element.255), channel_id=1, source_target_pairs={{0,16},{1,17},{2,18},{3,19},{4,20},{5,21},{6,22},{7,23},{8,24},{9,... | collective-permute-start | bytes 221192 | tf_op jit(solution)/shard_map/ppermute | solution.py:99
  321.4 8.1 %collective-permute-start.47 = (bf16[1,96,384]{2,1,0:T(8,128)(2,1)S(1)}, bf16[1,96,384]{2,1,0:T(8,128)(2,1)S(1)}, u32[]{:S(2)}, u32[]{:S(2)}) collective-permute-start(bf16[1,96,384]{2,1,0:T(8,128)(2,1)S(1)} %get-tuple-element.258), channel_id=1, source_target_pairs={{0,16},{1,17},{2,18},{3,19},{4,20},{5,21},{6,22},{7,23},{8,24},{9,... | collective-permute-start | bytes 221192 | tf_op jit(solution)/shard_map/ppermute | solution.py:99
  326.8 13.6 %collective-permute-start.45 = (bf16[1,144,768]{2,1,0:T(8,128)(2,1)S(1)}, bf16[1,144,768]{2,1,0:T(8,128)(2,1)S(1)}, u32[]{:S(2)}, u32[]{:S(2)}) collective-permute-start(bf16[1,144,768]{2,1,0:T(8,128)(2,1)S(1)} %get-tuple-element.244), channel_id=1, source_target_pairs={{0,16},{1,17},{2,18},{3,19},{4,20},{5,21},{6,22},{7,23},{8,24},{9,... | collective-permute-start | bytes 663560 | tf_op jit(solution)/shard_map/ppermute | solution.py:99
  (88 other events, 865.8 us)
Sparse Core Ops, SparseCore 0:
  182.8 21.8 all-gather.2
where the time goes:
time: 350 us; the launch traced here: 348 us
  waiting for transfers between devices  123 us (35%)
  starting transfers between devices  82.2 us (23%)
  Pallas kernels  79.1 us (23%)
  local copies, waits for them, and re-layouts  30.8 us (9%)
  other arithmetic  16.6 us (5%)
  between operations  16.3 us (5%)
    ppermute x54, waiting for transfers between devices, swap(): return lax.ppermute(values, AXES, [(at, at ^ mask) for at in range(total)])  115 us
    ppermute x54, starting transfers between devices, swap(): return lax.ppermute(values, AXES, [(at, at ^ mask) for at in range(total)])  62.1 us
    pallas_call x28, Pallas kernels, call(): pl.pallas_call(body, out_shape=[jax.ShapeDtypeStruct(shape, kind) for sha...  39.9 us
    pallas_call x3, Pallas kernels, sweep(): pl.pallas_call(body, out_shape=[jax.ShapeDtypeStruct(shape, kind) for sha...  39.2 us
    unnamed x185, local copies, waits for them, and re-layouts  26.7 us
    concatenate x15, other arithmetic, grown(): return jnp.concatenate([values, got], axis=0)  10.9 us
    all_to_all x1, waiting for transfers between devices, shards(): lax.all_to_all(terms, AXES, split_axis=0, concat_axis=0, tiled=True)  7.87 us
    all_to_all x2, starting transfers between devices, shards(): lax.all_to_all(sent, AXES, split_axis=0, concat_axis=0, tiled=True)  7.28 us
  transfers between devices with their start and end apart: 60, of which 28 were waited for; matrix products, arithmetic and copies ran while one was open for 5% of the time, Pallas kernels for 17%

commit v1 on v0

--- a/solution.py
+++ b/solution.py
@@ -15,6 +15,7 @@
 WIDE = jnp.float32
 LANES = 128
 EXTRA = 16
+LIMIT = 24
 CURVE = 0.7978845608028654
 CUBIC = 0.044715
 
@@ -35,7 +36,7 @@
     return -(-value // step) * step
 
 
-def call(body, outs, args, scratch=(), smem=(), limit=48):
+def call(body, outs, args, scratch=(), smem=(), limit=LIMIT):
     specs = [pl.BlockSpec(memory_space=pltpu.SMEM) if at in smem else pl.BlockSpec() for at in range(len(args))]
     return pl.pallas_call(
         body,
@@ -47,7 +48,7 @@
     )(*args)
 
 
-def sweep(body, steps, ins, outs, scratch=(), limit=56):
+def sweep(body, steps, ins, outs, scratch=(), limit=40):
     return pl.pallas_call(
         body,
         out_shape=[jax.ShapeDtypeStruct(shape, kind) for shape, kind, _, _ in outs],
@@ -119,6 +120,19 @@
     half = keep.shape[0]
     keep[...] = (low[:half].astype(WIDE) + got[:half].astype(WIDE)).astype(keep.dtype)
     send[...] = (low[half:].astype(WIDE) + got[half:].astype(WIDE)).astype(send.dtype)
+
+
+def add_split_body(low, got, keep, send0, send1):
+    half, part = keep.shape[0], send0.shape[0]
+    for start, out in ((0, keep), (half, send0), (half + part, send1)):
+        here = slice(start, start + out.shape[0])
+        out[...] = (low[here].astype(WIDE) + got[here].astype(WIDE)).astype(out.dtype)
+
+
+def add_join_body(low, got0, got1, keep, send):
+    half = keep.shape[0]
+    keep[...] = (low[:half].astype(WIDE) + got0[...].astype(WIDE)).astype(keep.dtype)
+    send[...] = (low[half:].astype(WIDE) + got1[...].astype(WIDE)).astype(send.dtype)
 
 
 def fold(lows, highs, orders, waits=()):
@@ -539,14 +553,18 @@
 
 
 def write_twins(where, up_sum, down_sum, outs):
-    keep_up, send_up, keep_down, send_down = outs
+    keep_up, send_up0, send_up1, keep_down, send_down = outs
     place, twin = place_and_twin(where)
     rows, units = keep_up.shape[1], 2 * (down_sum.shape[0] - 2 * LANES) // 2
     size = (keep_up.shape[2] - units) // 2
     mine, other = slice(units, units + size), slice(units + LANES, units + LANES + size)
-    for out, at_twin, order_ in ((keep_up, twin, (mine, other)), (send_up, 1 - twin, (other, mine))):
+    for out, first, at_twin, order_ in (
+        (keep_up, 0, twin, (mine, other)),
+        (send_up0, 0, 1 - twin, (other, mine)),
+        (send_up1, 2, 1 - twin, (other, mine)),
+    ):
         for at in range(out.shape[0]):
-            here = rows_at(2 * (place ^ at) + at_twin, rows)
+            here = rows_at(2 * (place ^ (first + at)) + at_twin, rows)
             out[at, :, :units] = up_sum[here, :units].astype(LOW)
             for number, cols in enumerate(order_):
                 start = units + number * size
@@ -557,12 +575,16 @@
         out[half:] = down_sum[rows_].astype(out.dtype)
 
 
-def twins_body(keep_up, got_up, keep_down, got_down, grad_down, shared_down, *ups):
+def twin_up_body(keep, got0, got1, *ups):
     for at, out in enumerate(ups):
-        out[...] = (keep_up[at].astype(WIDE) + got_up[at].astype(WIDE)).astype(LOW)
+        got = (got0, got1)[at // 2][at % 2]
+        out[...] = (keep[at].astype(WIDE) + got.astype(WIDE)).astype(LOW)
+
+
+def twin_down_body(keep, got, grad_down, shared_down):
     half = grad_down.shape[0]
-    grad_down[...] = keep_down[:half] + got_down[:half].astype(WIDE)
-    shared_down[...] = (keep_down[half:] + got_down[half:].astype(WIDE)).astype(LOW)
+    grad_down[...] = keep[:half] + got[:half].astype(WIDE)
+    shared_down[...] = (keep[half:] + got[half:].astype(WIDE)).astype(LOW)
 
 
 def up_rows_body(where, up0, up1, up2, up3, shared_down, grad_up, sent):
@@ -592,13 +614,13 @@
         grad_down[source * size : (source + 1) * size] = held[source, :, 2 * size :].astype(WIDE)
 
 
-def attn_terms_body(masks, where, both, cols0, cols1, cols2, cols3, low0, low1, high0, high1, term):
-    expert, group = where[1], where[2]
-    width = both.shape[2] // 2
+def attn_terms_body(masks, where, both0, both1, both2, both3, cols0, cols1, cols2, cols3, low0, low1, high0, high1, term):
+    group = where[2]
+    width = both0.shape[1] // 2
     cut = 3 * width // 4
     rows = low0.shape[1]
-    for at, cols in enumerate((cols0, cols1, cols2, cols3)):
-        inputs = both[expert ^ at]
+    pairs = zip((both0, both1, both2, both3), (cols0, cols1, cols2, cols3))
+    for at, (inputs, cols) in enumerate(pairs):
         parts = (dot_tn(inputs[:, :width], cols[:, :cut]), dot_tn(inputs[:, width:], cols[:, cut:]))
         for start, part in ((0, parts[0]), (cut, parts[1])):
             here = slice(start, start + part.shape[1])
@@ -733,13 +755,14 @@
 
     attn_w = jnp.concatenate([qkv_weight, out_weight], axis=1)[None]
     cot = cotangent[None]
+    down_own = jnp.concatenate([expert_down[0], shared_down], axis=0)
+    down_other = swap(down_own, far[0])
     first_links = far[1:] + away
     for at, mask in enumerate(first_links):
         attn_got = swap(attn_w, mask)
-        if at == len(far) - 1:
+        if at == 0:
             cot_got = swap(cot, away[0])
-            attn_got, cot_got, cond_all = together(attn_got, cot_got, cond_all)
-            cot = grown(cot, cot_got)
+            attn_got, cond_all = together(attn_got, cond_all)
             terms, loads = call(
                 terms_body,
                 [((total, up_to(up_to(piece, 8) + lines, 8), LANES), LOW), ((1, LANES), WIDE)],
@@ -747,15 +770,11 @@
                 smem=(0,),
             )
             terms_got = lax.all_to_all(terms, AXES, split_axis=0, concat_axis=0, tiled=True)
+        if at == len(first_links) - 1:
+            attn_got, terms, down_other, cot_got = together(attn_got, terms, down_other, cot_got)
+            cot = grown(cot, cot_got)
         attn_w = grown(attn_w, attn_got)
-        if at == len(first_links) - 1:
-            cot_links = away[:1] + across[:1]
-            cot_got = swap(cot, across[0])
-            attn_w, cot_got, terms = together(attn_w, cot_got, terms)
-            cot = grown(cot, cot_got)
-    cot_links = away[:1] + across + away[1:]
-    for mask in across[1:]:
-        cot = grown(cot, swap(cot, mask))
+    cot_links = away + across
     tallies = loads[0, group_rows : group_rows + experts + 1]
     expert_load = tallies[:experts] * experts / (2.0 * tallies[experts])
     attn_parts = [attn_w[:, :, : 2 * width], attn_w[:, :, 2 * width :]]
@@ -766,28 +785,30 @@
         up_near, up_away = call(
             up_sent_body, [((2, group_rows, place_units), LOW)] * 2, (where, expert_up[0]), smem=(0,)
         )
-        down_own = jnp.concatenate([expert_down[0], shared_down], axis=0)
-        down_other = swap(down_own, far[0])
     for at in range(len(last_links[0])):
         got = [swap(part, masks[at]) for part, masks in zip(attn_parts, last_links)]
         if at == 0:
-            cot_got = swap(cot, away[1])
             if paired:
                 up_got = swap(up_away, away[0])
                 got, up_got = together(got, up_got)
         elif at == len(last_links[0]) - 1:
-            got, cot_got = together(got, cot_got)
-            cot_low = grown(cot, cot_got)
-            if paired:
-                got, down_other = together(got, down_other)
+            cot_got = swap(cot, away[1])
+            got, cot_got, terms_got = together(got, cot_got, terms_got)
+            cot = grown(cot, cot_got)
         attn_parts = [grown(*pair) for pair in zip(attn_parts, got)]
+    part_shared_up = terms_got[:, :piece, :shared_units].reshape(width, shared_units)
     modulation, own_lines = call(
         functools.partial(shift_body, piece),
         [((1, 6 * width), WIDE), ((total, 16, LANES), WIDE)],
         (terms_got, pair_weight),
     )
     attn_far = [swap(part, core[0]) for part in attn_parts]
-    cot_high = swap(cot_low, core[0])
+    cot_got = swap(cot, across[0])
+    if paired:
+        up_mine = jnp.stack([up_near[0], up_got[0]])
+        up_sent = jnp.stack([up_near[1], up_got[1]])
+        up_last = swap(up_sent, away[1])
+        shared_up_other = swap(part_shared_up, far[0])
     weights = []
     row_places = []
     for low, high, masks in zip(attn_parts, attn_far, weight_links):
@@ -809,7 +830,6 @@
         smem=(0, 3),
     )
 
-    part_shared_up = terms_got[:, :piece, :shared_units].reshape(width, shared_units)
     shared_slot = up_to(shared_units, LANES)
     second_low = [part[None] for part in seconds]
     for at in range(len(away + across)):
@@ -817,16 +837,13 @@
         if at == 0:
             item_lines = lax.all_to_all(tie(own_lines, *seconds), AXES, split_axis=0, concat_axis=0, tiled=True)
             if paired:
-                up_mine = jnp.stack([up_near[0], up_got[0]])
-                up_sent = jnp.stack([up_near[1], up_got[1]])
-                up_last = swap(up_sent, away[1])
-                got, up_last = together(got, up_last)
+                got, up_last, shared_up_other = together(got, up_last, shared_up_other)
                 up_own = jnp.concatenate([up_mine, up_last], axis=0)
                 up_other = swap(up_own, far[0])
-                shared_up_other = swap(part_shared_up, far[0])
         elif at == 1:
             got, item_lines = together(got, item_lines)
             if paired:
+                got, up_other = together(got, up_other)
                 routed, hidden = 2 * units, 2 * units + 2 * shared_slot
                 (down_cat,) = call(
                     down_join_body, [((hidden, width), LOW)], (where, down_own, down_other), smem=(0,)
@@ -889,6 +906,10 @@
 
     scalars = (where, None, None)
 
+    cot_low = grown(cot, tie(cot_got, *second_low))
+    for mask in across[1:]:
+        cot_low = grown(cot_low, swap(cot_low, mask))
+    cot_high = swap(cot_low, core[0])
     cots = [block_in(cot_low, cot_links), block_in(cot_high, cot_links)]
     d_act, d_mlp = sweep(
         functools.partial(d_act_body, links),
@@ -913,10 +934,16 @@
     )
     parts = [flat(part) for part in parts]
     if paired:
+        both_sent = tie(both, *second_high)
+        both_group = [swap(both_sent, mask) for mask in range(1, 4)]
+        parts, both_group = together(parts, both_group)
+        both_group = [both] + both_group
+    if paired:
         up_lanes = place_units + 2 * shared_units
         sum_outs = [
             sum_out((4, group_rows, up_lanes), LOW),
-            sum_out((4, group_rows, up_lanes), LOW),
+            sum_out((2, group_rows, up_lanes), LOW),
+            sum_out((2, group_rows, up_lanes), LOW),
             sum_out((units + shared_units, width), WIDE),
             sum_out((units + shared_units, width), LOW),
         ]
@@ -933,24 +960,43 @@
     lows, highs, orders = list(parts[:2]), list(parts[2:4]), [masks + core for masks in team_links]
     out_low, out_high, out_order = parts[4], parts[5], away + across + core
     sums_at = len(orders[0]) - 1
+    out_got = swap(out_high, core[0])
     for at in range(sums_at + 1):
         got = [swap(high, masks[-1 - at]) for high, masks in zip(highs, orders)]
-        if at in (0, 2):
-            out_got = swap(out_high, out_order[-1 - at // 2])
         if at == 1:
             got, grads, out_got = together(got, list(grads), out_got)
             if paired:
-                twin_up, twin_down = swap(grads[1], far[0]), swap(grads[3], far[0])
-        elif at < sums_at or not paired:
+                keep_up, send_up0, send_up1, keep_down, send_down = grads
+                twin_up0, twin_up1 = swap(send_up0, far[0]), swap(send_up1, far[0])
+                twin_down = swap(send_down, far[0])
+        elif at == 2 and paired:
+            out_got = swap(out_send0, across[0])
+            got, out_got, twin_up0 = together(got, out_got, twin_up0)
+        elif at == sums_at and paired:
+            out_got1 = swap(out_send1, across[0])
+            got, twin_up1 = together(got, twin_up1)
+        else:
             got = together(*got)
-        else:
-            got, twin_up, twin_down = together(got, twin_up, twin_down)
         if at < sums_at:
             pairs = [added(low, other) for low, other in zip(lows, got)]
             lows, highs = [pair[0] for pair in pairs], [pair[1] for pair in pairs]
-        if at == 1:
-            out_low, out_high = added(out_low, out_got)
+        if at == 1 and paired:
+            block = out_low.shape[1:]
+            out_low, out_send0, out_send1 = call(
+                add_split_body,
+                [((4, *block), LOW), ((2, *block), LOW), ((2, *block), LOW)],
+                (out_low, out_got),
+            )
+        elif at == 1:
+            for mask in reversed((away + across)):
+                out_low, out_high = added(out_low, out_got)
+                out_got = swap(out_high, mask)
     folded = [half_[0] for pair in zip(lows, got) for half_ in pair]
+    if paired:
+        up_own = call(twin_up_body, [((group_rows, up_lanes), LOW)] * 4, (keep_up, twin_up0, twin_up1))
+        folded, up_own = together(folded, up_own)
+        up_got = [piece_ if at < 2 else swap(piece_, away_masks[at]) for at, piece_ in enumerate(up_own)]
+
     grad_tokens, d_cols, d_mod_sent = call(
         functools.partial(backward_body, piece),
         [(tall, WIDE), ((experts, count, 4 * width // experts), LOW), ((total, lines, LANES), LOW)],
@@ -962,32 +1008,50 @@
         smem=(0, 4),
     )
 
-    both_group = lax.all_gather(tie(both, *second_high), "expert", axis=0)
     d_mod_all = lax.all_to_all(d_mod_sent, AXES, split_axis=0, concat_axis=0, tiled=True)
     if paired:
+        d_cols, up_got[2], out_got1 = together(d_cols, up_got[2], out_got1)
         cols_got = [d_cols[at] if not at else swap(d_cols[at], at) for at in range(4)]
-        cols_got, out_got = together(cols_got, out_got)
+        out_low, out_high = call(
+            add_join_body, [((2, *block), LOW), ((2, *block), LOW)], (out_low, out_got, out_got1)
+        )
+        cols_got, up_got, twin_down = together(cols_got, up_got, twin_down)
+        out_got = swap(out_high, away[1])
+        up_got[1] = swap(up_got[1], away_masks[1])
+        grad_expert_down, shared_own = call(
+            twin_down_body, [((units, width), WIDE), ((shared_units, width), LOW)], (keep_down, twin_down)
+        )
         sum_links = [away + far, away[:1] + far + away[1:]]
         sum_masks = [[mask // experts for mask in order(masks)] for masks in sum_links]
         term_half = ((4, group_rows, width // 2), LOW)
         attn_sent = call(
             functools.partial(attn_terms_body, sum_masks),
             [term_half] * 4,
-            (where, both_group, *cols_got),
+            (where, *both_group, *cols_got),
             scratch=[((width, width), WIDE)],
             smem=(0,),
         )
-        out_low, out_high = added(out_low, out_got)
-        out_got = swap(out_high, out_order[-3])
         term_lows, term_highs = attn_sent[:2], attn_sent[2:]
         for at in range(3):
             got = [swap(high, masks[-1 - at]) for high, masks in zip(term_highs, sum_links)]
-            if at == 1:
+            if at == 0:
                 got, out_got = together(got, out_got)
                 out_low, out_high = added(out_low, out_got)
-                out_got = swap(out_high, out_order[-4])
+                out_got = swap(out_high, away[0])
+            elif at == 1:
+                got, up_got = together(got, up_got)
+                grad_expert_up, crossed = call(
+                    up_rows_body,
+                    [
+                        ((group_rows, groups * units), WIDE),
+                        ((4, group_rows, 2 * shared_units + width // experts), LOW),
+                    ],
+                    (where, *up_got, shared_own),
+                    smem=(0,),
+                )
+                crossed = [crossed[mask] if not mask else swap(crossed[mask], mask) for mask in range(4)]
             else:
-                got = together(*got)
+                got, out_got, crossed = together(got, out_got, crossed)
             if at < 2:
                 pairs = [added(low, other) for low, other in zip(term_lows, got)]
                 term_lows, term_highs = [pair[0] for pair in pairs], [pair[1] for pair in pairs]
@@ -999,6 +1063,7 @@
         )
     else:
         natural = jnp.arange(experts, dtype=jnp.int32) ^ my_expert
+        both_group = lax.all_gather(both, "expert", axis=0)
         d_cols = jnp.take(d_cols, natural, axis=0)
         d_cols = lax.all_to_all(d_cols, "expert", split_axis=0, concat_axis=0, tiled=True)
         (attn_terms,) = call(
@@ -1010,9 +1075,6 @@
             [((group_rows, 3 * width // experts), WIDE), ((group_rows, width // experts), WIDE)],
             (attn_terms,),
         )
-        for mask in reversed(out_order[:-2]):
-            out_low, out_high = added(out_low, out_got)
-            out_got = swap(out_high, mask)
 
     block_out, grad_gate_weights = call(
         finish_body,
@@ -1022,26 +1084,6 @@
     )
 
     if paired:
-        grad_expert_down, shared_own, *up_own = call(
-            twins_body,
-            [
-                ((units, width), WIDE),
-                ((shared_units, width), LOW),
-                *[((group_rows, up_lanes), LOW)] * 4,
-            ],
-            (grads[0], twin_up, grads[2], twin_down),
-        )
-        up_got = [piece if not mask else swap(piece, mask) for piece, mask in zip(up_own, away_masks)]
-        grad_expert_up, crossed = call(
-            up_rows_body,
-            [
-                ((group_rows, groups * units), WIDE),
-                ((4, group_rows, 2 * shared_units + width // experts), LOW),
-            ],
-            (where, *up_got, shared_own),
-            smem=(0,),
-        )
-        crossed = [crossed[at] if not at else swap(crossed[at], at) for at in range(4)]
         grad_shared_up, grad_shared_down = call(
             shared_rows_body,
             [((group_rows, width), WIDE), ((experts * shared_units, width // experts), WIDE)],

time: 350 us -> 288 us (0.82)
  waiting for transfers between devices: 123 us -> 90 us
  between operations: 16.3 us -> 3.15 us
  local copies, waits for them, and re-layouts: 30.8 us -> 18.9 us
  Pallas kernels: 79.1 us -> 73.8 us
    ppermute x54 -> x59, waiting for transfers between devices: 115 us -> 90 us  [swap(): return lax.ppermute(values, AXES, [(at, at ^ mask) for at in range(total)])]
    unnamed x185 -> x195, local copies, waits for them, and re-layouts: 26.7 us -> 14.8 us
    all_to_all x1, waiting for transfers between devices: 7.87 us -> 0.01 us  [shards(): lax.all_to_all(terms, AXES, split_axis=0, concat_axis=0, tiled=True)]
    pallas_call x3, Pallas kernels: 39.2 us -> 33 us  [sweep(): pl.pallas_call(body, out_shape=[jax.ShapeDtypeStruct(shape, kind) for sha...]
    pallas_call x28 -> x29, Pallas kernels: 39.9 us -> 40.8 us  [call(): pl.pallas_call(body, out_shape=[jax.ShapeDtypeStruct(shape, kind) for sha...]
    ppermute x54 -> x59, starting transfers between devices: 62.1 us -> 61.2 us  [swap(): return lax.ppermute(values, AXES, [(at, at ^ mask) for at in range(total)])]
  transfers between devices with their start and end apart: 60 -> 64, of which waited for: 28 -> 28; matrix products, arithmetic and copies ran while one was open for 5% -> 6% of each run, Pallas kernels for 17% -> 24%
where the time goes in v1:
time: 288 us; the launch traced here: 287 us
  waiting for transfers between devices  90 us (31%)
  starting transfers between devices  82.1 us (29%)
  Pallas kernels  73.8 us (26%)
  other arithmetic  19.2 us (7%)
  local copies, waits for them, and re-layouts  18.9 us (7%)
  between operations  3.15 us (1%)
    ppermute x59, waiting for transfers between devices, swap(): return lax.ppermute(values, AXES, [(at, at ^ mask) for at in range(total)])  90 us
    ppermute x59, starting transfers between devices, swap(): return lax.ppermute(values, AXES, [(at, at ^ mask) for at in range(total)])  61.2 us
    pallas_call x29, Pallas kernels, call(): pl.pallas_call(body, out_shape=[jax.ShapeDtypeStruct(shape, kind) for sha...  40.8 us
    pallas_call x3, Pallas kernels, sweep(): pl.pallas_call(body, out_shape=[jax.ShapeDtypeStruct(shape, kind) for sha...  33 us
    unnamed x195, local copies, waits for them, and re-layouts  14.8 us
    concatenate x15, other arithmetic, grown(): return jnp.concatenate([values, got], axis=0)  14.1 us
    all_to_all x2, starting transfers between devices, shards(): lax.all_to_all(sent, AXES, split_axis=0, concat_axis=0, tiled=True)  10.6 us
  transfers between devices with their start and end apart: 64, of which 28 were waited for; matrix products, arithmetic and copies ran while one was open for 6% of the time, Pallas kernels for 24%

profile of v1, /device:TPU:0, one launch (start us, length us, event | category | flops | bytes accessed | tf_op | source)
XLA Modules:
  0.0 287.2 jit_solution(17622920217141569947)
XLA Ops:
  4.2 7.3 %all-to-all-start = ((bf16[32,16,128]{2,1,0:T(8,128)(2,1)}), bf16[32,16,128]{2,1,0:T(8,128)(2,1)S(1)}, u32[]{:S(2)}, u32[]{:S(2)}) async-start(bf16[32,16,128]{2,1,0:T(8,128)(2,1)} %get-tuple-element.186), calls=%async_computation | async-start | bytes 262144 | tf_op jit(solution)/shard_map/all_to_all | solution.py:754
  12.5 2.7 collective-permute-start
  16.5 1.5 collective-permute-start.2
  18.0 6.4 %collective-permute-done = bf16[1,24,3072]{2,1,0:T(8,128)(2,1)S(1)} collective-permute-done((bf16[1,24,3072]{2,1,0:T(8,128)(2,1)S(1)}, bf16[1,24,3072]{2,1,0:T(8,128)(2,1)S(1)}, u32[]{:S(2)}, u32[]{:S(2)}) %collective-permute-start) | collective-permute-done | bytes 147488 | tf_op jit(solution)/shard_map/ppermute | solution.py:100
  25.2 2.3 collective-permute-start.3
  29.6 2.6 shard_map.256
  32.2 4.9 %collective-permute-done.3 = bf16[1,128,768]{2,1,0:T(8,128)(2,1)S(1)} collective-permute-done((bf16[1,128,768]{2,1,0:T(8,128)(2,1)S(1)}, bf16[1,128,768]{2,1,0:T(8,128)(2,1)S(1)}, u32[]{:S(2)}, u32[]{:S(2)}) %collective-permute-start.3) | collective-permute-done | bytes 196640 | tf_op jit(solution)/shard_map/ppermute | solution.py:100
  37.1 3.1 %collective-permute-done.1 = bf16[2,24,3072]{2,1,0:T(8,128)(2,1)} collective-permute-done((bf16[2,24,3072]{2,1,0:T(8,128)(2,1)}, bf16[2,24,3072]{2,1,0:T(8,128)(2,1)}, u32[]{:S(2)}, u32[]{:S(2)}) %collective-permute-start.1) | collective-permute-done | bytes 294944 | tf_op jit(solution)/shard_map/ppermute | solution.py:100
  41.6 1.5 collective-permute-start.4
  43.1 1.5 collective-permute-start.5
  44.6 2.6 all-to-all-start.1
  47.2 2.4 collective-permute-done.6
  49.9 4.1 %collective-permute-done.5 = bf16[4,24,1536]{2,1,0:T(8,128)(2,1)S(1)} collective-permute-done((bf16[4,24,1536]{2,1,0:T(8,128)(2,1)S(1)}, bf16[4,24,1536]{2,1,0:T(8,128)(2,1)S(1)}, u32[]{:S(2)}, u32[]{:S(2)}) %collective-permute-start.5) | collective-permute-done | bytes 294944 | tf_op jit(solution)/shard_map/ppermute | solution.py:100
  54.0 2.8 collective-permute-start.7
  57.7 9.5 %collective-permute-done.9 = bf16[2,128,768]{2,1,0:T(8,128)(2,1)S(1)} collective-permute-done((bf16[2,128,768]{2,1,0:T(8,128)(2,1)S(1)}, bf16[2,128,768]{2,1,0:T(8,128)(2,1)S(1)}, u32[]{:S(2)}, u32[]{:S(2)}) %collective-permute-start.9) | collective-permute-done | bytes 393248 | tf_op jit(solution)/shard_map/ppermute | solution.py:100
  67.2 2.2 collective-permute-done.7
  76.6 3.8 %shard_map.259 = (bf16[128,1536]{1,0:T(8,128)(2,1)S(1)}, bf16[128,2304]{1,0:T(8,128)(2,1)S(1)}, f32[128,128]{1,0:T(8,128)S(1)}, f32[128,768]{1,0:T(8,128)S(1)}, ...) custom-call(s32[3]{0:T(128)S(1)} %pad_add_fusion.where, ...), custom_call_target="tpu_custom_call" | custom-call | tf_op jit(solution)/shard_map/pallas_call | solution.py:41
  80.5 2.5 collective-permute-start.12
  83.6 4.3 %collective-permute-done.12 = bf16[1,128,384]{2,1,0:T(8,128)(2,1)S(1)} collective-permute-done((bf16[1,128,384]{2,1,0:T(8,128)(2,1)S(1)}, bf16[1,128,384]{2,1,0:T(8,128)(2,1)S(1)}, u32[]{:S(2)}, u32[]{:S(2)}) %collective-permute-start.12) | collective-permute-done | bytes 98336 | tf_op jit(solution)/shard_map/ppermute | solution.py:100
  92.4 4.1 %all-to-all-start.2 = ((f32[32,16,128]{2,1,0:T(8,128)}), f32[32,16,128]{2,1,0:T(8,128)}, u32[]{:S(2)}, u32[]{:S(2)}) async-start(f32[32,16,128]{2,1,0:T(8,128)} %copy-done.55), calls=%async_computation.2 | async-start | bytes 524288 | tf_op jit(solution)/shard_map/all_to_all | solution.py:838
  97.6 1.6 collective-permute-start.16
  100.1 2.5 collective-permute-start.17
  102.6 8.9 %collective-permute-done.16 = bf16[2,128,384]{2,1,0:T(8,128)(2,1)} collective-permute-done((bf16[2,128,384]{2,1,0:T(8,128)(2,1)S(1)}, bf16[2,128,384]{2,1,0:T(8,128)(2,1)}, u32[]{:S(2)}, u32[]{:S(2)}) %collective-permute-start.16) | collective-permute-done | bytes 196640 | tf_op jit(solution)/shard_map/ppermute | solution.py:100
  111.5 2.7 collective-permute-done.17
  118.0 1.5 collective-permute-start.19
  120.5 1.5 shard_map.262.refs_8_
  122.0 5.2 %shard_map.261 = (bf16[4,512,1024]{2,1,0:T(8,128)(2,1)S(1)}, bf16[4,512,768]{2,1,0:T(8,128)(2,1)S(1)}) custom-call(s32[3]{0:T(128)S(1)} %pad_add_fusion.where, bf16[2,2,2,128,768]{4,3,2,1,0:T(8,128)(2,1)S(1)} %bitcast.61, bf16[2,2,2,128,768]{4,3,2,1,0:T(8,128)(2,1)S(1)} %bitcast.71, f32[32,16,128]{2,1,0:T(8,128)} %all-to-all-done.2.lines.refs_6_, ...), custom_call_target="tpu_custom_call" | custom-call | tf_op jit(solution)/shard_map/pallas_call | solution.py:52
  127.3 2.0 copy-done.3
  133.5 1.8 collective-permute-done.23
  138.2 17.0 %shard_map.263 = (bf16[2,2,2,144,384]{4,3,2,1,0:T(8,128)(2,1)S(1)}, bf16[2,2,2,144,384]{4,3,2,1,0:T(8,128)(2,1)S(1)}, bf16[2,2,2,144,384]{4,3,2,1,0:T(8,128)(2,1...) custom-call(s32[3]{0:T(128)S(1)} %pad_add_fusion.where, ...), custom_call_target="tpu_custom_call" | custom-call | tf_op jit(solution)/shard_map/pallas_call | solution.py:52
  156.7 4.1 %collective-permute-done.28.got = bf16[8,144,384]{2,1,0:T(8,128)(2,1)S(1)} collective-permute-done((bf16[8,144,384]{2,1,0:T(8,128)(2,1)S(1)}, bf16[8,144,384]{2,1,0:T(8,128)(2,1)S(1)}, u32[]{:S(2)}, u32[]{:S(2)}) %collective-permute-start.28) | collective-permute-done | bytes 884768 | tf_op jit(solution)/shard_map/ppermute | solution.py:100
  163.5 2.2 copy-done.2
  165.7 10.8 %shard_map.266 = (bf16[4,96,960]{2,1,0:T(8,128)(2,1)S(1)}, bf16[2,96,960]{2,1,0:T(8,128)(2,1)S(1)}, bf16[2,96,960]{2,1,0:T(8,128)(2,1)S(1)}, f32[480,768]{1,0:T(8,128)S(1)}, bf16[480,768]{1,0:T(8,128)(2,1)}) custom-call(s32[3]{0:T(128)S(1)} %pad_add_fusion.where, bf16[2,2,2,128,384]{4,3,2,1,0:T(8,128)(2,1)S(1)} %bitcast.68, ...), custom_call_target="tpu_custom_call" | custom-call | tf_op jit(solution)/shard_map/pallas_call | solution.py:52
  177.8 1.5 collective-permute-start.35
  179.2 1.5 collective-permute-start.36
  180.8 1.8 collective-permute-start.33
  183.7 6.9 %collective-permute-done.33.got = bf16[2,144,384]{2,1,0:T(8,128)(2,1)S(1)} collective-permute-done((bf16[2,144,384]{2,1,0:T(8,128)(2,1)S(1)}, bf16[2,144,384]{2,1,0:T(8,128)(2,1)S(1)}, u32[]{:S(2)}, u32[]{:S(2)}) %collective-permute-start.33) | collective-permute-done | bytes 221216 | tf_op jit(solution)/shard_map/ppermute | solution.py:100
  191.1 4.0 %collective-permute-done.34.got = bf16[2,144,384]{2,1,0:T(8,128)(2,1)S(1)} collective-permute-done((bf16[2,144,384]{2,1,0:T(8,128)(2,1)S(1)}, bf16[2,144,384]{2,1,0:T(8,128)(2,1)S(1)}, u32[]{:S(2)}, u32[]{:S(2)}) %collective-permute-start.34) | collective-permute-done | bytes 221216 | tf_op jit(solution)/shard_map/ppermute | solution.py:100
  198.6 3.0 %collective-permute-done.37 = bf16[1,144,384]{2,1,0:T(8,128)(2,1)S(1)} collective-permute-done((bf16[1,144,384]{2,1,0:T(8,128)(2,1)S(1)}, bf16[1,144,384]{2,1,0:T(8,128)(2,1)S(1)}, u32[]{:S(2)}, u32[]{:S(2)}) %collective-permute-start.37) | collective-permute-done | bytes 110624 | tf_op jit(solution)/shard_map/ppermute | solution.py:100
  202.6 2.1 collective-permute-start.40
  204.7 1.7 collective-permute-start.45
  206.4 7.7 %shard_map.273 = (f32[128,768]{1,0:T(8,128)}, bf16[4,128,768]{2,1,0:T(8,128)(2,1)S(1)}, bf16[32,36,128]{2,1,0:T(8,128)(2,1)S(1)}) custom-call(s32[3]{0:T(128)S(1)} %pad_add_fusion.where, bf16[128,768]{1,0:T(8,128)(2,1)S(1)} %copy-done.28, bf16[128,768]{1,0:T(8,128)(2,1)S(1)} %copy-done.6, f32[1,4608]{1,0:T(1,128)S(1)} %copy-done.61, s32[1]{0:T(128)S(6)} %copy.31.lengths, ...), custom_call_target="tpu_custom_call" | custom-call | tf_op jit(solution)/shard_map/pallas_call | solution.py:41
  215.8 3.6 %all-to-all-start.3 = ((bf16[32,36,128]{2,1,0:T(8,128)(2,1)}), bf16[32,36,128]{2,1,0:T(8,128)(2,1)S(1)}, u32[]{:S(2)}, u32[]{:S(2)}) async-start(bf16[32,36,128]{2,1,0:T(8,128)(2,1)} %copy-done.50), calls=%async_computation.3 | async-start | bytes 655360 | tf_op jit(solution)/shard_map/all_to_all | solution.py:1011
  221.2 1.7 collective-permute-start.43
  222.9 1.9 shard_map.274
  224.8 1.8 collective-permute-start.49
  226.5 4.2 %collective-permute-done.43.cols2 = bf16[128,768]{1,0:T(8,128)(2,1)S(1)} collective-permute-done((bf16[128,768]{1,0:T(8,128)(2,1)S(1)}, bf16[128,768]{1,0:T(8,128)(2,1)S(1)}, u32[]{:S(2)}, u32[]{:S(2)}) %collective-permute-start.43) | collective-permute-done | bytes 196640 | tf_op jit(solution)/shard_map/ppermute | solution.py:100
  230.7 4.0 %collective-permute-done.44.cols3 = bf16[128,768]{1,0:T(8,128)(2,1)S(1)} collective-permute-done((bf16[128,768]{1,0:T(8,128)(2,1)S(1)}, bf16[128,768]{1,0:T(8,128)(2,1)S(1)}, u32[]{:S(2)}, u32[]{:S(2)}) %collective-permute-start.44) | collective-permute-done | bytes 196640 | tf_op jit(solution)/shard_map/ppermute | solution.py:100
  234.7 3.3 %shard_map.275 = (bf16[4,96,384]{2,1,0:T(8,128)(2,1)S(1)}, bf16[4,96,384]{2,1,0:T(8,128)(2,1)S(1)}, bf16[4,96,384]{2,1,0:T(8,128)(2,1)}, bf16[4,96,384]{2,1,0:T(8,128)(2,1)}) custom-call(s32[3]{0:T(128)S(1)} %pad_add_fusion.where, bf16[128,1536]{1,0:T(8,128)(2,1)S(1)} %copy-done.41, bf16[128,1536]{1,0:T(8,128)(2,1)S(1)} %copy-done.45, ...), custom_call_target="tpu_custom_call" | custom-call | tf_op jit(solution)/shard_map/pallas_call | solution.py:41
  238.8 1.5 collective-permute-start.47
  243.6 2.1 shard_map.284
  247.0 3.3 %all-to-all-start.4 = ((f32[32,8,128]{2,1,0:T(8,128)}), f32[32,8,128]{2,1,0:T(8,128)}, u32[]{:S(2)}, u32[]{:S(2)}) async-start(f32[32,8,128]{2,1,0:T(8,128)} %copy-done.64), calls=%async_computation.4 | async-start | bytes 262144 | tf_op jit(solution)/shard_map/all_to_all | solution.py:1127
  251.4 1.7 shard_map.277
  253.1 1.5 collective-permute-start.50
  254.6 1.7 shard_map.278
  256.3 1.5 collective-permute-start.51
  258.3 2.3 shard_map.281
  261.4 2.5 collective-permute-start.55
  266.7 2.3 collective-permute-start.54
  268.9 2.3 shard_map.282
  271.3 1.5 collective-permute-start.57
  273.9 5.0 %collective-permute-done.53 = bf16[1,96,384]{2,1,0:T(8,128)(2,1)S(1)} collective-permute-done((bf16[1,96,384]{2,1,0:T(8,128)(2,1)S(1)}, bf16[1,96,384]{2,1,0:T(8,128)(2,1)S(1)}, u32[]{:S(2)}, u32[]{:S(2)}) %collective-permute-start.53) | collective-permute-done | bytes 73760 | tf_op jit(solution)/shard_map/ppermute | solution.py:100
  280.5 2.8 collective-permute-done.58.got3
  283.3 1.4 shard_map.286
  (324 shorter events, 66.3 us)
Async XLA Ops:
  4.2 20.2 %all-to-all-start = ((bf16[32,16,128]{2,1,0:T(8,128)(2,1)}), bf16[32,16,128]{2,1,0:T(8,128)(2,1)S(1)}, u32[]{:S(2)}, u32[]{:S(2)}) async-start(bf16[32,16,128]{2,1,0:T(8,128)(2,1)} %get-tuple-element.186), calls=%async_computation | async-start | bytes 262144 | tf_op jit(solution)/shard_map/all_to_all | solution.py:754
  12.5 11.9 %collective-permute-start = (bf16[1,24,3072]{2,1,0:T(8,128)(2,1)S(1)}, bf16[1,24,3072]{2,1,0:T(8,128)(2,1)S(1)}, u32[]{:S(2)}, u32[]{:S(2)}) collective-permute-start(bf16[1,24,3072]{2,1,0:T(8,128)(2,1)S(1)} %maximum_bitcast_fusion), channel_id=1, source_target_pairs={{0,16},{1,17},{2,18},{3,19},{4,20},{5,21},{6,22},{7,23},{8,24},{9,... | collective-permute-start | bytes 442376 | tf_op jit(solution)/shard_map/ppermute | solution.py:100
  16.5 23.7 %collective-permute-start.2 = (bf16[480,768]{1,0:T(8,128)(2,1)S(1)}, bf16[480,768]{1,0:T(8,128)(2,1)S(1)}, u32[]{:S(2)}, u32[]{:S(2)}) collective-permute-start(bf16[480,768]{1,0:T(8,128)(2,1)S(1)} %pad_maximum_fusion.6.own), channel_id=1, source_target_pairs={{0,4},{1,5},{2,6},{3,7},{4,0},{5,1},{6,2},{7,3},{8,12},{9,13},{10,... | collective-permute-start | bytes 2211848 | tf_op jit(solution)/shard_map/ppermute | solution.py:100
  25.2 14.9 %collective-permute-start.1 = (bf16[2,24,3072]{2,1,0:T(8,128)(2,1)}, bf16[2,24,3072]{2,1,0:T(8,128)(2,1)}, u32[]{:S(2)}, u32[]{:S(2)}) collective-permute-start(bf16[2,24,3072]{2,1,0:T(8,128)(2,1)} %pad_maximum_fusion.14), channel_id=1, source_target_pairs={{0,8},{1,9},{2,10},{3,11},{4,12},{5,13},{6,14},{7,15},{8,0},{9,1},... | collective-permute-start | bytes 884744 | tf_op jit(solution)/shard_map/ppermute | solution.py:100
  25.2 11.9 %collective-permute-start.3 = (bf16[1,128,768]{2,1,0:T(8,128)(2,1)S(1)}, bf16[1,128,768]{2,1,0:T(8,128)(2,1)S(1)}, u32[]{:S(2)}, u32[]{:S(2)}) collective-permute-start(bf16[1,128,768]{2,1,0:T(8,128)(2,1)S(1)} %bitcast.77), channel_id=1, source_target_pairs={{0,16},{1,17},{2,18},{3,19},{4,20},{5,21},{6,22},{7,23},{8,24},{9,... | collective-permute-start | bytes 589832 | tf_op jit(solution)/shard_map/ppermute | solution.py:100
  28.9 20.7 %collective-permute-start.6 = (bf16[2,96,768]{2,1,0:T(8,128)(2,1)S(1)}, bf16[2,96,768]{2,1,0:T(8,128)(2,1)}, u32[]{:S(2)}, u32[]{:S(2)}) collective-permute-start(bf16[2,96,768]{2,1,0:T(8,128)(2,1)S(1)} %get-tuple-element.191), channel_id=1, source_target_pairs={{0,16},{1,17},{2,18},{3,19},{4,20},{5,21},{6,22},{7,23},{8,24},{9,... | collective-permute-start | bytes 884744 | tf_op jit(solution)/shard_map/ppermute | solution.py:100
  41.6 8.3 %collective-permute-start.4 = (bf16[4,24,1536]{2,1,0:T(8,128)(2,1)S(1)}, bf16[4,24,1536]{2,1,0:T(8,128)(2,1)S(1)}, u32[]{:S(2)}, u32[]{:S(2)}) collective-permute-start(bf16[4,24,1536]{2,1,0:T(8,128)(2,1)S(1)} %get-tuple-element.390), channel_id=1, source_target_pairs={{0,4},{1,5},{2,6},{3,7},{4,0},{5,1},{6,2},{7,3},{8,12},{9,13},{10,... | collective-permute-start | bytes 884744 | tf_op jit(solution)/shard_map/ppermute | solution.py:100
  43.1 10.8 %collective-permute-start.5 = (bf16[4,24,1536]{2,1,0:T(8,128)(2,1)S(1)}, bf16[4,24,1536]{2,1,0:T(8,128)(2,1)S(1)}, u32[]{:S(2)}, u32[]{:S(2)}) collective-permute-start(bf16[4,24,1536]{2,1,0:T(8,128)(2,1)S(1)} %get-tuple-element.389), channel_id=1, source_target_pairs={{0,2},{1,3},{2,0},{3,1},{4,6},{5,7},{6,4},{7,5},{8,10},{9,11},{10,... | collective-permute-start | bytes 884744 | tf_op jit(solution)/shard_map/ppermute | solution.py:100
  44.6 22.6 %all-to-all-start.1 = ((bf16[32,64,128]{2,1,0:T(8,128)(2,1)}), bf16[32,64,128]{2,1,0:T(8,128)(2,1)S(1)}, u32[]{:S(2)}, u32[]{:S(2)}) async-start(bf16[32,64,128]{2,1,0:T(8,128)(2,1)} %get-tuple-element.189), calls=%async_computation.1 | async-start | bytes 1048576 | tf_op jit(solution)/shard_map/all_to_all | solution.py:772
  54.0 15.4 %collective-permute-start.7 = (bf16[8,24,1536]{2,1,0:T(8,128)(2,1)S(1)}, bf16[8,24,1536]{2,1,0:T(8,128)(2,1)}, u32[]{:S(2)}, u32[]{:S(2)}) collective-permute-start(bf16[8,24,1536]{2,1,0:T(8,128)(2,1)S(1)} %pad_maximum_fusion.8), channel_id=1, source_target_pairs={{0,2},{1,3},{2,0},{3,1},{4,6},{5,7},{6,4},{7,5},{8,10},{9,11},{10,... | collective-permute-start | bytes 1769480 | tf_op jit(solution)/shard_map/ppermute | solution.py:100
  57.6 12.4 %collective-permute-start.8 = (bf16[8,24,1536]{2,1,0:T(8,128)(2,1)}, bf16[8,24,1536]{2,1,0:T(8,128)(2,1)}, u32[]{:S(2)}, u32[]{:S(2)}) collective-permute-start(bf16[8,24,1536]{2,1,0:T(8,128)(2,1)} %pad_maximum_fusion.9), channel_id=1, source_target_pairs={{0,4},{1,5},{2,6},{3,7},{4,0},{5,1},{6,2},{7,3},{8,12},{9,13},{10,... | collective-permute-start | bytes 1769480 | tf_op jit(solution)/shard_map/ppermute | solution.py:100
  57.7 9.5 %collective-permute-start.9 = (bf16[2,128,768]{2,1,0:T(8,128)(2,1)S(1)}, bf16[2,128,768]{2,1,0:T(8,128)(2,1)S(1)}, u32[]{:S(2)}, u32[]{:S(2)}) collective-permute-start(bf16[2,128,768]{2,1,0:T(8,128)(2,1)S(1)} %pad_maximum_fusion.11), channel_id=1, source_target_pairs={{0,8},{1,9},{2,10},{3,11},{4,12},{5,13},{6,14},{7,15},{8,0},{9,1},... | collective-permute-start | bytes 1179656 | tf_op jit(solution)/shard_map/ppermute | solution.py:100
  71.2 5.3 %collective-permute-start.10 = (bf16[16,24,1536]{2,1,0:T(8,128)(2,1)S(1)}, bf16[16,24,1536]{2,1,0:T(8,128)(2,1)S(1)}, u32[]{:S(2)}, u32[]{:S(2)}) collective-permute-start(bf16[16,24,1536]{2,1,0:T(8,128)(2,1)S(1)} %pad_maximum_fusion.1), channel_id=1, source_target_pairs={{0,1},{1,0},{2,3},{3,2},{4,5},{5,4},{6,7},{7,6},{8,9},{9,8},{10,11... | collective-permute-start | bytes 3538952 | tf_op jit(solution)/shard_map/ppermute | solution.py:100
  72.5 4.0 %collective-permute-start.11 = (bf16[16,24,1536]{2,1,0:T(8,128)(2,1)S(1)}, bf16[16,24,1536]{2,1,0:T(8,128)(2,1)S(1)}, u32[]{:S(2)}, u32[]{:S(2)}) collective-permute-start(bf16[16,24,1536]{2,1,0:T(8,128)(2,1)S(1)} %pad_maximum_fusion.2), channel_id=1, source_target_pairs={{0,1},{1,0},{2,3},{3,2},{4,5},{5,4},{6,7},{7,6},{8,9},{9,8},{10,11... | collective-permute-start | bytes 3538952 | tf_op jit(solution)/shard_map/ppermute | solution.py:100
  74.1 9.5 %collective-permute-start.14 = (bf16[2,96,768]{2,1,0:T(8,128)(2,1)S(1)}, bf16[2,96,768]{2,1,0:T(8,128)(2,1)S(1)}, u32[]{:S(2)}, u32[]{:S(2)}) collective-permute-start(bf16[2,96,768]{2,1,0:T(8,128)(2,1)S(1)} %pad_maximum_fusion.15), channel_id=1, source_target_pairs={{0,8},{1,9},{2,10},{3,11},{4,12},{5,13},{6,14},{7,15},{8,0},{9,1},... | collective-permute-start | bytes 884744 | tf_op jit(solution)/shard_map/ppermute | solution.py:100
  74.8 8.8 %collective-permute-start.15 = (bf16[768,96]{1,0:T(8,128)(2,1)S(1)}, bf16[768,96]{1,0:T(8,128)(2,1)S(1)}, u32[]{:S(2)}, u32[]{:S(2)}) collective-permute-start(bf16[768,96]{1,0:T(8,128)(2,1)S(1)} %bitcast.96), channel_id=1, source_target_pairs={{0,4},{1,5},{2,6},{3,7},{4,0},{5,1},{6,2},{7,3},{8,12},{9,13},{10,... | collective-permute-start | bytes 442376 | tf_op jit(solution)/shard_map/ppermute | solution.py:100
  80.5 7.3 %collective-permute-start.12 = (bf16[1,128,384]{2,1,0:T(8,128)(2,1)S(1)}, bf16[1,128,384]{2,1,0:T(8,128)(2,1)S(1)}, u32[]{:S(2)}, u32[]{:S(2)}) collective-permute-start(bf16[1,128,384]{2,1,0:T(8,128)(2,1)S(1)} %bitcast.92), channel_id=1, source_target_pairs={{0,16},{1,17},{2,18},{3,19},{4,20},{5,21},{6,22},{7,23},{8,24},{9,... | collective-permute-start | bytes 294920 | tf_op jit(solution)/shard_map/ppermute | solution.py:100
  83.0 4.8 %collective-permute-start.13 = (bf16[1,128,384]{2,1,0:T(8,128)(2,1)S(1)}, bf16[1,128,384]{2,1,0:T(8,128)(2,1)S(1)}, u32[]{:S(2)}, u32[]{:S(2)}) collective-permute-start(bf16[1,128,384]{2,1,0:T(8,128)(2,1)S(1)} %bitcast.88), channel_id=1, source_target_pairs={{0,2},{1,3},{2,0},{3,1},{4,6},{5,7},{6,4},{7,5},{8,10},{9,11},{10,... | collective-permute-start | bytes 294920 | tf_op jit(solution)/shard_map/ppermute | solution.py:100
  89.4 24.8 %collective-permute-start.18 = (bf16[4,96,768]{2,1,0:T(8,128)(2,1)}, bf16[4,96,768]{2,1,0:T(8,128)(2,1)}, u32[]{:S(2)}, u32[]{:S(2)}) collective-permute-start(bf16[4,96,768]{2,1,0:T(8,128)(2,1)} %pad_maximum_fusion.10.own), channel_id=1, source_target_pairs={{0,4},{1,5},{2,6},{3,7},{4,0},{5,1},{6,2},{7,3},{8,12},{9,13},{10,... | collective-permute-start | bytes 1769480 | tf_op jit(solution)/shard_map/ppermute | solution.py:100
  91.6 24.9 %collective-permute-start.21 = (bf16[4,128,768]{2,1,0:T(8,128)(2,1)}, bf16[4,128,768]{2,1,0:T(8,128)(2,1)}, u32[]{:S(2)}, u32[]{:S(2)}) collective-permute-start(bf16[4,128,768]{2,1,0:T(8,128)(2,1)} %pad_maximum_fusion.3), channel_id=1, source_target_pairs={{0,2},{1,3},{2,0},{3,1},{4,6},{5,7},{6,4},{7,5},{8,10},{9,11},{10,... | collective-permute-start | bytes 2359304 | tf_op jit(solution)/shard_map/ppermute | solution.py:100
  92.4 21.8 %all-to-all-start.2 = ((f32[32,16,128]{2,1,0:T(8,128)}), f32[32,16,128]{2,1,0:T(8,128)}, u32[]{:S(2)}, u32[]{:S(2)}) async-start(f32[32,16,128]{2,1,0:T(8,128)} %copy-done.55), calls=%async_computation.2 | async-start | bytes 524288 | tf_op jit(solution)/shard_map/all_to_all | solution.py:838
  97.6 14.0 %collective-permute-start.16 = (bf16[2,128,384]{2,1,0:T(8,128)(2,1)S(1)}, bf16[2,128,384]{2,1,0:T(8,128)(2,1)}, u32[]{:S(2)}, u32[]{:S(2)}) collective-permute-start(bf16[2,128,384]{2,1,0:T(8,128)(2,1)S(1)} %pad_maximum_fusion.16), channel_id=1, source_target_pairs={{0,8},{1,9},{2,10},{3,11},{4,12},{5,13},{6,14},{7,15},{8,0},{9,1},... | collective-permute-start | bytes 589832 | tf_op jit(solution)/shard_map/ppermute | solution.py:100
  100.1 14.1 %collective-permute-start.17 = (bf16[2,128,384]{2,1,0:T(8,128)(2,1)S(1)}, bf16[2,128,384]{2,1,0:T(8,128)(2,1)}, u32[]{:S(2)}, u32[]{:S(2)}) collective-permute-start(bf16[2,128,384]{2,1,0:T(8,128)(2,1)S(1)} %pad_maximum_fusion.17), channel_id=1, source_target_pairs={{0,16},{1,17},{2,18},{3,19},{4,20},{5,21},{6,22},{7,23},{8,24},{9,... | collective-permute-start | bytes 589832 | tf_op jit(solution)/shard_map/ppermute | solution.py:100
  117.9 4.1 %collective-permute-start.22 = (bf16[8,128,768]{2,1,0:T(8,128)(2,1)S(1)}, bf16[8,128,768]{2,1,0:T(8,128)(2,1)S(1)}, u32[]{:S(2)}, u32[]{:S(2)}) collective-permute-start(bf16[8,128,768]{2,1,0:T(8,128)(2,1)S(1)} %pad_maximum_fusion), channel_id=1, source_target_pairs={{0,1},{1,0},{2,3},{3,2},{4,5},{5,4},{6,7},{7,6},{8,9},{9,8},{10,11... | collective-permute-start | bytes 4718600 | tf_op jit(solution)/shard_map/ppermute | solution.py:100
  118.0 11.5 %collective-permute-start.19 = (bf16[4,128,384]{2,1,0:T(8,128)(2,1)S(1)}, bf16[4,128,384]{2,1,0:T(8,128)(2,1)S(1)}, u32[]{:S(2)}, u32[]{:S(2)}) collective-permute-start(bf16[4,128,384]{2,1,0:T(8,128)(2,1)S(1)} %pad_maximum_fusion.12), channel_id=1, source_target_pairs={{0,2},{1,3},{2,0},{3,1},{4,6},{5,7},{6,4},{7,5},{8,10},{9,11},{10,... | collective-permute-start | bytes 1179656 | tf_op jit(solution)/shard_map/ppermute | solution.py:100
  119.6 11.2 %collective-permute-start.20 = (bf16[4,128,384]{2,1,0:T(8,128)(2,1)S(1)}, bf16[4,128,384]{2,1,0:T(8,128)(2,1)S(1)}, u32[]{:S(2)}, u32[]{:S(2)}) collective-permute-start(bf16[4,128,384]{2,1,0:T(8,128)(2,1)S(1)} %pad_maximum_fusion.13), channel_id=1, source_target_pairs={{0,8},{1,9},{2,10},{3,11},{4,12},{5,13},{6,14},{7,15},{8,0},{9,1},... | collective-permute-start | bytes 1179656 | tf_op jit(solution)/shard_map/ppermute | solution.py:100
  132.9 2.4 collective-permute-start.23
  133.0 3.4 %collective-permute-start.24 = (bf16[8,128,384]{2,1,0:T(8,128)(2,1)S(1)}, bf16[8,128,384]{2,1,0:T(8,128)(2,1)S(1)}, u32[]{:S(2)}, u32[]{:S(2)}) collective-permute-start(bf16[8,128,384]{2,1,0:T(8,128)(2,1)S(1)} %pad_maximum_fusion.5), channel_id=1, source_target_pairs={{0,1},{1,0},{2,3},{3,2},{4,5},{5,4},{6,7},{7,6},{8,9},{9,8},{10,11... | collective-permute-start | bytes 2359304 | tf_op jit(solution)/shard_map/ppermute | solution.py:100
  136.4 18.9 %collective-permute-start.25 = (bf16[128,1536]{1,0:T(8,128)(2,1)S(1)}, bf16[128,1536]{1,0:T(8,128)(2,1)S(1)}, u32[]{:S(2)}, u32[]{:S(2)}) collective-permute-start(bf16[128,1536]{1,0:T(8,128)(2,1)S(1)} %copy-done.40), channel_id=1, source_target_pairs={{0,1},{1,0},{2,3},{3,2},{4,5},{5,4},{6,7},{7,6},{8,9},{9,8},{10,11... | collective-permute-start | bytes 1179656 | tf_op jit(solution)/shard_map/ppermute | solution.py:100
  136.5 18.7 %collective-permute-start.26 = (bf16[128,1536]{1,0:T(8,128)(2,1)S(1)}, bf16[128,1536]{1,0:T(8,128)(2,1)S(1)}, u32[]{:S(2)}, u32[]{:S(2)}) collective-permute-start(bf16[128,1536]{1,0:T(8,128)(2,1)S(1)} %copy-done.40), channel_id=1, source_target_pairs={{0,2},{1,3},{2,0},{3,1},{4,6},{5,7},{6,4},{7,5},{8,10},{9,11},{10,... | collective-permute-start | bytes 1179656 | tf_op jit(solution)/shard_map/ppermute | solution.py:100
  137.1 18.7 %collective-permute-start.27 = (bf16[128,1536]{1,0:T(8,128)(2,1)S(1)}, bf16[128,1536]{1,0:T(8,128)(2,1)S(1)}, u32[]{:S(2)}, u32[]{:S(2)}) collective-permute-start(bf16[128,1536]{1,0:T(8,128)(2,1)S(1)} %copy-done.40), channel_id=1, source_target_pairs={{0,3},{1,2},{2,1},{3,0},{4,7},{5,6},{6,5},{7,4},{8,11},{9,10},{10,... | collective-permute-start | bytes 1179656 | tf_op jit(solution)/shard_map/ppermute | solution.py:100
  155.8 20.7 %collective-permute-start.32 = (bf16[8,144,768]{2,1,0:T(8,128)(2,1)}, bf16[8,144,768]{2,1,0:T(8,128)(2,1)S(1)}, u32[]{:S(2)}, u32[]{:S(2)}) collective-permute-start(bf16[8,144,768]{2,1,0:T(8,128)(2,1)} %bitcast.114), channel_id=1, source_target_pairs={{0,1},{1,0},{2,3},{3,2},{4,5},{5,4},{6,7},{7,6},{8,9},{9,8},{10,11... | collective-permute-start | bytes 5308424 | tf_op jit(solution)/shard_map/ppermute | solution.py:100
  156.1 4.6 %collective-permute-start.28 = (bf16[8,144,384]{2,1,0:T(8,128)(2,1)S(1)}, bf16[8,144,384]{2,1,0:T(8,128)(2,1)S(1)}, u32[]{:S(2)}, u32[]{:S(2)}) collective-permute-start(bf16[8,144,384]{2,1,0:T(8,128)(2,1)S(1)} %bitcast.112), channel_id=1, source_target_pairs={{0,1},{1,0},{2,3},{3,2},{4,5},{5,4},{6,7},{7,6},{8,9},{9,8},{10,11... | collective-permute-start | bytes 2654216 | tf_op jit(solution)/shard_map/ppermute | solution.py:100
  156.3 5.7 %collective-permute-start.29 = (bf16[8,144,384]{2,1,0:T(8,128)(2,1)S(1)}, bf16[8,144,384]{2,1,0:T(8,128)(2,1)S(1)}, u32[]{:S(2)}, u32[]{:S(2)}) collective-permute-start(bf16[8,144,384]{2,1,0:T(8,128)(2,1)S(1)} %bitcast.111), channel_id=1, source_target_pairs={{0,1},{1,0},{2,3},{3,2},{4,5},{5,4},{6,7},{7,6},{8,9},{9,8},{10,11... | collective-permute-start | bytes 2654216 | tf_op jit(solution)/shard_map/ppermute | solution.py:100
  162.2 14.3 %collective-permute-start.30 = (bf16[4,144,384]{2,1,0:T(8,128)(2,1)S(1)}, bf16[4,144,384]{2,1,0:T(8,128)(2,1)S(1)}, u32[]{:S(2)}, u32[]{:S(2)}) collective-permute-start(bf16[4,144,384]{2,1,0:T(8,128)(2,1)S(1)} %get-tuple-element.239), channel_id=1, source_target_pairs={{0,2},{1,3},{2,0},{3,1},{4,6},{5,7},{6,4},{7,5},{8,10},{9,11},{10,... | collective-permute-start | bytes 1327112 | tf_op jit(solution)/shard_map/ppermute | solution.py:100
  163.1 13.4 %collective-permute-start.31 = (bf16[4,144,384]{2,1,0:T(8,128)(2,1)S(1)}, bf16[4,144,384]{2,1,0:T(8,128)(2,1)S(1)}, u32[]{:S(2)}, u32[]{:S(2)}) collective-permute-start(bf16[4,144,384]{2,1,0:T(8,128)(2,1)S(1)} %get-tuple-element.242), channel_id=1, source_target_pairs={{0,8},{1,9},{2,10},{3,11},{4,12},{5,13},{6,14},{7,15},{8,0},{9,1},... | collective-permute-start | bytes 1327112 | tf_op jit(solution)/shard_map/ppermute | solution.py:100
  177.8 17.4 %collective-permute-start.35 = (bf16[2,144,768]{2,1,0:T(8,128)(2,1)S(1)}, bf16[2,144,768]{2,1,0:T(8,128)(2,1)S(1)}, u32[]{:S(2)}, u32[]{:S(2)}) collective-permute-start(bf16[2,144,768]{2,1,0:T(8,128)(2,1)S(1)} %get-tuple-element.260), channel_id=1, source_target_pairs={{0,2},{1,3},{2,0},{3,1},{4,6},{5,7},{6,4},{7,5},{8,10},{9,11},{10,... | collective-permute-start | bytes 1327112 | tf_op jit(solution)/shard_map/ppermute | solution.py:100
  179.2 15.9 %collective-permute-start.36 = (bf16[2,96,960]{2,1,0:T(8,128)(2,1)S(1)}, bf16[2,96,960]{2,1,0:T(8,128)(2,1)S(1)}, u32[]{:S(2)}, u32[]{:S(2)}) collective-permute-start(bf16[2,96,960]{2,1,0:T(8,128)(2,1)S(1)} %get-tuple-element.261), channel_id=1, source_target_pairs={{0,4},{1,5},{2,6},{3,7},{4,0},{5,1},{6,2},{7,3},{8,12},{9,13},{10,... | collective-permute-start | bytes 1105928 | tf_op jit(solution)/shard_map/ppermute | solution.py:100
  180.8 9.7 %collective-permute-start.33 = (bf16[2,144,384]{2,1,0:T(8,128)(2,1)S(1)}, bf16[2,144,384]{2,1,0:T(8,128)(2,1)S(1)}, u32[]{:S(2)}, u32[]{:S(2)}) collective-permute-start(bf16[2,144,384]{2,1,0:T(8,128)(2,1)S(1)} %get-tuple-element.256), channel_id=1, source_target_pairs={{0,8},{1,9},{2,10},{3,11},{4,12},{5,13},{6,14},{7,15},{8,0},{9,1},... | collective-permute-start | bytes 663560 | tf_op jit(solution)/shard_map/ppermute | solution.py:100
  182.6 16.1 %collective-permute-start.39 = (bf16[2,96,960]{2,1,0:T(8,128)(2,1)S(1)}, bf16[2,96,960]{2,1,0:T(8,128)(2,1)S(1)}, u32[]{:S(2)}, u32[]{:S(2)}) collective-permute-start(bf16[2,96,960]{2,1,0:T(8,128)(2,1)S(1)} %get-tuple-element.273), channel_id=1, source_target_pairs={{0,4},{1,5},{2,6},{3,7},{4,0},{5,1},{6,2},{7,3},{8,12},{9,13},{10,... | collective-permute-start | bytes 1105928 | tf_op jit(solution)/shard_map/ppermute | solution.py:100
  183.3 11.8 %collective-permute-start.34 = (bf16[2,144,384]{2,1,0:T(8,128)(2,1)S(1)}, bf16[2,144,384]{2,1,0:T(8,128)(2,1)S(1)}, u32[]{:S(2)}, u32[]{:S(2)}) collective-permute-start(bf16[2,144,384]{2,1,0:T(8,128)(2,1)S(1)} %get-tuple-element.259), channel_id=1, source_target_pairs={{0,16},{1,17},{2,18},{3,19},{4,20},{5,21},{6,22},{7,23},{8,24},{9,... | collective-permute-start | bytes 663560 | tf_op jit(solution)/shard_map/ppermute | solution.py:100
  190.5 28.9 %collective-permute-start.41 = (bf16[2,144,768]{2,1,0:T(8,128)(2,1)}, bf16[2,144,768]{2,1,0:T(8,128)(2,1)}, u32[]{:S(2)}, u32[]{:S(2)}) collective-permute-start(bf16[2,144,768]{2,1,0:T(8,128)(2,1)} %get-tuple-element.290), channel_id=1, source_target_pairs={{0,2},{1,3},{2,0},{3,1},{4,6},{5,7},{6,4},{7,5},{8,10},{9,11},{10,... | collective-permute-start | bytes 1327112 | tf_op jit(solution)/shard_map/ppermute | solution.py:100
  196.0 5.7 %collective-permute-start.37 = (bf16[1,144,384]{2,1,0:T(8,128)(2,1)S(1)}, bf16[1,144,384]{2,1,0:T(8,128)(2,1)S(1)}, u32[]{:S(2)}, u32[]{:S(2)}) collective-permute-start(bf16[1,144,384]{2,1,0:T(8,128)(2,1)S(1)} %get-tuple-element.269), channel_id=1, source_target_pairs={{0,16},{1,17},{2,18},{3,19},{4,20},{5,21},{6,22},{7,23},{8,24},{9,... | collective-permute-start | bytes 331784 | tf_op jit(solution)/shard_map/ppermute | solution.py:100
  196.1 5.6 %collective-permute-start.38 = (bf16[1,144,384]{2,1,0:T(8,128)(2,1)S(1)}, bf16[1,144,384]{2,1,0:T(8,128)(2,1)S(1)}, u32[]{:S(2)}, u32[]{:S(2)}) collective-permute-start(bf16[1,144,384]{2,1,0:T(8,128)(2,1)S(1)} %get-tuple-element.272), channel_id=1, source_target_pairs={{0,2},{1,3},{2,0},{3,1},{4,6},{5,7},{6,4},{7,5},{8,10},{9,11},{10,... | collective-permute-start | bytes 331784 | tf_op jit(solution)/shard_map/ppermute | solution.py:100
  196.7 29.8 %collective-permute-start.46 = (bf16[480,768]{1,0:T(8,128)(2,1)}, bf16[480,768]{1,0:T(8,128)(2,1)}, u32[]{:S(2)}, u32[]{:S(2)}) collective-permute-start(bf16[480,768]{1,0:T(8,128)(2,1)} %get-tuple-element.301), channel_id=1, source_target_pairs={{0,4},{1,5},{2,6},{3,7},{4,0},{5,1},{6,2},{7,3},{8,12},{9,13},{10,... | collective-permute-start | bytes 2211848 | tf_op jit(solution)/shard_map/ppermute | solution.py:100
  202.6 16.9 %collective-permute-start.40 = (bf16[96,960]{1,0:T(8,128)(2,1)}, bf16[96,960]{1,0:T(8,128)(2,1)}, u32[]{:S(2)}, u32[]{:S(2)}) collective-permute-start(bf16[96,960]{1,0:T(8,128)(2,1)} %get-tuple-element.289), channel_id=1, source_target_pairs={{0,16},{1,17},{2,18},{3,19},{4,20},{5,21},{6,22},{7,23},{8,24},{9,... | collective-permute-start | bytes 552968 | tf_op jit(solution)/shard_map/ppermute | solution.py:100
  204.7 20.1 %collective-permute-start.45 = (bf16[96,960]{1,0:T(8,128)(2,1)}, bf16[96,960]{1,0:T(8,128)(2,1)}, u32[]{:S(2)}, u32[]{:S(2)}) collective-permute-start(bf16[96,960]{1,0:T(8,128)(2,1)} %get-tuple-element.300), channel_id=1, source_target_pairs={{0,24},{1,25},{2,26},{3,27},{4,28},{5,29},{6,30},{7,31},{8,16},{9,... | collective-permute-start | bytes 552968 | tf_op jit(solution)/shard_map/ppermute | solution.py:100
  215.8 27.8 %all-to-all-start.3 = ((bf16[32,36,128]{2,1,0:T(8,128)(2,1)}), bf16[32,36,128]{2,1,0:T(8,128)(2,1)S(1)}, u32[]{:S(2)}, u32[]{:S(2)}) async-start(bf16[32,36,128]{2,1,0:T(8,128)(2,1)} %copy-done.50), calls=%async_computation.3 | async-start | bytes 655360 | tf_op jit(solution)/shard_map/all_to_all | solution.py:1011
  220.9 5.7 %collective-permute-start.42 = (bf16[128,768]{1,0:T(8,128)(2,1)S(1)}, bf16[128,768]{1,0:T(8,128)(2,1)S(1)}, u32[]{:S(2)}, u32[]{:S(2)}) collective-permute-start(bf16[128,768]{1,0:T(8,128)(2,1)S(1)} %get-tuple-element.387), channel_id=1, source_target_pairs={{0,1},{1,0},{2,3},{3,2},{4,5},{5,4},{6,7},{7,6},{8,9},{9,8},{10,11... | collective-permute-start | bytes 589832 | tf_op jit(solution)/shard_map/ppermute | solution.py:100
  221.2 9.6 %collective-permute-start.43 = (bf16[128,768]{1,0:T(8,128)(2,1)S(1)}, bf16[128,768]{1,0:T(8,128)(2,1)S(1)}, u32[]{:S(2)}, u32[]{:S(2)}) collective-permute-start(bf16[128,768]{1,0:T(8,128)(2,1)S(1)} %get-tuple-element.386), channel_id=1, source_target_pairs={{0,2},{1,3},{2,0},{3,1},{4,6},{5,7},{6,4},{7,5},{8,10},{9,11},{10,... | collective-permute-start | bytes 589832 | tf_op jit(solution)/shard_map/ppermute | solution.py:100
  222.9 11.9 %collective-permute-start.44 = (bf16[128,768]{1,0:T(8,128)(2,1)S(1)}, bf16[128,768]{1,0:T(8,128)(2,1)S(1)}, u32[]{:S(2)}, u32[]{:S(2)}) collective-permute-start(bf16[128,768]{1,0:T(8,128)(2,1)S(1)} %get-tuple-element.385), channel_id=1, source_target_pairs={{0,3},{1,2},{2,1},{3,0},{4,7},{5,6},{6,5},{7,4},{8,11},{9,10},{10,... | collective-permute-start | bytes 589832 | tf_op jit(solution)/shard_map/ppermute | solution.py:100
  224.8 25.5 %collective-permute-start.49 = (bf16[2,144,768]{2,1,0:T(8,128)(2,1)}, bf16[2,144,768]{2,1,0:T(8,128)(2,1)S(1)}, u32[]{:S(2)}, u32[]{:S(2)}) collective-permute-start(bf16[2,144,768]{2,1,0:T(8,128)(2,1)} %get-tuple-element.308), channel_id=1, source_target_pairs={{0,8},{1,9},{2,10},{3,11},{4,12},{5,13},{6,14},{7,15},{8,0},{9,1},... | collective-permute-start | bytes 1327112 | tf_op jit(solution)/shard_map/ppermute | solution.py:100
  238.8 11.5 %collective-permute-start.47 = (bf16[4,96,384]{2,1,0:T(8,128)(2,1)}, bf16[4,96,384]{2,1,0:T(8,128)(2,1)}, u32[]{:S(2)}, u32[]{:S(2)}) collective-permute-start(bf16[4,96,384]{2,1,0:T(8,128)(2,1)} %get-tuple-element.306), channel_id=1, source_target_pairs={{0,4},{1,5},{2,6},{3,7},{4,0},{5,1},{6,2},{7,3},{8,12},{9,13},{10,... | collective-permute-start | bytes 884744 | tf_op jit(solution)/shard_map/ppermute | solution.py:100
  240.3 10.2 %collective-permute-start.48 = (bf16[4,96,384]{2,1,0:T(8,128)(2,1)}, bf16[4,96,384]{2,1,0:T(8,128)(2,1)}, u32[]{:S(2)}, u32[]{:S(2)}) collective-permute-start(bf16[4,96,384]{2,1,0:T(8,128)(2,1)} %get-tuple-element.307), channel_id=1, source_target_pairs={{0,8},{1,9},{2,10},{3,11},{4,12},{5,13},{6,14},{7,15},{8,0},{9,1},... | collective-permute-start | bytes 884744 | tf_op jit(solution)/shard_map/ppermute | solution.py:100
  242.7 21.3 %collective-permute-start.52 = (bf16[96,960]{1,0:T(8,128)(2,1)}, bf16[96,960]{1,0:T(8,128)(2,1)S(1)}, u32[]{:S(2)}, u32[]{:S(2)}) collective-permute-start(bf16[96,960]{1,0:T(8,128)(2,1)} %get-tuple-element.319), channel_id=1, source_target_pairs={{0,8},{1,9},{2,10},{3,11},{4,12},{5,13},{6,14},{7,15},{8,0},{9,1},... | collective-permute-start | bytes 552968 | tf_op jit(solution)/shard_map/ppermute | solution.py:100
  247.0 25.8 %all-to-all-start.4 = ((f32[32,8,128]{2,1,0:T(8,128)}), f32[32,8,128]{2,1,0:T(8,128)}, u32[]{:S(2)}, u32[]{:S(2)}) async-start(f32[32,8,128]{2,1,0:T(8,128)} %copy-done.64), calls=%async_computation.4 | async-start | bytes 262144 | tf_op jit(solution)/shard_map/all_to_all | solution.py:1127
  253.1 10.8 %collective-permute-start.50 = (bf16[2,96,384]{2,1,0:T(8,128)(2,1)}, bf16[2,96,384]{2,1,0:T(8,128)(2,1)}, u32[]{:S(2)}, u32[]{:S(2)}) collective-permute-start(bf16[2,96,384]{2,1,0:T(8,128)(2,1)} %get-tuple-element.314), channel_id=1, source_target_pairs={{0,8},{1,9},{2,10},{3,11},{4,12},{5,13},{6,14},{7,15},{8,0},{9,1},... | collective-permute-start | bytes 442376 | tf_op jit(solution)/shard_map/ppermute | solution.py:100
  256.3 7.6 %collective-permute-start.51 = (bf16[2,96,384]{2,1,0:T(8,128)(2,1)}, bf16[2,96,384]{2,1,0:T(8,128)(2,1)}, u32[]{:S(2)}, u32[]{:S(2)}) collective-permute-start(bf16[2,96,384]{2,1,0:T(8,128)(2,1)} %get-tuple-element.317), channel_id=1, source_target_pairs={{0,4},{1,5},{2,6},{3,7},{4,0},{5,1},{6,2},{7,3},{8,12},{9,13},{10,... | collective-permute-start | bytes 442376 | tf_op jit(solution)/shard_map/ppermute | solution.py:100
  261.4 19.1 %collective-permute-start.55 = (bf16[1,144,768]{2,1,0:T(8,128)(2,1)S(1)}, bf16[1,144,768]{2,1,0:T(8,128)(2,1)S(1)}, u32[]{:S(2)}, u32[]{:S(2)}) collective-permute-start(bf16[1,144,768]{2,1,0:T(8,128)(2,1)S(1)} %get-tuple-element.327), channel_id=1, source_target_pairs={{0,16},{1,17},{2,18},{3,19},{4,20},{5,21},{6,22},{7,23},{8,24},{9,... | collective-permute-start | bytes 663560 | tf_op jit(solution)/shard_map/ppermute | solution.py:100
  264.9 13.9 %collective-permute-start.53 = (bf16[1,96,384]{2,1,0:T(8,128)(2,1)S(1)}, bf16[1,96,384]{2,1,0:T(8,128)(2,1)S(1)}, u32[]{:S(2)}, u32[]{:S(2)}) collective-permute-start(bf16[1,96,384]{2,1,0:T(8,128)(2,1)S(1)} %get-tuple-element.323), channel_id=1, source_target_pairs={{0,16},{1,17},{2,18},{3,19},{4,20},{5,21},{6,22},{7,23},{8,24},{9,... | collective-permute-start | bytes 221192 | tf_op jit(solution)/shard_map/ppermute | solution.py:100
  266.7 13.8 %collective-permute-start.54 = (bf16[1,96,384]{2,1,0:T(8,128)(2,1)S(1)}, bf16[1,96,384]{2,1,0:T(8,128)(2,1)S(1)}, u32[]{:S(2)}, u32[]{:S(2)}) collective-permute-start(bf16[1,96,384]{2,1,0:T(8,128)(2,1)S(1)} %get-tuple-element.326), channel_id=1, source_target_pairs={{0,16},{1,17},{2,18},{3,19},{4,20},{5,21},{6,22},{7,23},{8,24},{9,... | collective-permute-start | bytes 221192 | tf_op jit(solution)/shard_map/ppermute | solution.py:100
  271.2 9.2 %collective-permute-start.56 = (bf16[96,384]{1,0:T(8,128)(2,1)S(1)}, bf16[96,384]{1,0:T(8,128)(2,1)S(1)}, u32[]{:S(2)}, u32[]{:S(2)}) collective-permute-start(bf16[96,384]{1,0:T(8,128)(2,1)S(1)} %get-tuple-element.393), channel_id=1, source_target_pairs={{0,1},{1,0},{2,3},{3,2},{4,5},{5,4},{6,7},{7,6},{8,9},{9,8},{10,11... | collective-permute-start | bytes 221192 | tf_op jit(solution)/shard_map/ppermute | solution.py:100
  271.3 9.2 %collective-permute-start.57 = (bf16[96,384]{1,0:T(8,128)(2,1)S(1)}, bf16[96,384]{1,0:T(8,128)(2,1)S(1)}, u32[]{:S(2)}, u32[]{:S(2)}) collective-permute-start(bf16[96,384]{1,0:T(8,128)(2,1)S(1)} %get-tuple-element.392), channel_id=1, source_target_pairs={{0,2},{1,3},{2,0},{3,1},{4,6},{5,7},{6,4},{7,5},{8,10},{9,11},{10,... | collective-permute-start | bytes 221192 | tf_op jit(solution)/shard_map/ppermute | solution.py:100
  278.8 4.5 %collective-permute-start.58 = (bf16[96,384]{1,0:T(8,128)(2,1)S(1)}, bf16[96,384]{1,0:T(8,128)(2,1)S(1)}, u32[]{:S(2)}, u32[]{:S(2)}) collective-permute-start(bf16[96,384]{1,0:T(8,128)(2,1)S(1)} %get-tuple-element.391), channel_id=1, source_target_pairs={{0,3},{1,2},{2,1},{3,0},{4,7},{5,6},{6,5},{7,4},{8,11},{9,10},{10,... | collective-permute-start | bytes 221192 | tf_op jit(solution)/shard_map/ppermute | solution.py:100
  (97 other events, 959.2 us)

commit v2 on v1

--- a/solution.py
+++ b/solution.py
@@ -48,7 +48,7 @@
     )(*args)
 
 
-def sweep(body, steps, ins, outs, scratch=(), limit=40):
+def sweep(body, steps, ins, outs, scratch=(), limit=48):
     return pl.pallas_call(
         body,
         out_shape=[jax.ShapeDtypeStruct(shape, kind) for shape, kind, _, _ in outs],
@@ -212,7 +212,7 @@
     return (lax.broadcasted_iota(jnp.int32, (width, width), 0) == natural).astype(LOW)
 
 
-def terms_body(where, got, weight, bias, shared, out, loads):
+def terms_body(spot_at, where, got, weight, bias, shared, out, loads):
     me, expert = where[0], where[1]
     total, _, _ = got.shape
     piece, wide = weight.shape
@@ -234,8 +234,12 @@
     cols = shared.shape[1] // total
     for at in range(total):
         out[at, :piece, :cols] = shared[:, at * cols : (at + 1) * cols]
-    load = jnp.sum(rows.astype(WIDE), axis=0, keepdims=True)
-    loads[...] = load
+    experts = loads.shape[1]
+    tally = pltpu.roll(jnp.sum(rows.astype(WIDE), axis=0, keepdims=True), LANES - spot_at, 1)
+    valid = jnp.sum(
+        jnp.where(lax.broadcasted_iota(jnp.int32, tally.shape, 1) == experts, tally, 0.0), axis=1, keepdims=True
+    )
+    loads[...] = (tally * experts / (2.0 * valid))[:, :experts]
 
 
 def shift_body(piece, terms, weight, modulation, lines):
@@ -324,8 +328,9 @@
 def backward_body(
     piece, where, tokens, cotangent, modulation, lengths, rows0, rows1, low0, high0, low1, high1,
     joined, totals, attn_in, middle_in, near0, far0, near1, far1,
-    grad_tokens, sent, lines, d_rows, d_cols, d_mod,
+    grad_tokens, lines, *refs,
 ):
+    sents, (sent, d_rows, d_cols, d_mod) = refs[:-4], refs[-4:]
     count, width = tokens.shape
     length = lengths[0]
     mod = modulation[...]
@@ -402,6 +407,8 @@
         to = expert ^ where[1]
         sent[to, :, :cols] = d_cols[:, expert * cols : (expert + 1) * cols]
         sent[to, :, cols:] = d_cols[:, 3 * width + expert * out_cols : 3 * width + (expert + 1) * out_cols]
+    for to, out in enumerate(sents):
+        out[...] = sent[to]
 
 
 def join_rows(lows, highs, rows):
@@ -484,28 +491,39 @@
         ref[block, extra, :count] = jnp.where(spare[:, :count] == expert, line, 0.0).astype(LOW)
 
 
-def grads_body(write, where, *refs):
-    second, d_mlp, d_pre, act = refs[:4], refs[4], refs[5], refs[6]
-    outs, (rows, up_sum, down_sum) = refs[7:-3], refs[-3:]
+def up_grads_body(write, where, *refs):
+    second, d_pre, outs, (rows, up_sum) = refs[:4], refs[4], refs[5:-2], refs[-2:]
     step = pl.program_id(0)
 
     @pl.when(step == 0)
     def _():
         up_sum[...] = jnp.zeros(up_sum.shape, WIDE)
-        down_sum[...] = jnp.zeros(down_sum.shape, WIDE)
 
     join_rows(second[:2], second[2:], rows)
     up_sum[...] += dot_tn(rows[...], d_pre[0])
-    down_sum[...] += dot_tn(act[0], d_mlp[0])
 
     @pl.when(step == pl.num_programs(0) - 1)
     def _():
-        write(where, up_sum, down_sum, outs)
-
-
-def write_whole(where, up_sum, down_sum, outs):
-    outs[0][...] = up_sum[...]
-    outs[1][...] = down_sum[...]
+        write(where, up_sum, outs)
+
+
+def down_grads_body(write, where, d_mlp, act, *refs):
+    outs, down_sum = refs[:-1], refs[-1]
+    step = pl.program_id(0)
+
+    @pl.when(step == 0)
+    def _():
+        down_sum[...] = jnp.zeros(down_sum.shape, WIDE)
+
+    down_sum[...] += dot_tn(act[0], d_mlp[0])
+
+    @pl.when(step == pl.num_programs(0) - 1)
+    def _():
+        write(where, down_sum, outs)
+
+
+def write_whole(where, total, outs):
+    outs[0][...] = total[...]
 
 
 def place_and_twin(where):
@@ -552,10 +570,10 @@
         full[start + size : start + LANES] = blank
 
 
-def write_twins(where, up_sum, down_sum, outs):
-    keep_up, send_up0, send_up1, keep_down, send_down = outs
+def write_up_twins(where, up_sum, outs):
+    keep_up, send_up0, send_up1 = outs
     place, twin = place_and_twin(where)
-    rows, units = keep_up.shape[1], 2 * (down_sum.shape[0] - 2 * LANES) // 2
+    rows, units = keep_up.shape[1], up_sum.shape[1] - 2 * LANES
     size = (keep_up.shape[2] - units) // 2
     mine, other = slice(units, units + size), slice(units + LANES, units + LANES + size)
     for out, first, at_twin, order_ in (
@@ -569,10 +587,17 @@
             for number, cols in enumerate(order_):
                 start = units + number * size
                 out[at, :, start : start + size] = up_sum[here, cols].astype(LOW)
-    half = units // 2
-    for out, at_twin, rows_ in ((keep_down, twin, mine), (send_down, 1 - twin, other)):
+
+
+def write_down_twins(where, down_sum, outs):
+    keep_down, send_down = outs
+    _, twin = place_and_twin(where)
+    half = (down_sum.shape[0] - 2 * LANES) // 2
+    size = keep_down.shape[0] - half
+    start = 2 * half
+    for out, at_twin, first in ((keep_down, twin, start), (send_down, 1 - twin, start + LANES)):
         out[:half] = down_sum[rows_at(at_twin, half)].astype(out.dtype)
-        out[half:] = down_sum[rows_].astype(out.dtype)
+        out[half:] = down_sum[first : first + size].astype(out.dtype)
 
 
 def twin_up_body(keep, got0, got1, *ups):
@@ -743,6 +768,7 @@
     steps = 2 ** len(outer)
     weight_links = [far[1:] + away + far[:1] + across, far[1:] + away + across + far[:1]]
     paired = groups == 8 and experts == 4
+    room = 24 if paired else 48
     away_masks = order(sorted(away))
 
     pair_weight, kept, sent = call(
@@ -764,8 +790,8 @@
             cot_got = swap(cot, away[0])
             attn_got, cond_all = together(attn_got, cond_all)
             terms, loads = call(
-                terms_body,
-                [((total, up_to(up_to(piece, 8) + lines, 8), LANES), LOW), ((1, LANES), WIDE)],
+                functools.partial(terms_body, group_rows),
+                [((total, up_to(up_to(piece, 8) + lines, 8), LANES), LOW), ((1, experts), WIDE)],
                 (where, cond_all, ada_weight, ada_bias[None], shared_up),
                 smem=(0,),
             )
@@ -775,8 +801,6 @@
             cot = grown(cot, cot_got)
         attn_w = grown(attn_w, attn_got)
     cot_links = away + across
-    tallies = loads[0, group_rows : group_rows + experts + 1]
-    expert_load = tallies[:experts] * experts / (2.0 * tallies[experts])
     attn_parts = [attn_w[:, :, : 2 * width], attn_w[:, :, 2 * width :]]
     last_links = [far[:1] + across, across + far[:1]]
     weight_links = [first_links + masks for masks in last_links]
@@ -835,15 +859,15 @@
     for at in range(len(away + across)):
         got = [swap(part, masks[at]) for part, masks in zip(second_low, team_links)]
         if at == 0:
-            item_lines = lax.all_to_all(tie(own_lines, *seconds), AXES, split_axis=0, concat_axis=0, tiled=True)
+            item_lines = lax.all_to_all(own_lines, AXES, split_axis=0, concat_axis=0, tiled=True)
+            got, item_lines = together(got, item_lines)
             if paired:
                 got, up_last, shared_up_other = together(got, up_last, shared_up_other)
                 up_own = jnp.concatenate([up_mine, up_last], axis=0)
                 up_other = swap(up_own, far[0])
         elif at == 1:
-            got, item_lines = together(got, item_lines)
             if paired:
-                got, up_other = together(got, up_other)
+                got, up_other, cot_got = together(got, up_other, cot_got)
                 routed, hidden = 2 * units, 2 * units + 2 * shared_slot
                 (down_cat,) = call(
                     down_join_body, [((hidden, width), LOW)], (where, down_own, down_other), smem=(0,)
@@ -916,6 +940,7 @@
         steps,
         [scalars, *cots, whole(item_lines), whole(down_cat)],
         [rows_out(hidden), rows_out(width)],
+        limit=room,
     )
     second_got, d_act, up_cat = together(second_got, d_act, up_cat)
     second_low = [grown(*pair) for pair in zip(second_low, second_got)]
@@ -931,6 +956,7 @@
         [scalars, *second_in, *cots, whole(item_lines), rows_of(d_act), whole(up_cat), whole(down_cat)],
         [*back, *back, side, side, rows_out(hidden), rows_out(hidden)],
         scratch=[((2 * half, width), LOW)],
+        limit=room,
     )
     parts = [flat(part) for part in parts]
     if paired:
@@ -940,21 +966,25 @@
         both_group = [both] + both_group
     if paired:
         up_lanes = place_units + 2 * shared_units
-        sum_outs = [
-            sum_out((4, group_rows, up_lanes), LOW),
-            sum_out((2, group_rows, up_lanes), LOW),
-            sum_out((2, group_rows, up_lanes), LOW),
-            sum_out((units + shared_units, width), WIDE),
-            sum_out((units + shared_units, width), LOW),
-        ]
+        up_outs = [sum_out((blocks, group_rows, up_lanes), LOW) for blocks in (4, 2, 2)]
+        down_outs = [sum_out((units + shared_units, width), kind) for kind in (WIDE, LOW)]
     else:
-        sum_outs = [sum_out((width, hidden), WIDE), sum_out((hidden, width), WIDE)]
-    grads = sweep(
-        functools.partial(grads_body, write_twins if paired else write_whole),
+        up_outs, down_outs = [sum_out((width, hidden), WIDE)], [sum_out((hidden, width), WIDE)]
+    up_grads = sweep(
+        functools.partial(up_grads_body, write_up_twins if paired else write_whole),
         steps,
-        [scalars, *second_in, rows_of(d_mlp), rows_of(d_pre), rows_of(act)],
-        sum_outs,
-        scratch=[((2 * half, width), LOW), ((width, hidden), WIDE), ((hidden, width), WIDE)],
+        [scalars, *second_in, rows_of(d_pre)],
+        up_outs,
+        scratch=[((2 * half, width), LOW), ((width, hidden), WIDE)],
+        limit=room,
+    )
+    down_grads = sweep(
+        functools.partial(down_grads_body, write_down_twins if paired else write_whole),
+        steps,
+        [scalars, rows_of(d_mlp), rows_of(act)],
+        down_outs,
+        scratch=[((hidden, width), WIDE)],
+        limit=room,
     )
 
     lows, highs, orders = list(parts[:2]), list(parts[2:4]), [masks + core for masks in team_links]
@@ -963,15 +993,18 @@
     out_got = swap(out_high, core[0])
     for at in range(sums_at + 1):
         got = [swap(high, masks[-1 - at]) for high, masks in zip(highs, orders)]
-        if at == 1:
-            got, grads, out_got = together(got, list(grads), out_got)
+        if at == 0:
+            got, up_grads = together(got, list(up_grads))
+        elif at == 1:
+            got, down_grads, out_got = together(got, list(down_grads), out_got)
             if paired:
-                keep_up, send_up0, send_up1, keep_down, send_down = grads
+                keep_up, send_up0, send_up1 = up_grads
+                keep_down, send_down = down_grads
                 twin_up0, twin_up1 = swap(send_up0, far[0]), swap(send_up1, far[0])
-                twin_down = swap(send_down, far[0])
         elif at == 2 and paired:
             out_got = swap(out_send0, across[0])
             got, out_got, twin_up0 = together(got, out_got, twin_up0)
+            twin_down = swap(tie(send_down, twin_up0), far[0])
         elif at == sums_at and paired:
             out_got1 = swap(out_send1, across[0])
             got, twin_up1 = together(got, twin_up1)
@@ -997,30 +1030,32 @@
         folded, up_own = together(folded, up_own)
         up_got = [piece_ if at < 2 else swap(piece_, away_masks[at]) for at, piece_ in enumerate(up_own)]
 
-    grad_tokens, d_cols, d_mod_sent = call(
+    sent_cols = (count, 4 * width // experts)
+    grad_tokens, d_mod_sent, *d_cols = call(
         functools.partial(backward_body, piece),
-        [(tall, WIDE), ((experts, count, 4 * width // experts), LOW), ((total, lines, LANES), LOW)],
+        [(tall, WIDE), ((total, lines, LANES), LOW), *[(sent_cols, LOW)] * experts],
         (
             where, tokens, cotangent, modulation, lengths, *row_places, *weights,
             joined, totals, attn, middle, *folded,
         ),
-        scratch=[(tall, WIDE), ((count, 4 * width), LOW), ((1, 6 * width), WIDE)],
+        scratch=[((experts, *sent_cols), LOW), (tall, WIDE), ((count, 4 * width), LOW), ((1, 6 * width), WIDE)],
         smem=(0, 4),
     )
 
-    d_mod_all = lax.all_to_all(d_mod_sent, AXES, split_axis=0, concat_axis=0, tiled=True)
     if paired:
         d_cols, up_got[2], out_got1 = together(d_cols, up_got[2], out_got1)
         cols_got = [d_cols[at] if not at else swap(d_cols[at], at) for at in range(4)]
         out_low, out_high = call(
             add_join_body, [((2, *block), LOW), ((2, *block), LOW)], (out_low, out_got, out_got1)
         )
-        cols_got, up_got, twin_down = together(cols_got, up_got, twin_down)
         out_got = swap(out_high, away[1])
-        up_got[1] = swap(up_got[1], away_masks[1])
+        cols_got[1], twin_down, up_got[3] = together(cols_got[1], twin_down, up_got[3])
         grad_expert_down, shared_own = call(
             twin_down_body, [((units, width), WIDE), ((shared_units, width), LOW)], (keep_down, twin_down)
         )
+        d_mod_sent = tie(d_mod_sent, shared_own)
+        cols_got, up_got, shared_own = together(cols_got, up_got, shared_own)
+        up_got[1] = swap(up_got[1], away_masks[1])
         sum_links = [away + far, away[:1] + far + away[1:]]
         sum_masks = [[mask // experts for mask in order(masks)] for masks in sum_links]
         term_half = ((4, group_rows, width // 2), LOW)
@@ -1035,11 +1070,10 @@
         for at in range(3):
             got = [swap(high, masks[-1 - at]) for high, masks in zip(term_highs, sum_links)]
             if at == 0:
-                got, out_got = together(got, out_got)
+                got, out_got, up_got = together(got, out_got, up_got)
                 out_low, out_high = added(out_low, out_got)
                 out_got = swap(out_high, away[0])
             elif at == 1:
-                got, up_got = together(got, up_got)
                 grad_expert_up, crossed = call(
                     up_rows_body,
                     [
@@ -1049,6 +1083,7 @@
                     (where, *up_got, shared_own),
                     smem=(0,),
                 )
+                got, crossed = together(got, crossed)
                 crossed = [crossed[mask] if not mask else swap(crossed[mask], mask) for mask in range(4)]
             else:
                 got, out_got, crossed = together(got, out_got, crossed)
@@ -1064,7 +1099,7 @@
     else:
         natural = jnp.arange(experts, dtype=jnp.int32) ^ my_expert
         both_group = lax.all_gather(both, "expert", axis=0)
-        d_cols = jnp.take(d_cols, natural, axis=0)
+        d_cols = jnp.take(jnp.stack(d_cols), natural, axis=0)
         d_cols = lax.all_to_all(d_cols, "expert", split_axis=0, concat_axis=0, tiled=True)
         (attn_terms,) = call(
             attn_grads_body, [((groups, group_rows, 4 * width // experts), LOW)], (both_group, d_cols)
@@ -1092,7 +1127,7 @@
             smem=(0,),
         )
     else:
-        grad_up, grad_down = grads
+        (grad_up,), (grad_down,) = up_grads, down_grads
         replicas = hidden // (slot + shared_slot)
         sums = []
         for taken, size, first in ((grad_up.T, units, 0), (grad_up.T, shared_units, routed), (grad_down, units, 0), (grad_down, shared_units, routed)):
@@ -1117,6 +1152,7 @@
         shared_rows = lax.all_to_all(shared_rows, "expert", split_axis=0, concat_axis=0, tiled=True)
         grad_shared_up = shared_rows.transpose(2, 1, 0, 3).reshape(group_rows, groups * shared_units).astype(WIDE)
 
+    d_mod_all = lax.all_to_all(d_mod_sent, AXES, split_axis=0, concat_axis=0, tiled=True)
     grad_ada_weight, grad_ada_bias, sent = call(
         functools.partial(ada_body, experts),
         [((group_rows, 6 * width // experts), WIDE), ((1, 6 * width), WIDE), ((total, 8, LANES), WIDE)],
@@ -1142,7 +1178,7 @@
         grad_shared_down,
         grad_expert_up[None],
         grad_expert_down[None],
-        expert_load,
+        loads.reshape(experts),
     )
 
 

time: 288 us -> 280 us (0.972)
  Pallas kernels: 73.8 us -> 64.7 us
  waiting for transfers between devices: 90 us -> 99 us
  starting transfers between devices: 82.1 us -> 76.1 us
  local copies, waits for them, and re-layouts: 18.9 us -> 15 us
  other arithmetic: 19.2 us -> 22.2 us
    ppermute x59, waiting for transfers between devices: 90 us -> 99 us  [swap(): return lax.ppermute(values, AXES, [(at, at ^ mask) for at in range(total)])]
    pallas_call x29, Pallas kernels: 40.8 us -> 33.2 us  [call(): pl.pallas_call(body, out_shape=[jax.ShapeDtypeStruct(shape, kind) for sha...]
    ppermute x59, starting transfers between devices: 61.2 us -> 56.2 us  [swap(): return lax.ppermute(values, AXES, [(at, at ^ mask) for at in range(total)])]
    unnamed x195 -> x145, local copies, waits for them, and re-layouts: 14.8 us -> 10.7 us
    pallas_call x3 -> x4, Pallas kernels: 33 us -> 31.4 us  [sweep(): pl.pallas_call(body, out_shape=[jax.ShapeDtypeStruct(shape, kind) for sha...]
  transfers between devices with their start and end apart: 64 -> 64, of which waited for: 28 -> 32; matrix products, arithmetic and copies ran while one was open for 6% -> 7% of each run, Pallas kernels for 24% -> 23%
where the time goes in v2:
time: 280 us; the launch traced here: 279 us
  waiting for transfers between devices  99 us (35%)
  starting transfers between devices  76.1 us (27%)
  Pallas kernels  64.7 us (23%)
  other arithmetic  22.2 us (8%)
  local copies, waits for them, and re-layouts  15 us (5%)
    ppermute x59, waiting for transfers between devices, swap(): return lax.ppermute(values, AXES, [(at, at ^ mask) for at in range(total)])  99 us
    ppermute x59, starting transfers between devices, swap(): return lax.ppermute(values, AXES, [(at, at ^ mask) for at in range(total)])  56.2 us
    pallas_call x29, Pallas kernels, call(): pl.pallas_call(body, out_shape=[jax.ShapeDtypeStruct(shape, kind) for sha...  33.2 us
    pallas_call x4, Pallas kernels, sweep(): pl.pallas_call(body, out_shape=[jax.ShapeDtypeStruct(shape, kind) for sha...  31.4 us
    concatenate x15, other arithmetic, grown(): return jnp.concatenate([values, got], axis=0)  15.9 us
    unnamed x145, local copies, waits for them, and re-layouts  10.7 us
    all_to_all x2, starting transfers between devices, shards(): lax.all_to_all(sent, AXES, split_axis=0, concat_axis=0, tiled=True)  10.4 us
  transfers between devices with their start and end apart: 64, of which 32 were waited for; matrix products, arithmetic and copies ran while one was open for 7% of the time, Pallas kernels for 23%

profile of v2, /device:TPU:0, one launch (start us, length us, event | category | flops | bytes accessed | tf_op | source)
XLA Modules:
  0.0 279.1 jit_solution(16459601569803766785)
XLA Ops:
  4.2 7.3 %all-to-all-start = ((bf16[32,16,128]{2,1,0:T(8,128)(2,1)}), bf16[32,16,128]{2,1,0:T(8,128)(2,1)S(1)}, u32[]{:S(2)}, u32[]{:S(2)}) async-start(bf16[32,16,128]{2,1,0:T(8,128)(2,1)} %get-tuple-element.198), calls=%async_computation | async-start | bytes 262144 | tf_op jit(solution)/shard_map/all_to_all | solution.py:780
  12.5 2.7 collective-permute-start
  15.2 1.2 pad_maximum_fusion.6.own
  16.4 1.5 collective-permute-start.2
  18.0 6.4 %collective-permute-done = bf16[1,24,3072]{2,1,0:T(8,128)(2,1)S(1)} collective-permute-done((bf16[1,24,3072]{2,1,0:T(8,128)(2,1)S(1)}, bf16[1,24,3072]{2,1,0:T(8,128)(2,1)S(1)}, u32[]{:S(2)}, u32[]{:S(2)}) %collective-permute-start) | collective-permute-done | bytes 147488 | tf_op jit(solution)/shard_map/ppermute | solution.py:100
  25.2 2.3 collective-permute-start.3
  29.5 2.6 shard_map.256
  32.1 4.9 %collective-permute-done.3 = bf16[1,128,768]{2,1,0:T(8,128)(2,1)} collective-permute-done((bf16[1,128,768]{2,1,0:T(8,128)(2,1)S(1)}, bf16[1,128,768]{2,1,0:T(8,128)(2,1)}, u32[]{:S(2)}, u32[]{:S(2)}) %collective-permute-start.3) | collective-permute-done | bytes 196640 | tf_op jit(solution)/shard_map/ppermute | solution.py:100
  37.0 3.1 %collective-permute-done.1 = bf16[2,24,3072]{2,1,0:T(8,128)(2,1)} collective-permute-done((bf16[2,24,3072]{2,1,0:T(8,128)(2,1)}, bf16[2,24,3072]{2,1,0:T(8,128)(2,1)}, u32[]{:S(2)}, u32[]{:S(2)}) %collective-permute-start.1) | collective-permute-done | bytes 294944 | tf_op jit(solution)/shard_map/ppermute | solution.py:100
  40.1 1.4 pad_maximum_fusion.7
  41.6 1.5 collective-permute-start.4
  43.1 1.5 collective-permute-start.5
  44.6 2.6 all-to-all-start.1
  47.2 2.4 collective-permute-done.6
  49.9 4.1 %collective-permute-done.5 = bf16[4,24,1536]{2,1,0:T(8,128)(2,1)S(1)} collective-permute-done((bf16[4,24,1536]{2,1,0:T(8,128)(2,1)S(1)}, bf16[4,24,1536]{2,1,0:T(8,128)(2,1)S(1)}, u32[]{:S(2)}, u32[]{:S(2)}) %collective-permute-start.5) | collective-permute-done | bytes 294944 | tf_op jit(solution)/shard_map/ppermute | solution.py:100
  54.0 2.8 collective-permute-start.7
  58.7 8.8 %collective-permute-done.9 = bf16[2,128,768]{2,1,0:T(8,128)(2,1)S(1)} collective-permute-done((bf16[2,128,768]{2,1,0:T(8,128)(2,1)S(1)}, bf16[2,128,768]{2,1,0:T(8,128)(2,1)S(1)}, u32[]{:S(2)}, u32[]{:S(2)}) %collective-permute-start.9) | collective-permute-done | bytes 393248 | tf_op jit(solution)/shard_map/ppermute | solution.py:100
  70.0 1.2 pad_maximum_fusion.1
  71.3 1.2 pad_maximum_fusion.2
  75.1 3.5 %all-to-all-start.2 = ((f32[32,16,128]{2,1,0:T(8,128)}), f32[32,16,128]{2,1,0:T(8,128)}, u32[]{:S(2)}, u32[]{:S(2)}) async-start(f32[32,16,128]{2,1,0:T(8,128)} %copy-done.35), calls=%async_computation.2 | async-start | bytes 524288 | tf_op jit(solution)/shard_map/all_to_all | solution.py:862
  78.7 1.7 fusion.4
  80.4 1.7 pad_maximum_fusion.15
  82.0 1.4 collective-permute-start.14
  83.4 1.6 slice.40
  85.1 1.5 collective-permute-start.15
  87.3 5.3 %shard_map.259 = (bf16[128,1536]{1,0:T(8,128)(2,1)S(1)}, bf16[128,2304]{1,0:T(8,128)(2,1)S(1)}, f32[128,128]{1,0:T(8,128)S(1)}, f32[128,768]{1,0:T(8,128)S(1)}, ...) custom-call(s32[3]{0:T(128)S(1)} %pad_add_fusion.where, ...), custom_call_target="tpu_custom_call" | custom-call | tf_op jit(solution)/shard_map/pallas_call | solution.py:41
  93.4 2.6 collective-permute-start.12
  95.9 1.5 collective-permute-start.13
  97.4 1.9 pad_maximum_fusion.3
  105.1 2.8 collective-permute-start.17
  107.9 10.3 %collective-permute-done.19 = bf16[4,128,768]{2,1,0:T(8,128)(2,1)} collective-permute-done((bf16[4,128,768]{2,1,0:T(8,128)(2,1)}, bf16[4,128,768]{2,1,0:T(8,128)(2,1)}, u32[]{:S(2)}, u32[]{:S(2)}) %collective-permute-start.19) | collective-permute-done | bytes 786464 | tf_op jit(solution)/shard_map/ppermute | solution.py:100
  120.2 1.4 pad_maximum_fusion
  124.0 1.3 shard_map.262.refs_8_
  125.3 5.1 %shard_map.261 = (bf16[4,512,1024]{2,1,0:T(8,128)(2,1)S(1)}, bf16[4,512,768]{2,1,0:T(8,128)(2,1)S(1)}) custom-call(s32[3]{0:T(128)S(1)} %pad_add_fusion.where, bf16[2,2,2,128,768]{4,3,2,1,0:T(8,128)(2,1)S(1)} %bitcast.51, bf16[2,2,2,128,768]{4,3,2,1,0:T(8,128)(2,1)S(1)} %bitcast.61, f32[32,16,128]{2,1,0:T(8,128)} %all-to-all-done.2.lines.refs_6_, ...), custom_call_target="tpu_custom_call" | custom-call | tf_op jit(solution)/shard_map/pallas_call | solution.py:52
  130.5 2.8 %collective-permute-done.20 = bf16[4,128,384]{2,1,0:T(8,128)(2,1)S(1)} collective-permute-done((bf16[4,128,384]{2,1,0:T(8,128)(2,1)S(1)}, bf16[4,128,384]{2,1,0:T(8,128)(2,1)S(1)}, u32[]{:S(2)}, u32[]{:S(2)}) %collective-permute-start.20) | collective-permute-done | bytes 393248 | tf_op jit(solution)/shard_map/ppermute | solution.py:100
  136.7 1.8 collective-permute-done.23
  141.5 15.5 %shard_map.263 = (bf16[2,2,2,144,384]{4,3,2,1,0:T(8,128)(2,1)S(1)}, bf16[2,2,2,144,384]{4,3,2,1,0:T(8,128)(2,1)S(1)}, bf16[2,2,2,144,384]{4,3,2,1,0:T(8,128)(2,1...) custom-call(s32[3]{0:T(128)S(1)} %pad_add_fusion.where, ...), custom_call_target="tpu_custom_call" | custom-call | tf_op jit(solution)/shard_map/pallas_call | solution.py:52
  157.0 2.0 collective-permute-done.27.both3
  159.9 5.5 %shard_map.264 = (bf16[4,96,960]{2,1,0:T(8,128)(2,1)S(1)}, bf16[2,96,960]{2,1,0:T(8,128)(2,1)S(1)}, bf16[2,96,960]{2,1,0:T(8,128)(2,1)S(1)}) custom-call(s32[3]{0:T(128)S(1)} %pad_add_fusion.where, bf16[2,2,2,128,384]{4,3,2,1,0:T(8,128)(2,1)S(1)} %bitcast.58, bf16[2,2,2,128,384]{4,3,2,1,0:T(8,128)(2,1)S(1)} %bitcast.60, ...), custom_call_target="tpu_custom_call" | custom-call | tf_op jit(solution)/shard_map/pallas_call | solution.py:52
  167.6 5.3 %shard_map.267 = (f32[480,768]{1,0:T(8,128)S(1)}, bf16[480,768]{1,0:T(8,128)(2,1)S(1)}) custom-call(s32[3]{0:T(128)S(1)} %pad_add_fusion.where, bf16[4,512,768]{2,1,0:T(8,128)(2,1)S(1)} %get-tuple-element.259.d_mlp, bf16[4,512,1024]{2,1,0:T(8,128)(2,1)S(1)} %get-tuple-element.260.act), custom_call_target="tpu_custom_call" | custom-call | tf_op jit(solution)/shard_map/pallas_call | solution.py:52
  172.9 5.1 %collective-permute-done.30.got = bf16[4,144,384]{2,1,0:T(8,128)(2,1)S(1)} collective-permute-done((bf16[4,144,384]{2,1,0:T(8,128)(2,1)S(1)}, bf16[4,144,384]{2,1,0:T(8,128)(2,1)S(1)}, u32[]{:S(2)}, u32[]{:S(2)}) %collective-permute-start.30) | collective-permute-done | bytes 442400 | tf_op jit(solution)/shard_map/ppermute | solution.py:100
  183.8 8.7 %collective-permute-done.36.got0 = bf16[2,96,960]{2,1,0:T(8,128)(2,1)S(1)} collective-permute-done((bf16[2,96,960]{2,1,0:T(8,128)(2,1)S(1)}, bf16[2,96,960]{2,1,0:T(8,128)(2,1)S(1)}, u32[]{:S(2)}, u32[]{:S(2)}) %collective-permute-start.36) | collective-permute-done | bytes 368672 | tf_op jit(solution)/shard_map/ppermute | solution.py:100
  193.0 1.5 collective-permute-start.43
  196.9 4.1 %collective-permute-done.39.got1 = bf16[2,96,960]{2,1,0:T(8,128)(2,1)S(1)} collective-permute-done((bf16[2,96,960]{2,1,0:T(8,128)(2,1)S(1)}, bf16[2,96,960]{2,1,0:T(8,128)(2,1)S(1)}, u32[]{:S(2)}, u32[]{:S(2)}) %collective-permute-start.39) | collective-permute-done | bytes 368672 | tf_op jit(solution)/shard_map/ppermute | solution.py:100
  201.4 2.7 collective-permute-done.38
  205.7 1.8 collective-permute-start.40
  207.5 1.6 collective-permute-start.44
  209.2 8.7 %shard_map.274 = (f32[128,768]{1,0:T(8,128)}, bf16[32,36,128]{2,1,0:T(8,128)(2,1)S(1)}, bf16[128,768]{1,0:T(8,128)(2,1)S(1)}, bf16[128,768]{1,0:T(8,128)(2,1)S(1...) custom-call(s32[3]{0:T(128)S(1)} %pad_add_fusion.where, bf16[128,768]{1,0:T(8,128)(2,1)S(1)} %copy-done.15, ...), custom_call_target="tpu_custom_call" | custom-call | tf_op jit(solution)/shard_map/pallas_call | solution.py:41
  223.0 3.4 %all-to-all-start.3 = ((bf16[32,36,128]{2,1,0:T(8,128)(2,1)}), bf16[32,36,128]{2,1,0:T(8,128)(2,1)S(1)}, u32[]{:S(2)}, u32[]{:S(2)}) async-start(bf16[32,36,128]{2,1,0:T(8,128)(2,1)} %copy-done.32), calls=%async_computation.3 | async-start | bytes 655360 | tf_op jit(solution)/shard_map/all_to_all | solution.py:1155
  226.6 3.4 %collective-permute-done.46.cols3 = bf16[128,768]{1,0:T(8,128)(2,1)S(1)} collective-permute-done((bf16[128,768]{1,0:T(8,128)(2,1)}, bf16[128,768]{1,0:T(8,128)(2,1)S(1)}, u32[]{:S(2)}, u32[]{:S(2)}) %collective-permute-start.46) | collective-permute-done | bytes 196640 | tf_op jit(solution)/shard_map/ppermute | solution.py:100
  231.9 2.6 shard_map.277
  235.3 2.0 collective-permute-start.50
  237.5 12.4 %collective-permute-done.50.up1 = bf16[96,960]{1,0:T(8,128)(2,1)S(1)} collective-permute-done((bf16[96,960]{1,0:T(8,128)(2,1)S(1)}, bf16[96,960]{1,0:T(8,128)(2,1)S(1)}, u32[]{:S(2)}, u32[]{:S(2)}) %collective-permute-start.50) | collective-permute-done | bytes 184352 | tf_op jit(solution)/shard_map/ppermute | solution.py:100
  251.2 2.2 collective-permute-start.55
  253.4 1.8 shard_map.281
  255.2 2.0 collective-permute-done.51.got
  258.1 2.2 collective-permute-start.54
  260.4 2.1 shard_map.285
  262.5 3.1 %all-to-all-start.4 = ((f32[32,8,128]{2,1,0:T(8,128)}), f32[32,8,128]{2,1,0:T(8,128)S(1)}, u32[]{:S(2)}, u32[]{:S(2)}) async-start(f32[32,8,128]{2,1,0:T(8,128)} %get-tuple-element.364), calls=%async_computation.4 | async-start | bytes 262144 | tf_op jit(solution)/shard_map/all_to_all | solution.py:1163
  266.0 1.7 collective-permute-start.57
  267.7 1.7 collective-permute-done.53
  269.4 1.6 collective-permute-done.54
  271.0 2.9 %collective-permute-done.58.got3 = bf16[96,384]{1,0:T(8,128)(2,1)S(1)} collective-permute-done((bf16[96,384]{1,0:T(8,128)(2,1)S(1)}, bf16[96,384]{1,0:T(8,128)(2,1)S(1)}, u32[]{:S(2)}, u32[]{:S(2)}) %collective-permute-start.58) | collective-permute-done | bytes 73760 | tf_op jit(solution)/shard_map/ppermute | solution.py:100
  273.8 1.4 shard_map.287
  (272 shorter events, 60.1 us)
Async XLA Ops:
  4.2 20.2 %all-to-all-start = ((bf16[32,16,128]{2,1,0:T(8,128)(2,1)}), bf16[32,16,128]{2,1,0:T(8,128)(2,1)S(1)}, u32[]{:S(2)}, u32[]{:S(2)}) async-start(bf16[32,16,128]{2,1,0:T(8,128)(2,1)} %get-tuple-element.198), calls=%async_computation | async-start | bytes 262144 | tf_op jit(solution)/shard_map/all_to_all | solution.py:780
  12.5 11.9 %collective-permute-start = (bf16[1,24,3072]{2,1,0:T(8,128)(2,1)S(1)}, bf16[1,24,3072]{2,1,0:T(8,128)(2,1)S(1)}, u32[]{:S(2)}, u32[]{:S(2)}) collective-permute-start(bf16[1,24,3072]{2,1,0:T(8,128)(2,1)S(1)} %maximum_bitcast_fusion), channel_id=1, source_target_pairs={{0,16},{1,17},{2,18},{3,19},{4,20},{5,21},{6,22},{7,23},{8,24},{9,... | collective-permute-start | bytes 442376 | tf_op jit(solution)/shard_map/ppermute | solution.py:100
  16.4 23.7 %collective-permute-start.2 = (bf16[480,768]{1,0:T(8,128)(2,1)S(1)}, bf16[480,768]{1,0:T(8,128)(2,1)S(1)}, u32[]{:S(2)}, u32[]{:S(2)}) collective-permute-start(bf16[480,768]{1,0:T(8,128)(2,1)S(1)} %pad_maximum_fusion.6.own), channel_id=1, source_target_pairs={{0,4},{1,5},{2,6},{3,7},{4,0},{5,1},{6,2},{7,3},{8,12},{9,13},{10,... | collective-permute-start | bytes 2211848 | tf_op jit(solution)/shard_map/ppermute | solution.py:100
  25.2 14.9 %collective-permute-start.1 = (bf16[2,24,3072]{2,1,0:T(8,128)(2,1)}, bf16[2,24,3072]{2,1,0:T(8,128)(2,1)}, u32[]{:S(2)}, u32[]{:S(2)}) collective-permute-start(bf16[2,24,3072]{2,1,0:T(8,128)(2,1)} %pad_maximum_fusion.14), channel_id=1, source_target_pairs={{0,8},{1,9},{2,10},{3,11},{4,12},{5,13},{6,14},{7,15},{8,0},{9,1},... | collective-permute-start | bytes 884744 | tf_op jit(solution)/shard_map/ppermute | solution.py:100
  25.2 11.9 %collective-permute-start.3 = (bf16[1,128,768]{2,1,0:T(8,128)(2,1)S(1)}, bf16[1,128,768]{2,1,0:T(8,128)(2,1)}, u32[]{:S(2)}, u32[]{:S(2)}) collective-permute-start(bf16[1,128,768]{2,1,0:T(8,128)(2,1)S(1)} %bitcast.65), channel_id=1, source_target_pairs={{0,16},{1,17},{2,18},{3,19},{4,20},{5,21},{6,22},{7,23},{8,24},{9,... | collective-permute-start | bytes 589832 | tf_op jit(solution)/shard_map/ppermute | solution.py:100
  28.9 20.7 %collective-permute-start.6 = (bf16[2,96,768]{2,1,0:T(8,128)(2,1)S(1)}, bf16[2,96,768]{2,1,0:T(8,128)(2,1)}, u32[]{:S(2)}, u32[]{:S(2)}) collective-permute-start(bf16[2,96,768]{2,1,0:T(8,128)(2,1)S(1)} %get-tuple-element.203), channel_id=1, source_target_pairs={{0,16},{1,17},{2,18},{3,19},{4,20},{5,21},{6,22},{7,23},{8,24},{9,... | collective-permute-start | bytes 884744 | tf_op jit(solution)/shard_map/ppermute | solution.py:100
  41.6 8.3 %collective-permute-start.4 = (bf16[4,24,1536]{2,1,0:T(8,128)(2,1)S(1)}, bf16[4,24,1536]{2,1,0:T(8,128)(2,1)S(1)}, u32[]{:S(2)}, u32[]{:S(2)}) collective-permute-start(bf16[4,24,1536]{2,1,0:T(8,128)(2,1)S(1)} %get-tuple-element.410), channel_id=1, source_target_pairs={{0,4},{1,5},{2,6},{3,7},{4,0},{5,1},{6,2},{7,3},{8,12},{9,13},{10,... | collective-permute-start | bytes 884744 | tf_op jit(solution)/shard_map/ppermute | solution.py:100
  43.1 10.8 %collective-permute-start.5 = (bf16[4,24,1536]{2,1,0:T(8,128)(2,1)S(1)}, bf16[4,24,1536]{2,1,0:T(8,128)(2,1)S(1)}, u32[]{:S(2)}, u32[]{:S(2)}) collective-permute-start(bf16[4,24,1536]{2,1,0:T(8,128)(2,1)S(1)} %get-tuple-element.409), channel_id=1, source_target_pairs={{0,2},{1,3},{2,0},{3,1},{4,6},{5,7},{6,4},{7,5},{8,10},{9,11},{10,... | collective-permute-start | bytes 884744 | tf_op jit(solution)/shard_map/ppermute | solution.py:100
  44.6 22.9 %all-to-all-start.1 = ((bf16[32,64,128]{2,1,0:T(8,128)(2,1)}), bf16[32,64,128]{2,1,0:T(8,128)(2,1)S(1)}, u32[]{:S(2)}, u32[]{:S(2)}) async-start(bf16[32,64,128]{2,1,0:T(8,128)(2,1)} %get-tuple-element.201), calls=%async_computation.1 | async-start | bytes 1048576 | tf_op jit(solution)/shard_map/all_to_all | solution.py:798
  54.0 15.4 %collective-permute-start.7 = (bf16[8,24,1536]{2,1,0:T(8,128)(2,1)S(1)}, bf16[8,24,1536]{2,1,0:T(8,128)(2,1)}, u32[]{:S(2)}, u32[]{:S(2)}) collective-permute-start(bf16[8,24,1536]{2,1,0:T(8,128)(2,1)S(1)} %pad_maximum_fusion.8), channel_id=1, source_target_pairs={{0,2},{1,3},{2,0},{3,1},{4,6},{5,7},{6,4},{7,5},{8,10},{9,11},{10,... | collective-permute-start | bytes 1769480 | tf_op jit(solution)/shard_map/ppermute | solution.py:100
  57.6 12.4 %collective-permute-start.8 = (bf16[8,24,1536]{2,1,0:T(8,128)(2,1)}, bf16[8,24,1536]{2,1,0:T(8,128)(2,1)}, u32[]{:S(2)}, u32[]{:S(2)}) collective-permute-start(bf16[8,24,1536]{2,1,0:T(8,128)(2,1)} %pad_maximum_fusion.9), channel_id=1, source_target_pairs={{0,4},{1,5},{2,6},{3,7},{4,0},{5,1},{6,2},{7,3},{8,12},{9,13},{10,... | collective-permute-start | bytes 1769480 | tf_op jit(solution)/shard_map/ppermute | solution.py:100
  58.6 8.9 %collective-permute-start.9 = (bf16[2,128,768]{2,1,0:T(8,128)(2,1)S(1)}, bf16[2,128,768]{2,1,0:T(8,128)(2,1)S(1)}, u32[]{:S(2)}, u32[]{:S(2)}) collective-permute-start(bf16[2,128,768]{2,1,0:T(8,128)(2,1)S(1)} %pad_maximum_fusion.11), channel_id=1, source_target_pairs={{0,8},{1,9},{2,10},{3,11},{4,12},{5,13},{6,14},{7,15},{8,0},{9,1},... | collective-permute-start | bytes 1179656 | tf_op jit(solution)/shard_map/ppermute | solution.py:100
  71.2 15.4 %collective-permute-start.10 = (bf16[16,24,1536]{2,1,0:T(8,128)(2,1)S(1)}, bf16[16,24,1536]{2,1,0:T(8,128)(2,1)S(1)}, u32[]{:S(2)}, u32[]{:S(2)}) collective-permute-start(bf16[16,24,1536]{2,1,0:T(8,128)(2,1)S(1)} %pad_maximum_fusion.1), channel_id=1, source_target_pairs={{0,1},{1,0},{2,3},{3,2},{4,5},{5,4},{6,7},{7,6},{8,9},{9,8},{10,11... | collective-permute-start | bytes 3538952 | tf_op jit(solution)/shard_map/ppermute | solution.py:100
  72.5 14.1 %collective-permute-start.11 = (bf16[16,24,1536]{2,1,0:T(8,128)(2,1)S(1)}, bf16[16,24,1536]{2,1,0:T(8,128)(2,1)}, u32[]{:S(2)}, u32[]{:S(2)}) collective-permute-start(bf16[16,24,1536]{2,1,0:T(8,128)(2,1)S(1)} %pad_maximum_fusion.2), channel_id=1, source_target_pairs={{0,1},{1,0},{2,3},{3,2},{4,5},{5,4},{6,7},{7,6},{8,9},{9,8},{10,11... | collective-permute-start | bytes 3538952 | tf_op jit(solution)/shard_map/ppermute | solution.py:100
  75.1 24.8 %all-to-all-start.2 = ((f32[32,16,128]{2,1,0:T(8,128)}), f32[32,16,128]{2,1,0:T(8,128)}, u32[]{:S(2)}, u32[]{:S(2)}) async-start(f32[32,16,128]{2,1,0:T(8,128)} %copy-done.35), calls=%async_computation.2 | async-start | bytes 524288 | tf_op jit(solution)/shard_map/all_to_all | solution.py:862
  82.0 19.0 %collective-permute-start.14 = (bf16[2,96,768]{2,1,0:T(8,128)(2,1)}, bf16[2,96,768]{2,1,0:T(8,128)(2,1)}, u32[]{:S(2)}, u32[]{:S(2)}) collective-permute-start(bf16[2,96,768]{2,1,0:T(8,128)(2,1)} %pad_maximum_fusion.15), channel_id=1, source_target_pairs={{0,8},{1,9},{2,10},{3,11},{4,12},{5,13},{6,14},{7,15},{8,0},{9,1},... | collective-permute-start | bytes 884744 | tf_op jit(solution)/shard_map/ppermute | solution.py:100
  85.1 15.9 %collective-permute-start.15 = (bf16[768,96]{1,0:T(8,128)(2,1)}, bf16[768,96]{1,0:T(8,128)(2,1)}, u32[]{:S(2)}, u32[]{:S(2)}) collective-permute-start(bf16[768,96]{1,0:T(8,128)(2,1)} %bitcast.15.shared), channel_id=1, source_target_pairs={{0,4},{1,5},{2,6},{3,7},{4,0},{5,1},{6,2},{7,3},{8,12},{9,13},{10,... | collective-permute-start | bytes 442376 | tf_op jit(solution)/shard_map/ppermute | solution.py:100
  93.4 7.6 %collective-permute-start.12 = (bf16[1,128,384]{2,1,0:T(8,128)(2,1)}, bf16[1,128,384]{2,1,0:T(8,128)(2,1)}, u32[]{:S(2)}, u32[]{:S(2)}) collective-permute-start(bf16[1,128,384]{2,1,0:T(8,128)(2,1)} %bitcast.13), channel_id=1, source_target_pairs={{0,16},{1,17},{2,18},{3,19},{4,20},{5,21},{6,22},{7,23},{8,24},{9,... | collective-permute-start | bytes 294920 | tf_op jit(solution)/shard_map/ppermute | solution.py:100
  95.9 5.1 %collective-permute-start.13 = (bf16[1,128,384]{2,1,0:T(8,128)(2,1)}, bf16[1,128,384]{2,1,0:T(8,128)(2,1)}, u32[]{:S(2)}, u32[]{:S(2)}) collective-permute-start(bf16[1,128,384]{2,1,0:T(8,128)(2,1)} %bitcast.14), channel_id=1, source_target_pairs={{0,2},{1,3},{2,0},{3,1},{4,6},{5,7},{6,4},{7,5},{8,10},{9,11},{10,... | collective-permute-start | bytes 294920 | tf_op jit(solution)/shard_map/ppermute | solution.py:100
  99.3 18.8 %collective-permute-start.19 = (bf16[4,128,768]{2,1,0:T(8,128)(2,1)}, bf16[4,128,768]{2,1,0:T(8,128)(2,1)}, u32[]{:S(2)}, u32[]{:S(2)}) collective-permute-start(bf16[4,128,768]{2,1,0:T(8,128)(2,1)} %pad_maximum_fusion.3), channel_id=1, source_target_pairs={{0,2},{1,3},{2,0},{3,1},{4,6},{5,7},{6,4},{7,5},{8,10},{9,11},{10,... | collective-permute-start | bytes 2359304 | tf_op jit(solution)/shard_map/ppermute | solution.py:100
  102.1 16.0 %collective-permute-start.18 = (bf16[4,96,768]{2,1,0:T(8,128)(2,1)S(1)}, bf16[4,96,768]{2,1,0:T(8,128)(2,1)S(1)}, u32[]{:S(2)}, u32[]{:S(2)}) collective-permute-start(bf16[4,96,768]{2,1,0:T(8,128)(2,1)S(1)} %pad_maximum_fusion.10.own), channel_id=1, source_target_pairs={{0,4},{1,5},{2,6},{3,7},{4,0},{5,1},{6,2},{7,3},{8,12},{9,13},{10,... | collective-permute-start | bytes 1769480 | tf_op jit(solution)/shard_map/ppermute | solution.py:100
  103.6 14.6 %collective-permute-start.16 = (bf16[2,128,384]{2,1,0:T(8,128)(2,1)S(1)}, bf16[2,128,384]{2,1,0:T(8,128)(2,1)S(1)}, u32[]{:S(2)}, u32[]{:S(2)}) collective-permute-start(bf16[2,128,384]{2,1,0:T(8,128)(2,1)S(1)} %pad_maximum_fusion.16), channel_id=1, source_target_pairs={{0,8},{1,9},{2,10},{3,11},{4,12},{5,13},{6,14},{7,15},{8,0},{9,1},... | collective-permute-start | bytes 589832 | tf_op jit(solution)/shard_map/ppermute | solution.py:100
  105.1 13.1 %collective-permute-start.17 = (bf16[2,128,384]{2,1,0:T(8,128)(2,1)S(1)}, bf16[2,128,384]{2,1,0:T(8,128)(2,1)S(1)}, u32[]{:S(2)}, u32[]{:S(2)}) collective-permute-start(bf16[2,128,384]{2,1,0:T(8,128)(2,1)S(1)} %pad_maximum_fusion.17), channel_id=1, source_target_pairs={{0,16},{1,17},{2,18},{3,19},{4,20},{5,21},{6,22},{7,23},{8,24},{9,... | collective-permute-start | bytes 589832 | tf_op jit(solution)/shard_map/ppermute | solution.py:100
  121.6 3.7 %collective-permute-start.22 = (bf16[8,128,768]{2,1,0:T(8,128)(2,1)S(1)}, bf16[8,128,768]{2,1,0:T(8,128)(2,1)S(1)}, u32[]{:S(2)}, u32[]{:S(2)}) collective-permute-start(bf16[8,128,768]{2,1,0:T(8,128)(2,1)S(1)} %pad_maximum_fusion), channel_id=1, source_target_pairs={{0,1},{1,0},{2,3},{3,2},{4,5},{5,4},{6,7},{7,6},{8,9},{9,8},{10,11... | collective-permute-start | bytes 4718600 | tf_op jit(solution)/shard_map/ppermute | solution.py:100
  121.7 11.5 %collective-permute-start.20 = (bf16[4,128,384]{2,1,0:T(8,128)(2,1)S(1)}, bf16[4,128,384]{2,1,0:T(8,128)(2,1)S(1)}, u32[]{:S(2)}, u32[]{:S(2)}) collective-permute-start(bf16[4,128,384]{2,1,0:T(8,128)(2,1)S(1)} %pad_maximum_fusion.12), channel_id=1, source_target_pairs={{0,2},{1,3},{2,0},{3,1},{4,6},{5,7},{6,4},{7,5},{8,10},{9,11},{10,... | collective-permute-start | bytes 1179656 | tf_op jit(solution)/shard_map/ppermute | solution.py:100
  122.8 11.2 %collective-permute-start.21 = (bf16[4,128,384]{2,1,0:T(8,128)(2,1)S(1)}, bf16[4,128,384]{2,1,0:T(8,128)(2,1)S(1)}, u32[]{:S(2)}, u32[]{:S(2)}) collective-permute-start(bf16[4,128,384]{2,1,0:T(8,128)(2,1)S(1)} %pad_maximum_fusion.13), channel_id=1, source_target_pairs={{0,8},{1,9},{2,10},{3,11},{4,12},{5,13},{6,14},{7,15},{8,0},{9,1},... | collective-permute-start | bytes 1179656 | tf_op jit(solution)/shard_map/ppermute | solution.py:100
  136.1 2.4 collective-permute-start.23
  136.2 3.4 %collective-permute-start.24 = (bf16[8,128,384]{2,1,0:T(8,128)(2,1)S(1)}, bf16[8,128,384]{2,1,0:T(8,128)(2,1)S(1)}, u32[]{:S(2)}, u32[]{:S(2)}) collective-permute-start(bf16[8,128,384]{2,1,0:T(8,128)(2,1)S(1)} %pad_maximum_fusion.5), channel_id=1, source_target_pairs={{0,1},{1,0},{2,3},{3,2},{4,5},{5,4},{6,7},{7,6},{8,9},{9,8},{10,11... | collective-permute-start | bytes 2359304 | tf_op jit(solution)/shard_map/ppermute | solution.py:100
  139.6 17.4 %collective-permute-start.25 = (bf16[128,1536]{1,0:T(8,128)(2,1)S(1)}, bf16[128,1536]{1,0:T(8,128)(2,1)S(1)}, u32[]{:S(2)}, u32[]{:S(2)}) collective-permute-start(bf16[128,1536]{1,0:T(8,128)(2,1)S(1)} %copy-done.22), channel_id=1, source_target_pairs={{0,1},{1,0},{2,3},{3,2},{4,5},{5,4},{6,7},{7,6},{8,9},{9,8},{10,11... | collective-permute-start | bytes 1179656 | tf_op jit(solution)/shard_map/ppermute | solution.py:100
  139.8 17.2 %collective-permute-start.26 = (bf16[128,1536]{1,0:T(8,128)(2,1)S(1)}, bf16[128,1536]{1,0:T(8,128)(2,1)S(1)}, u32[]{:S(2)}, u32[]{:S(2)}) collective-permute-start(bf16[128,1536]{1,0:T(8,128)(2,1)S(1)} %copy-done.22), channel_id=1, source_target_pairs={{0,2},{1,3},{2,0},{3,1},{4,6},{5,7},{6,4},{7,5},{8,10},{9,11},{10,... | collective-permute-start | bytes 1179656 | tf_op jit(solution)/shard_map/ppermute | solution.py:100
  140.8 18.2 %collective-permute-start.27 = (bf16[128,1536]{1,0:T(8,128)(2,1)S(1)}, bf16[128,1536]{1,0:T(8,128)(2,1)S(1)}, u32[]{:S(2)}, u32[]{:S(2)}) collective-permute-start(bf16[128,1536]{1,0:T(8,128)(2,1)S(1)} %copy-done.22), channel_id=1, source_target_pairs={{0,3},{1,2},{2,1},{3,0},{4,7},{5,6},{6,5},{7,4},{8,11},{9,10},{10,... | collective-permute-start | bytes 1179656 | tf_op jit(solution)/shard_map/ppermute | solution.py:100
  159.0 20.0 %collective-permute-start.32 = (bf16[8,144,768]{2,1,0:T(8,128)(2,1)S(1)}, bf16[8,144,768]{2,1,0:T(8,128)(2,1)S(1)}, u32[]{:S(2)}, u32[]{:S(2)}) collective-permute-start(bf16[8,144,768]{2,1,0:T(8,128)(2,1)S(1)} %bitcast.89), channel_id=1, source_target_pairs={{0,1},{1,0},{2,3},{3,2},{4,5},{5,4},{6,7},{7,6},{8,9},{9,8},{10,11... | collective-permute-start | bytes 5308424 | tf_op jit(solution)/shard_map/ppermute | solution.py:100
  159.4 6.1 %collective-permute-start.28 = (bf16[8,144,384]{2,1,0:T(8,128)(2,1)S(1)}, bf16[8,144,384]{2,1,0:T(8,128)(2,1)S(1)}, u32[]{:S(2)}, u32[]{:S(2)}) collective-permute-start(bf16[8,144,384]{2,1,0:T(8,128)(2,1)S(1)} %bitcast.91), channel_id=1, source_target_pairs={{0,1},{1,0},{2,3},{3,2},{4,5},{5,4},{6,7},{7,6},{8,9},{9,8},{10,11... | collective-permute-start | bytes 2654216 | tf_op jit(solution)/shard_map/ppermute | solution.py:100
  159.5 6.0 %collective-permute-start.29 = (bf16[8,144,384]{2,1,0:T(8,128)(2,1)S(1)}, bf16[8,144,384]{2,1,0:T(8,128)(2,1)S(1)}, u32[]{:S(2)}, u32[]{:S(2)}) collective-permute-start(bf16[8,144,384]{2,1,0:T(8,128)(2,1)S(1)} %bitcast.90), channel_id=1, source_target_pairs={{0,1},{1,0},{2,3},{3,2},{4,5},{5,4},{6,7},{7,6},{8,9},{9,8},{10,11... | collective-permute-start | bytes 2654216 | tf_op jit(solution)/shard_map/ppermute | solution.py:100
  165.7 12.3 %collective-permute-start.30 = (bf16[4,144,384]{2,1,0:T(8,128)(2,1)S(1)}, bf16[4,144,384]{2,1,0:T(8,128)(2,1)S(1)}, u32[]{:S(2)}, u32[]{:S(2)}) collective-permute-start(bf16[4,144,384]{2,1,0:T(8,128)(2,1)S(1)} %get-tuple-element.255), channel_id=1, source_target_pairs={{0,2},{1,3},{2,0},{3,1},{4,6},{5,7},{6,4},{7,5},{8,10},{9,11},{10,... | collective-permute-start | bytes 1327112 | tf_op jit(solution)/shard_map/ppermute | solution.py:100
  167.0 12.0 %collective-permute-start.31 = (bf16[4,144,384]{2,1,0:T(8,128)(2,1)S(1)}, bf16[4,144,384]{2,1,0:T(8,128)(2,1)S(1)}, u32[]{:S(2)}, u32[]{:S(2)}) collective-permute-start(bf16[4,144,384]{2,1,0:T(8,128)(2,1)S(1)} %get-tuple-element.258), channel_id=1, source_target_pairs={{0,8},{1,9},{2,10},{3,11},{4,12},{5,13},{6,14},{7,15},{8,0},{9,1},... | collective-permute-start | bytes 1327112 | tf_op jit(solution)/shard_map/ppermute | solution.py:100
  179.4 13.6 %collective-permute-start.35 = (bf16[2,144,768]{2,1,0:T(8,128)(2,1)S(1)}, bf16[2,144,768]{2,1,0:T(8,128)(2,1)S(1)}, u32[]{:S(2)}, u32[]{:S(2)}) collective-permute-start(bf16[2,144,768]{2,1,0:T(8,128)(2,1)S(1)} %get-tuple-element.272), channel_id=1, source_target_pairs={{0,2},{1,3},{2,0},{3,1},{4,6},{5,7},{6,4},{7,5},{8,10},{9,11},{10,... | collective-permute-start | bytes 1327112 | tf_op jit(solution)/shard_map/ppermute | solution.py:100
  180.5 12.1 %collective-permute-start.36 = (bf16[2,96,960]{2,1,0:T(8,128)(2,1)S(1)}, bf16[2,96,960]{2,1,0:T(8,128)(2,1)S(1)}, u32[]{:S(2)}, u32[]{:S(2)}) collective-permute-start(bf16[2,96,960]{2,1,0:T(8,128)(2,1)S(1)} %get-tuple-element.273), channel_id=1, source_target_pairs={{0,4},{1,5},{2,6},{3,7},{4,0},{5,1},{6,2},{7,3},{8,12},{9,13},{10,... | collective-permute-start | bytes 1105928 | tf_op jit(solution)/shard_map/ppermute | solution.py:100
  181.1 11.4 %collective-permute-start.33 = (bf16[2,144,384]{2,1,0:T(8,128)(2,1)S(1)}, bf16[2,144,384]{2,1,0:T(8,128)(2,1)S(1)}, u32[]{:S(2)}, u32[]{:S(2)}) collective-permute-start(bf16[2,144,384]{2,1,0:T(8,128)(2,1)S(1)} %get-tuple-element.268), channel_id=1, source_target_pairs={{0,8},{1,9},{2,10},{3,11},{4,12},{5,13},{6,14},{7,15},{8,0},{9,1},... | collective-permute-start | bytes 663560 | tf_op jit(solution)/shard_map/ppermute | solution.py:100
  181.9 11.2 %collective-permute-start.34 = (bf16[2,144,384]{2,1,0:T(8,128)(2,1)S(1)}, bf16[2,144,384]{2,1,0:T(8,128)(2,1)S(1)}, u32[]{:S(2)}, u32[]{:S(2)}) collective-permute-start(bf16[2,144,384]{2,1,0:T(8,128)(2,1)S(1)} %get-tuple-element.271), channel_id=1, source_target_pairs={{0,16},{1,17},{2,18},{3,19},{4,20},{5,21},{6,22},{7,23},{8,24},{9,... | collective-permute-start | bytes 663560 | tf_op jit(solution)/shard_map/ppermute | solution.py:100
  182.9 18.0 %collective-permute-start.39 = (bf16[2,96,960]{2,1,0:T(8,128)(2,1)S(1)}, bf16[2,96,960]{2,1,0:T(8,128)(2,1)S(1)}, u32[]{:S(2)}, u32[]{:S(2)}) collective-permute-start(bf16[2,96,960]{2,1,0:T(8,128)(2,1)S(1)} %get-tuple-element.285), channel_id=1, source_target_pairs={{0,4},{1,5},{2,6},{3,7},{4,0},{5,1},{6,2},{7,3},{8,12},{9,13},{10,... | collective-permute-start | bytes 1105928 | tf_op jit(solution)/shard_map/ppermute | solution.py:100
  193.0 28.8 %collective-permute-start.43 = (bf16[480,768]{1,0:T(8,128)(2,1)S(1)}, bf16[480,768]{1,0:T(8,128)(2,1)S(1)}, u32[]{:S(2)}, u32[]{:S(2)}) collective-permute-start(bf16[480,768]{1,0:T(8,128)(2,1)S(1)} %get-tuple-element.314), channel_id=1, source_target_pairs={{0,4},{1,5},{2,6},{3,7},{4,0},{5,1},{6,2},{7,3},{8,12},{9,13},{10,... | collective-permute-start | bytes 2211848 | tf_op jit(solution)/shard_map/ppermute | solution.py:100
  194.5 23.3 %collective-permute-start.41 = (bf16[2,144,768]{2,1,0:T(8,128)(2,1)S(1)}, bf16[2,144,768]{2,1,0:T(8,128)(2,1)S(1)}, u32[]{:S(2)}, u32[]{:S(2)}) collective-permute-start(bf16[2,144,768]{2,1,0:T(8,128)(2,1)S(1)} %get-tuple-element.305), channel_id=1, source_target_pairs={{0,2},{1,3},{2,0},{3,1},{4,6},{5,7},{6,4},{7,5},{8,10},{9,11},{10,... | collective-permute-start | bytes 1327112 | tf_op jit(solution)/shard_map/ppermute | solution.py:100
  195.6 5.8 %collective-permute-start.37 = (bf16[1,144,384]{2,1,0:T(8,128)(2,1)S(1)}, bf16[1,144,384]{2,1,0:T(8,128)(2,1)S(1)}, u32[]{:S(2)}, u32[]{:S(2)}) collective-permute-start(bf16[1,144,384]{2,1,0:T(8,128)(2,1)S(1)} %get-tuple-element.281), channel_id=1, source_target_pairs={{0,16},{1,17},{2,18},{3,19},{4,20},{5,21},{6,22},{7,23},{8,24},{9,... | collective-permute-start | bytes 331784 | tf_op jit(solution)/shard_map/ppermute | solution.py:100
  195.8 8.3 %collective-permute-start.38 = (bf16[1,144,384]{2,1,0:T(8,128)(2,1)S(1)}, bf16[1,144,384]{2,1,0:T(8,128)(2,1)S(1)}, u32[]{:S(2)}, u32[]{:S(2)}) collective-permute-start(bf16[1,144,384]{2,1,0:T(8,128)(2,1)S(1)} %get-tuple-element.284), channel_id=1, source_target_pairs={{0,2},{1,3},{2,0},{3,1},{4,6},{5,7},{6,4},{7,5},{8,10},{9,11},{10,... | collective-permute-start | bytes 331784 | tf_op jit(solution)/shard_map/ppermute | solution.py:100
  205.7 13.0 %collective-permute-start.40 = (bf16[96,960]{1,0:T(8,128)(2,1)S(1)}, bf16[96,960]{1,0:T(8,128)(2,1)S(1)}, u32[]{:S(2)}, u32[]{:S(2)}) collective-permute-start(bf16[96,960]{1,0:T(8,128)(2,1)S(1)} %get-tuple-element.304), channel_id=1, source_target_pairs={{0,16},{1,17},{2,18},{3,19},{4,20},{5,21},{6,22},{7,23},{8,24},{9,... | collective-permute-start | bytes 552968 | tf_op jit(solution)/shard_map/ppermute | solution.py:100
  207.5 13.9 %collective-permute-start.44 = (bf16[96,960]{1,0:T(8,128)(2,1)S(1)}, bf16[96,960]{1,0:T(8,128)(2,1)S(1)}, u32[]{:S(2)}, u32[]{:S(2)}) collective-permute-start(bf16[96,960]{1,0:T(8,128)(2,1)S(1)} %get-tuple-element.315), channel_id=1, source_target_pairs={{0,24},{1,25},{2,26},{3,27},{4,28},{5,29},{6,30},{7,31},{8,16},{9,... | collective-permute-start | bytes 552968 | tf_op jit(solution)/shard_map/ppermute | solution.py:100
  218.7 3.1 %collective-permute-start.42 = (bf16[128,768]{1,0:T(8,128)(2,1)S(1)}, bf16[128,768]{1,0:T(8,128)(2,1)S(1)}, u32[]{:S(2)}, u32[]{:S(2)}) collective-permute-start(bf16[128,768]{1,0:T(8,128)(2,1)S(1)} %get-tuple-element.312), channel_id=1, source_target_pairs={{0,1},{1,0},{2,3},{3,2},{4,5},{5,4},{6,7},{7,6},{8,9},{9,8},{10,11... | collective-permute-start | bytes 589832 | tf_op jit(solution)/shard_map/ppermute | solution.py:100
  218.7 7.9 %collective-permute-start.45 = (bf16[128,768]{1,0:T(8,128)(2,1)}, bf16[128,768]{1,0:T(8,128)(2,1)S(1)}, u32[]{:S(2)}, u32[]{:S(2)}) collective-permute-start(bf16[128,768]{1,0:T(8,128)(2,1)} %get-tuple-element.317), channel_id=1, source_target_pairs={{0,2},{1,3},{2,0},{3,1},{4,6},{5,7},{6,4},{7,5},{8,10},{9,11},{10,... | collective-permute-start | bytes 589832 | tf_op jit(solution)/shard_map/ppermute | solution.py:100
  219.7 10.4 %collective-permute-start.46 = (bf16[128,768]{1,0:T(8,128)(2,1)}, bf16[128,768]{1,0:T(8,128)(2,1)S(1)}, u32[]{:S(2)}, u32[]{:S(2)}) collective-permute-start(bf16[128,768]{1,0:T(8,128)(2,1)} %get-tuple-element.318), channel_id=1, source_target_pairs={{0,3},{1,2},{2,1},{3,0},{4,7},{5,6},{6,5},{7,4},{8,11},{9,10},{10,... | collective-permute-start | bytes 589832 | tf_op jit(solution)/shard_map/ppermute | solution.py:100
  221.4 16.0 %collective-permute-start.49 = (bf16[2,144,768]{2,1,0:T(8,128)(2,1)}, bf16[2,144,768]{2,1,0:T(8,128)(2,1)S(1)}, u32[]{:S(2)}, u32[]{:S(2)}) collective-permute-start(bf16[2,144,768]{2,1,0:T(8,128)(2,1)} %get-tuple-element.332), channel_id=1, source_target_pairs={{0,8},{1,9},{2,10},{3,11},{4,12},{5,13},{6,14},{7,15},{8,0},{9,1},... | collective-permute-start | bytes 1327112 | tf_op jit(solution)/shard_map/ppermute | solution.py:100
  223.0 37.4 %all-to-all-start.3 = ((bf16[32,36,128]{2,1,0:T(8,128)(2,1)}), bf16[32,36,128]{2,1,0:T(8,128)(2,1)S(1)}, u32[]{:S(2)}, u32[]{:S(2)}) async-start(bf16[32,36,128]{2,1,0:T(8,128)(2,1)} %copy-done.32), calls=%async_computation.3 | async-start | bytes 655360 | tf_op jit(solution)/shard_map/all_to_all | solution.py:1155
  234.6 15.2 %collective-permute-start.47 = (bf16[4,96,384]{2,1,0:T(8,128)(2,1)S(1)}, bf16[4,96,384]{2,1,0:T(8,128)(2,1)S(1)}, u32[]{:S(2)}, u32[]{:S(2)}) collective-permute-start(bf16[4,96,384]{2,1,0:T(8,128)(2,1)S(1)} %get-tuple-element.330), channel_id=1, source_target_pairs={{0,4},{1,5},{2,6},{3,7},{4,0},{5,1},{6,2},{7,3},{8,12},{9,13},{10,... | collective-permute-start | bytes 884744 | tf_op jit(solution)/shard_map/ppermute | solution.py:100
  235.3 14.6 %collective-permute-start.48 = (bf16[4,96,384]{2,1,0:T(8,128)(2,1)S(1)}, bf16[4,96,384]{2,1,0:T(8,128)(2,1)S(1)}, u32[]{:S(2)}, u32[]{:S(2)}) collective-permute-start(bf16[4,96,384]{2,1,0:T(8,128)(2,1)S(1)} %get-tuple-element.331), channel_id=1, source_target_pairs={{0,8},{1,9},{2,10},{3,11},{4,12},{5,13},{6,14},{7,15},{8,0},{9,1},... | collective-permute-start | bytes 884744 | tf_op jit(solution)/shard_map/ppermute | solution.py:100
  235.3 14.5 %collective-permute-start.50 = (bf16[96,960]{1,0:T(8,128)(2,1)S(1)}, bf16[96,960]{1,0:T(8,128)(2,1)S(1)}, u32[]{:S(2)}, u32[]{:S(2)}) collective-permute-start(bf16[96,960]{1,0:T(8,128)(2,1)S(1)} %copy-done.61), channel_id=1, source_target_pairs={{0,8},{1,9},{2,10},{3,11},{4,12},{5,13},{6,14},{7,15},{8,0},{9,1},... | collective-permute-start | bytes 552968 | tf_op jit(solution)/shard_map/ppermute | solution.py:100
  250.0 7.2 %collective-permute-start.51 = (bf16[2,96,384]{2,1,0:T(8,128)(2,1)S(1)}, bf16[2,96,384]{2,1,0:T(8,128)(2,1)S(1)}, u32[]{:S(2)}, u32[]{:S(2)}) collective-permute-start(bf16[2,96,384]{2,1,0:T(8,128)(2,1)S(1)} %get-tuple-element.342), channel_id=1, source_target_pairs={{0,8},{1,9},{2,10},{3,11},{4,12},{5,13},{6,14},{7,15},{8,0},{9,1},... | collective-permute-start | bytes 442376 | tf_op jit(solution)/shard_map/ppermute | solution.py:100
  250.4 6.8 %collective-permute-start.52 = (bf16[2,96,384]{2,1,0:T(8,128)(2,1)S(1)}, bf16[2,96,384]{2,1,0:T(8,128)(2,1)S(1)}, u32[]{:S(2)}, u32[]{:S(2)}) collective-permute-start(bf16[2,96,384]{2,1,0:T(8,128)(2,1)S(1)} %get-tuple-element.345), channel_id=1, source_target_pairs={{0,4},{1,5},{2,6},{3,7},{4,0},{5,1},{6,2},{7,3},{8,12},{9,13},{10,... | collective-permute-start | bytes 442376 | tf_op jit(solution)/shard_map/ppermute | solution.py:100
  251.2 19.8 %collective-permute-start.55 = (bf16[1,144,768]{2,1,0:T(8,128)(2,1)S(1)}, bf16[1,144,768]{2,1,0:T(8,128)(2,1)S(1)}, u32[]{:S(2)}, u32[]{:S(2)}) collective-permute-start(bf16[1,144,768]{2,1,0:T(8,128)(2,1)S(1)} %get-tuple-element.357), channel_id=1, source_target_pairs={{0,16},{1,17},{2,18},{3,19},{4,20},{5,21},{6,22},{7,23},{8,24},{9,... | collective-permute-start | bytes 663560 | tf_op jit(solution)/shard_map/ppermute | solution.py:100
  257.3 12.1 %collective-permute-start.53 = (bf16[1,96,384]{2,1,0:T(8,128)(2,1)S(1)}, bf16[1,96,384]{2,1,0:T(8,128)(2,1)S(1)}, u32[]{:S(2)}, u32[]{:S(2)}) collective-permute-start(bf16[1,96,384]{2,1,0:T(8,128)(2,1)S(1)} %get-tuple-element.353), channel_id=1, source_target_pairs={{0,16},{1,17},{2,18},{3,19},{4,20},{5,21},{6,22},{7,23},{8,24},{9,... | collective-permute-start | bytes 221192 | tf_op jit(solution)/shard_map/ppermute | solution.py:100
  258.1 12.8 %collective-permute-start.54 = (bf16[1,96,384]{2,1,0:T(8,128)(2,1)S(1)}, bf16[1,96,384]{2,1,0:T(8,128)(2,1)S(1)}, u32[]{:S(2)}, u32[]{:S(2)}) collective-permute-start(bf16[1,96,384]{2,1,0:T(8,128)(2,1)S(1)} %get-tuple-element.356), channel_id=1, source_target_pairs={{0,16},{1,17},{2,18},{3,19},{4,20},{5,21},{6,22},{7,23},{8,24},{9,... | collective-permute-start | bytes 221192 | tf_op jit(solution)/shard_map/ppermute | solution.py:100
  262.5 15.9 %all-to-all-start.4 = ((f32[32,8,128]{2,1,0:T(8,128)}), f32[32,8,128]{2,1,0:T(8,128)S(1)}, u32[]{:S(2)}, u32[]{:S(2)}) async-start(f32[32,8,128]{2,1,0:T(8,128)} %get-tuple-element.364), calls=%async_computation.4 | async-start | bytes 262144 | tf_op jit(solution)/shard_map/all_to_all | solution.py:1163
  265.7 5.3 %collective-permute-start.56 = (bf16[96,384]{1,0:T(8,128)(2,1)S(1)}, bf16[96,384]{1,0:T(8,128)(2,1)S(1)}, u32[]{:S(2)}, u32[]{:S(2)}) collective-permute-start(bf16[96,384]{1,0:T(8,128)(2,1)S(1)} %get-tuple-element.413), channel_id=1, source_target_pairs={{0,1},{1,0},{2,3},{3,2},{4,5},{5,4},{6,7},{7,6},{8,9},{9,8},{10,11... | collective-permute-start | bytes 221192 | tf_op jit(solution)/shard_map/ppermute | solution.py:100
  266.0 4.9 %collective-permute-start.57 = (bf16[96,384]{1,0:T(8,128)(2,1)S(1)}, bf16[96,384]{1,0:T(8,128)(2,1)S(1)}, u32[]{:S(2)}, u32[]{:S(2)}) collective-permute-start(bf16[96,384]{1,0:T(8,128)(2,1)S(1)} %get-tuple-element.412), channel_id=1, source_target_pairs={{0,2},{1,3},{2,0},{3,1},{4,6},{5,7},{6,4},{7,5},{8,10},{9,11},{10,... | collective-permute-start | bytes 221192 | tf_op jit(solution)/shard_map/ppermute | solution.py:100
  269.4 4.5 %collective-permute-start.58 = (bf16[96,384]{1,0:T(8,128)(2,1)S(1)}, bf16[96,384]{1,0:T(8,128)(2,1)S(1)}, u32[]{:S(2)}, u32[]{:S(2)}) collective-permute-start(bf16[96,384]{1,0:T(8,128)(2,1)S(1)} %get-tuple-element.411), channel_id=1, source_target_pairs={{0,3},{1,2},{2,1},{3,0},{4,7},{5,6},{6,5},{7,4},{8,11},{9,10},{10,... | collective-permute-start | bytes 221192 | tf_op jit(solution)/shard_map/ppermute | solution.py:100
  (72 other events, 758.1 us)

commit v3 on v2

--- a/solution.py
+++ b/solution.py
@@ -15,7 +15,7 @@
 WIDE = jnp.float32
 LANES = 128
 EXTRA = 16
-LIMIT = 24
+LIMIT = 16
 CURVE = 0.7978845608028654
 CUBIC = 0.044715
 
@@ -234,6 +234,7 @@
     cols = shared.shape[1] // total
     for at in range(total):
         out[at, :piece, :cols] = shared[:, at * cols : (at + 1) * cols]
+        out[at, :piece, cols:] = jnp.zeros((piece, LANES - cols), LOW)
     experts = loads.shape[1]
     tally = pltpu.roll(jnp.sum(rows.astype(WIDE), axis=0, keepdims=True), LANES - spot_at, 1)
     valid = jnp.sum(
@@ -242,12 +243,14 @@
     loads[...] = (tally * experts / (2.0 * valid))[:, :experts]
 
 
-def shift_body(piece, terms, weight, modulation, lines):
+def shift_body(piece, terms, weight, modulation, lines, shared):
     total = modulation.shape[1] // LANES
     first = up_to(piece, 8)
     sums = jnp.sum(terms[:, first : first + total, :].astype(WIDE), axis=0)
     for at in range(total):
         modulation[:, at * LANES : (at + 1) * LANES] = sums[at : at + 1]
+    for at in range(terms.shape[0]):
+        shared[at * piece : (at + 1) * piece] = terms[at, :piece]
     gate = total // 6
     lines[:, :8] = jnp.zeros((lines.shape[0], 8, LANES), WIDE)
     lines[:, :gate] = jnp.broadcast_to(sums[5 * gate :], (lines.shape[0], gate, LANES))
@@ -550,12 +553,8 @@
     for at, mask in enumerate((0, 2, 1, 3)):
         full[rows_at(2 * (place ^ mask) + twin, rows), :cols] = own[at]
         full[rows_at(2 * (place ^ mask) + 1 - twin, rows), :cols] = other[at]
-    size = shared.shape[1]
-    blank = jnp.zeros((full.shape[0], LANES - size), LOW)
     for at, piece in enumerate((shared, shared_other)):
-        start = cols + at * LANES
-        full[:, start : start + size] = piece[...]
-        full[:, start + size : start + LANES] = blank
+        full[:, cols + at * LANES : cols + (at + 1) * LANES] = piece[...]
 
 
 def down_join_body(where, own, other, full):
@@ -683,7 +682,7 @@
     total, lines, _ = got.shape
     for at in range(lines):
         d_mod[:, at * LANES : (at + 1) * LANES] = got[:, at, :]
-    grad_bias[...] = jnp.sum(d_mod[...].astype(WIDE), axis=0, keepdims=True)
+    grad_bias[...] = jnp.sum(d_mod[...].astype(WIDE), axis=0)
     cols = grad_weight.shape[1]
     mine = d_mod[:, pl.ds(pl.multiple_of(expert * cols, LANES), cols)]
     grad_weight[...] = dot_tn(cond[:, 0, :], mine)[: grad_weight.shape[0]]
@@ -768,7 +767,7 @@
     steps = 2 ** len(outer)
     weight_links = [far[1:] + away + far[:1] + across, far[1:] + away + across + far[:1]]
     paired = groups == 8 and experts == 4
-    room = 24 if paired else 48
+    room = 20 if paired else 48
     away_masks = order(sorted(away))
 
     pair_weight, kept, sent = call(
@@ -784,10 +783,12 @@
     down_own = jnp.concatenate([expert_down[0], shared_down], axis=0)
     down_other = swap(down_own, far[0])
     first_links = far[1:] + away
+    cot_got = swap(cot, away[0])
+    attn_w, cot_got = together(attn_w, cot_got)
+    cot = grown(cot, cot_got)
     for at, mask in enumerate(first_links):
         attn_got = swap(attn_w, mask)
         if at == 0:
-            cot_got = swap(cot, away[0])
             attn_got, cond_all = together(attn_got, cond_all)
             terms, loads = call(
                 functools.partial(terms_body, group_rows),
@@ -797,8 +798,7 @@
             )
             terms_got = lax.all_to_all(terms, AXES, split_axis=0, concat_axis=0, tiled=True)
         if at == len(first_links) - 1:
-            attn_got, terms, down_other, cot_got = together(attn_got, terms, down_other, cot_got)
-            cot = grown(cot, cot_got)
+            attn_got, terms, down_other = together(attn_got, terms, down_other)
         attn_w = grown(attn_w, attn_got)
     cot_links = away + across
     attn_parts = [attn_w[:, :, : 2 * width], attn_w[:, :, 2 * width :]]
@@ -814,16 +814,16 @@
         if at == 0:
             if paired:
                 up_got = swap(up_away, away[0])
-                got, up_got = together(got, up_got)
         elif at == len(last_links[0]) - 1:
             cot_got = swap(cot, away[1])
             got, cot_got, terms_got = together(got, cot_got, terms_got)
+            if paired:
+                got, up_got = together(got, up_got)
             cot = grown(cot, cot_got)
         attn_parts = [grown(*pair) for pair in zip(attn_parts, got)]
-    part_shared_up = terms_got[:, :piece, :shared_units].reshape(width, shared_units)
-    modulation, own_lines = call(
+    modulation, own_lines, part_shared_up = call(
         functools.partial(shift_body, piece),
-        [((1, 6 * width), WIDE), ((total, 16, LANES), WIDE)],
+        [((1, 6 * width), WIDE), ((total, 16, LANES), WIDE), ((width, LANES), LOW)],
         (terms_got, pair_weight),
     )
     attn_far = [swap(part, core[0]) for part in attn_parts]
@@ -860,14 +860,13 @@
         got = [swap(part, masks[at]) for part, masks in zip(second_low, team_links)]
         if at == 0:
             item_lines = lax.all_to_all(own_lines, AXES, split_axis=0, concat_axis=0, tiled=True)
-            got, item_lines = together(got, item_lines)
             if paired:
                 got, up_last, shared_up_other = together(got, up_last, shared_up_other)
                 up_own = jnp.concatenate([up_mine, up_last], axis=0)
                 up_other = swap(up_own, far[0])
         elif at == 1:
             if paired:
-                got, up_other, cot_got = together(got, up_other, cot_got)
+                got, up_other, cot_got, item_lines = together(got, up_other, cot_got, item_lines)
                 routed, hidden = 2 * units, 2 * units + 2 * shared_slot
                 (down_cat,) = call(
                     down_join_body, [((hidden, width), LOW)], (where, down_own, down_other), smem=(0,)
@@ -884,7 +883,7 @@
         )
     else:
         part_up = lax.all_to_all(expert_up[0], "batch", split_axis=1, concat_axis=0, tiled=True)
-        held = gather_far([part_up, part_shared_up, expert_down[0], shared_down], far)
+        held = gather_far([part_up, part_shared_up[:, :shared_units], expert_down[0], shared_down], far)
         slot = up_to(units, LANES)
         routed, hidden = len(held) * slot, len(held) * (slot + shared_slot)
         up_cat = jnp.concatenate(
@@ -995,19 +994,22 @@
         got = [swap(high, masks[-1 - at]) for high, masks in zip(highs, orders)]
         if at == 0:
             got, up_grads = together(got, list(up_grads))
+            if paired:
+                keep_up, send_up0, send_up1 = up_grads
+                twin_up0 = swap(send_up0, far[0])
         elif at == 1:
             got, down_grads, out_got = together(got, list(down_grads), out_got)
             if paired:
-                keep_up, send_up0, send_up1 = up_grads
                 keep_down, send_down = down_grads
-                twin_up0, twin_up1 = swap(send_up0, far[0]), swap(send_up1, far[0])
+                got, twin_up0 = together(got, twin_up0)
+                twin_up1 = swap(send_up1, far[0])
         elif at == 2 and paired:
             out_got = swap(out_send0, across[0])
-            got, out_got, twin_up0 = together(got, out_got, twin_up0)
-            twin_down = swap(tie(send_down, twin_up0), far[0])
+            got, out_got, twin_up1 = together(got, out_got, twin_up1)
+            twin_down = swap(tie(send_down, twin_up1), far[0])
         elif at == sums_at and paired:
             out_got1 = swap(out_send1, across[0])
-            got, twin_up1 = together(got, twin_up1)
+            got = list(together(*got))
         else:
             got = together(*got)
         if at < sums_at:
@@ -1028,7 +1030,7 @@
     if paired:
         up_own = call(twin_up_body, [((group_rows, up_lanes), LOW)] * 4, (keep_up, twin_up0, twin_up1))
         folded, up_own = together(folded, up_own)
-        up_got = [piece_ if at < 2 else swap(piece_, away_masks[at]) for at, piece_ in enumerate(up_own)]
+        up_got = [piece_ if not at else swap(piece_, away_masks[at]) for at, piece_ in enumerate(up_own)]
 
     sent_cols = (count, 4 * width // experts)
     grad_tokens, d_mod_sent, *d_cols = call(
@@ -1049,20 +1051,27 @@
             add_join_body, [((2, *block), LOW), ((2, *block), LOW)], (out_low, out_got, out_got1)
         )
         out_got = swap(out_high, away[1])
-        cols_got[1], twin_down, up_got[3] = together(cols_got[1], twin_down, up_got[3])
+        twin_down = tie(twin_down, cols_got[1], up_got[3])
         grad_expert_down, shared_own = call(
             twin_down_body, [((units, width), WIDE), ((shared_units, width), LOW)], (keep_down, twin_down)
         )
         d_mod_sent = tie(d_mod_sent, shared_own)
-        cols_got, up_got, shared_own = together(cols_got, up_got, shared_own)
-        up_got[1] = swap(up_got[1], away_masks[1])
+        after = tie(where, shared_own, *up_got)
+        d_mod_all = lax.all_to_all(d_mod_sent, AXES, split_axis=0, concat_axis=0, tiled=True)
+        grad_ada_weight, grad_ada_bias, sent = call(
+            functools.partial(ada_body, experts),
+            [((group_rows, 6 * width // experts), WIDE), ((6 * width,), WIDE), ((total, 8, LANES), WIDE)],
+            (where, d_mod_all, cond_all, ada_weight),
+            scratch=[((total, 6 * width), LOW)],
+            smem=(0,),
+        )
         sum_links = [away + far, away[:1] + far + away[1:]]
         sum_masks = [[mask // experts for mask in order(masks)] for masks in sum_links]
         term_half = ((4, group_rows, width // 2), LOW)
         attn_sent = call(
             functools.partial(attn_terms_body, sum_masks),
             [term_half] * 4,
-            (where, *both_group, *cols_got),
+            (after, *both_group, *cols_got),
             scratch=[((width, width), WIDE)],
             smem=(0,),
         )
@@ -1074,6 +1083,7 @@
                 out_low, out_high = added(out_low, out_got)
                 out_got = swap(out_high, away[0])
             elif at == 1:
+                got, sent = together(got, sent)
                 grad_expert_up, crossed = call(
                     up_rows_body,
                     [
@@ -1097,6 +1107,14 @@
             scratch=[((group_rows, width), WIDE)],
         )
     else:
+        d_mod_all = lax.all_to_all(d_mod_sent, AXES, split_axis=0, concat_axis=0, tiled=True)
+        grad_ada_weight, grad_ada_bias, sent = call(
+            functools.partial(ada_body, experts),
+            [((group_rows, 6 * width // experts), WIDE), ((6 * width,), WIDE), ((total, 8, LANES), WIDE)],
+            (where, d_mod_all, cond_all, ada_weight),
+            scratch=[((total, 6 * width), LOW)],
+            smem=(0,),
+        )
         natural = jnp.arange(experts, dtype=jnp.int32) ^ my_expert
         both_group = lax.all_gather(both, "expert", axis=0)
         d_cols = jnp.take(jnp.stack(d_cols), natural, axis=0)
@@ -1152,14 +1170,6 @@
         shared_rows = lax.all_to_all(shared_rows, "expert", split_axis=0, concat_axis=0, tiled=True)
         grad_shared_up = shared_rows.transpose(2, 1, 0, 3).reshape(group_rows, groups * shared_units).astype(WIDE)
 
-    d_mod_all = lax.all_to_all(d_mod_sent, AXES, split_axis=0, concat_axis=0, tiled=True)
-    grad_ada_weight, grad_ada_bias, sent = call(
-        functools.partial(ada_body, experts),
-        [((group_rows, 6 * width // experts), WIDE), ((1, 6 * width), WIDE), ((total, 8, LANES), WIDE)],
-        (where, d_mod_all, cond_all, ada_weight),
-        scratch=[((total, 6 * width), LOW)],
-        smem=(0,),
-    )
     d_cond_act = lax.all_to_all(sent, AXES, split_axis=0, concat_axis=0, tiled=True)
     d_cond_act = d_cond_act[:, 0, :piece].reshape(1, width)
     _, silu_back = jax.vjp(jax.nn.silu, cond.astype(WIDE))
@@ -1171,7 +1181,7 @@
         grad_cond,
         grad_gate_weights.T,
         grad_ada_weight,
-        grad_ada_bias[0],
+        grad_ada_bias,
         grad_qkv,
         grad_out,
         grad_shared_up,

time: 280 us -> 269 us (0.961)
  waiting for transfers between devices: 99 us -> 91.7 us
  starting transfers between devices: 76.1 us -> 82.2 us
  other arithmetic: 22.2 us -> 17.1 us
  local copies, waits for them, and re-layouts: 15 us -> 11.4 us
    ppermute x59, waiting for transfers between devices: 99 us -> 82.7 us  [swap(): return lax.ppermute(values, AXES, [(at, at ^ mask) for at in range(total)])]
    ppermute x59, starting transfers between devices: 56.2 us -> 64.6 us  [swap(): return lax.ppermute(values, AXES, [(at, at ^ mask) for at in range(total)])]
    all_to_all x1, waiting for transfers between devices: 0.01 us -> 6.25 us  [shards(): lax.all_to_all(own_lines, AXES, split_axis=0, concat_axis=0, tiled=True)]
    all_to_all x2, starting transfers between devices: 10.4 us -> 6.38 us  [shards(): lax.all_to_all(sent, AXES, split_axis=0, concat_axis=0, tiled=True)]
    concatenate x15 -> x14, other arithmetic: 15.9 us -> 14.3 us  [grown(): return jnp.concatenate([values, got], axis=0)]
    unnamed x145 -> x181, local copies, waits for them, and re-layouts: 10.7 us -> 10.1 us
  transfers between devices with their start and end apart: 64 -> 64, of which waited for: 32 -> 31; matrix products, arithmetic and copies ran while one was open for 7% -> 5% of each run, Pallas kernels for 23% -> 24%
where the time goes in v3:
time: 269 us; the launch traced here: 268 us
  waiting for transfers between devices  91.7 us (34%)
  starting transfers between devices  82.2 us (31%)
  Pallas kernels  63.4 us (24%)
  other arithmetic  17.1 us (6%)
  local copies, waits for them, and re-layouts  11.4 us (4%)
    ppermute x59, waiting for transfers between devices, swap(): return lax.ppermute(values, AXES, [(at, at ^ mask) for at in range(total)])  82.7 us
    ppermute x59, starting transfers between devices, swap(): return lax.ppermute(values, AXES, [(at, at ^ mask) for at in range(total)])  64.6 us
    pallas_call x4, Pallas kernels, sweep(): pl.pallas_call(body, out_shape=[jax.ShapeDtypeStruct(shape, kind) for sha...  31.7 us
    pallas_call x29, Pallas kernels, call(): pl.pallas_call(body, out_shape=[jax.ShapeDtypeStruct(shape, kind) for sha...  31.7 us
    concatenate x14, other arithmetic, grown(): return jnp.concatenate([values, got], axis=0)  14.3 us
    unnamed x181, local copies, waits for them, and re-layouts  10.1 us
    all_to_all x2, starting transfers between devices, shards(): lax.all_to_all(sent, AXES, split_axis=0, concat_axis=0, tiled=True)  6.38 us
    all_to_all x1, waiting for transfers between devices, shards(): lax.all_to_all(own_lines, AXES, split_axis=0, concat_axis=0, tiled=True)  6.25 us
  transfers between devices with their start and end apart: 64, of which 31 were waited for; matrix products, arithmetic and copies ran while one was open for 5% of the time, Pallas kernels for 24%

profile of v3, /device:TPU:0, one launch (start us, length us, event | category | flops | bytes accessed | tf_op | source)
XLA Modules:
  0.0 268.2 jit_solution(10181126100757482834)
XLA Ops:
  0.7 4.1 %collective-permute-start = (bf16[1,128,768]{2,1,0:T(8,128)(2,1)}, bf16[1,128,768]{2,1,0:T(8,128)(2,1)S(1)}, u32[]{:S(2)}, u32[]{:S(2)}) collective-permute-start(bf16[1,128,768]{2,1,0:T(8,128)(2,1)} %bitcast.66), channel_id=1, source_target_pairs={{0,16},{1,17},{2,18},{3,19},{4,20},{5,21},{6,22},{7,23},{8,24},{9,... | collective-permute-start | bytes 589832 | tf_op jit(solution)/shard_map/ppermute | solution.py:100
  8.2 3.8 %all-to-all-start = ((bf16[32,16,128]{2,1,0:T(8,128)(2,1)}), bf16[32,16,128]{2,1,0:T(8,128)(2,1)S(1)}, u32[]{:S(2)}, u32[]{:S(2)}) async-start(bf16[32,16,128]{2,1,0:T(8,128)(2,1)} %get-tuple-element.194), calls=%async_computation | async-start | bytes 262144 | tf_op jit(solution)/shard_map/all_to_all | solution.py:779
  13.3 1.8 collective-permute-start.3
  15.3 2.4 collective-permute-start.1
  17.7 2.7 %all-to-all-done.got.cond = bf16[32,16,128]{2,1,0:T(8,128)(2,1)S(1)} async-done(((bf16[32,16,128]{2,1,0:T(8,128)(2,1)}), bf16[32,16,128]{2,1,0:T(8,128)(2,1)S(1)}, u32[]{:S(2)}, u32[]{:S(2)}) %all-to-all-start) | async-done | bytes 131104 | tf_op jit(solution)/shard_map/all_to_all | solution.py:779
  20.4 4.7 %collective-permute-done.1 = bf16[1,24,3072]{2,1,0:T(8,128)(2,1)S(1)} collective-permute-done((bf16[1,24,3072]{2,1,0:T(8,128)(2,1)S(1)}, bf16[1,24,3072]{2,1,0:T(8,128)(2,1)S(1)}, u32[]{:S(2)}, u32[]{:S(2)}) %collective-permute-start.1) | collective-permute-done | bytes 147488 | tf_op jit(solution)/shard_map/ppermute | solution.py:100
  26.1 2.6 shard_map.256
  29.6 4.4 %collective-permute-done.2 = bf16[2,24,3072]{2,1,0:T(8,128)(2,1)S(1)} collective-permute-done((bf16[2,24,3072]{2,1,0:T(8,128)(2,1)S(1)}, bf16[2,24,3072]{2,1,0:T(8,128)(2,1)S(1)}, u32[]{:S(2)}, u32[]{:S(2)}) %collective-permute-start.2) | collective-permute-done | bytes 294944 | tf_op jit(solution)/shard_map/ppermute | solution.py:100
  34.1 2.0 collective-permute-start.4
  37.5 3.8 %all-to-all-start.1 = ((bf16[32,64,128]{2,1,0:T(8,128)(2,1)}), bf16[32,64,128]{2,1,0:T(8,128)(2,1)S(1)}, u32[]{:S(2)}, u32[]{:S(2)}) async-start(bf16[32,64,128]{2,1,0:T(8,128)(2,1)} %get-tuple-element.197), calls=%async_computation.1 | async-start | bytes 1048576 | tf_op jit(solution)/shard_map/all_to_all | solution.py:799
  45.5 1.7 collective-permute-start.7
  49.3 2.6 collective-permute-start.9
  51.9 15.5 %collective-permute-done.8 = bf16[2,128,768]{2,1,0:T(8,128)(2,1)S(1)} collective-permute-done((bf16[2,128,768]{2,1,0:T(8,128)(2,1)S(1)}, bf16[2,128,768]{2,1,0:T(8,128)(2,1)S(1)}, u32[]{:S(2)}, u32[]{:S(2)}) %collective-permute-start.8) | collective-permute-done | bytes 393248 | tf_op jit(solution)/shard_map/ppermute | solution.py:100
  72.6 1.7 collective-permute-start.14
  75.1 1.5 collective-permute-start.15
  76.6 3.8 %shard_map.259 = (bf16[128,1536]{1,0:T(8,128)(2,1)S(1)}, bf16[128,2304]{1,0:T(8,128)(2,1)S(1)}, f32[128,128]{1,0:T(8,128)S(1)}, f32[128,768]{1,0:T(8,128)S(1)}, ...) custom-call(s32[3]{0:T(128)S(1)} %pad_add_fusion.where, ...), custom_call_target="tpu_custom_call" | custom-call | tf_op jit(solution)/shard_map/pallas_call | solution.py:41
  81.8 1.5 collective-permute-start.13
  84.8 2.9 %collective-permute-done.12 = bf16[1,128,384]{2,1,0:T(8,128)(2,1)S(1)} collective-permute-done((bf16[1,128,384]{2,1,0:T(8,128)(2,1)S(1)}, bf16[1,128,384]{2,1,0:T(8,128)(2,1)S(1)}, u32[]{:S(2)}, u32[]{:S(2)}) %collective-permute-start.12) | collective-permute-done | bytes 98336 | tf_op jit(solution)/shard_map/ppermute | solution.py:100
  89.4 3.8 %all-to-all-start.2 = ((f32[32,16,128]{2,1,0:T(8,128)}), f32[32,16,128]{2,1,0:T(8,128)}, u32[]{:S(2)}, u32[]{:S(2)}) async-start(f32[32,16,128]{2,1,0:T(8,128)} %copy-done.41), calls=%async_computation.2 | async-start | bytes 524288 | tf_op jit(solution)/shard_map/all_to_all | solution.py:862
  93.2 1.6 pad_maximum_fusion.15
  94.9 1.5 collective-permute-start.16
  96.4 1.6 pad_maximum_fusion.16
  98.1 2.4 collective-permute-start.17
  100.5 6.2 %all-to-all-done.2.lines.refs_6_ = f32[32,16,128]{2,1,0:T(8,128)} async-done(((f32[32,16,128]{2,1,0:T(8,128)}), f32[32,16,128]{2,1,0:T(8,128)}, u32[]{:S(2)}, u32[]{:S(2)}) %all-to-all-start.2) | async-done | bytes 262176 | tf_op jit(solution)/shard_map/all_to_all | solution.py:862
  106.7 1.6 collective-permute-done.16
  108.3 2.6 collective-permute-done.17
  114.6 1.5 collective-permute-start.20
  117.0 1.4 shard_map.262.refs_8_
  118.5 5.2 %shard_map.261 = (bf16[4,512,1024]{2,1,0:T(8,128)(2,1)S(1)}, bf16[4,512,768]{2,1,0:T(8,128)(2,1)S(1)}) custom-call(s32[3]{0:T(128)S(1)} %pad_add_fusion.where, bf16[2,2,2,128,768]{4,3,2,1,0:T(8,128)(2,1)S(1)} %bitcast.50, bf16[2,2,2,128,768]{4,3,2,1,0:T(8,128)(2,1)S(1)} %bitcast.60, f32[32,16,128]{2,1,0:T(8,128)} %all-to-all-done.2.lines.refs_6_, ...), custom_call_target="tpu_custom_call" | custom-call | tf_op jit(solution)/shard_map/pallas_call | solution.py:52
  123.7 2.4 collective-permute-done.20
  130.0 1.8 collective-permute-done.23
  134.8 15.5 %shard_map.263 = (bf16[2,2,2,144,384]{4,3,2,1,0:T(8,128)(2,1)S(1)}, bf16[2,2,2,144,384]{4,3,2,1,0:T(8,128)(2,1)S(1)}, bf16[2,2,2,144,384]{4,3,2,1,0:T(8,128)(2,1...) custom-call(s32[3]{0:T(128)S(1)} %pad_add_fusion.where, ...), custom_call_target="tpu_custom_call" | custom-call | tf_op jit(solution)/shard_map/pallas_call | solution.py:52
  150.3 2.0 collective-permute-done.27.both3
  153.2 5.5 %shard_map.264 = (bf16[4,96,960]{2,1,0:T(8,128)(2,1)S(1)}, bf16[2,96,960]{2,1,0:T(8,128)(2,1)S(1)}, bf16[2,96,960]{2,1,0:T(8,128)(2,1)S(1)}) custom-call(s32[3]{0:T(128)S(1)} %pad_add_fusion.where, bf16[2,2,2,128,384]{4,3,2,1,0:T(8,128)(2,1)S(1)} %bitcast.57, bf16[2,2,2,128,384]{4,3,2,1,0:T(8,128)(2,1)S(1)} %bitcast.59, ...), custom_call_target="tpu_custom_call" | custom-call | tf_op jit(solution)/shard_map/pallas_call | solution.py:52
  160.2 1.5 collective-permute-start.33
  161.7 5.5 %shard_map.267 = (f32[480,768]{1,0:T(8,128)S(1)}, bf16[480,768]{1,0:T(8,128)(2,1)S(1)}) custom-call(s32[3]{0:T(128)S(1)} %pad_add_fusion.where, bf16[4,512,768]{2,1,0:T(8,128)(2,1)S(1)} %get-tuple-element.254.d_mlp, bf16[4,512,1024]{2,1,0:T(8,128)(2,1)S(1)} %get-tuple-element.255.act), custom_call_target="tpu_custom_call" | custom-call | tf_op jit(solution)/shard_map/pallas_call | solution.py:52
  167.2 4.1 %collective-permute-done.30.got = bf16[4,144,384]{2,1,0:T(8,128)(2,1)S(1)} collective-permute-done((bf16[4,144,384]{2,1,0:T(8,128)(2,1)S(1)}, bf16[4,144,384]{2,1,0:T(8,128)(2,1)S(1)}, u32[]{:S(2)}, u32[]{:S(2)}) %collective-permute-start.30) | collective-permute-done | bytes 442400 | tf_op jit(solution)/shard_map/ppermute | solution.py:100
  172.3 1.5 collective-permute-start.36
  173.8 1.5 collective-permute-start.37
  175.9 2.0 collective-permute-start.35
  178.0 5.6 %collective-permute-done.37.got1 = bf16[2,96,960]{2,1,0:T(8,128)(2,1)S(1)} collective-permute-done((bf16[2,96,960]{2,1,0:T(8,128)(2,1)S(1)}, bf16[2,96,960]{2,1,0:T(8,128)(2,1)S(1)}, u32[]{:S(2)}, u32[]{:S(2)}) %collective-permute-start.37) | collective-permute-done | bytes 368672 | tf_op jit(solution)/shard_map/ppermute | solution.py:100
  184.7 2.5 collective-permute-done.35.got
  188.5 1.5 collective-permute-start.39
  191.5 2.6 collective-permute-done.38
  194.1 3.5 %collective-permute-done.39 = bf16[1,144,384]{2,1,0:T(8,128)(2,1)S(1)} collective-permute-done((bf16[1,144,384]{2,1,0:T(8,128)(2,1)S(1)}, bf16[1,144,384]{2,1,0:T(8,128)(2,1)S(1)}, u32[]{:S(2)}, u32[]{:S(2)}) %collective-permute-start.39) | collective-permute-done | bytes 110624 | tf_op jit(solution)/shard_map/ppermute | solution.py:100
  197.6 1.5 collective-permute-start.40
  199.1 1.8 collective-permute-start.44
  200.9 7.9 %shard_map.274 = (f32[128,768]{1,0:T(8,128)}, bf16[32,36,128]{2,1,0:T(8,128)(2,1)S(1)}, bf16[128,768]{1,0:T(8,128)(2,1)S(1)}, bf16[128,768]{1,0:T(8,128)(2,1)S(1...) custom-call(s32[3]{0:T(128)S(1)} %pad_add_fusion.where, bf16[128,768]{1,0:T(8,128)(2,1)S(1)} %copy-done.21, ...), custom_call_target="tpu_custom_call" | custom-call | tf_op jit(solution)/shard_map/pallas_call | solution.py:41
  216.7 3.5 %all-to-all-start.3 = ((bf16[32,36,128]{2,1,0:T(8,128)(2,1)}), bf16[32,36,128]{2,1,0:T(8,128)(2,1)S(1)}, u32[]{:S(2)}, u32[]{:S(2)}) async-start(bf16[32,36,128]{2,1,0:T(8,128)(2,1)} %copy-done.38), calls=%async_computation.3 | async-start | bytes 655360 | tf_op jit(solution)/shard_map/all_to_all | solution.py:1060
  222.9 2.6 shard_map.277
  225.6 1.6 collective-permute-start.48
  227.9 4.7 %collective-permute-done.50.got = bf16[2,144,768]{2,1,0:T(8,128)(2,1)S(1)} collective-permute-done((bf16[2,144,768]{2,1,0:T(8,128)(2,1)}, bf16[2,144,768]{2,1,0:T(8,128)(2,1)S(1)}, u32[]{:S(2)}, u32[]{:S(2)}) %collective-permute-start.50) | collective-permute-done | bytes 442400 | tf_op jit(solution)/shard_map/ppermute | solution.py:100
  232.6 4.1 %collective-permute-done.48.got = bf16[4,96,384]{2,1,0:T(8,128)(2,1)S(1)} collective-permute-done((bf16[4,96,384]{2,1,0:T(8,128)(2,1)S(1)}, bf16[4,96,384]{2,1,0:T(8,128)(2,1)S(1)}, u32[]{:S(2)}, u32[]{:S(2)}) %collective-permute-start.48) | collective-permute-done | bytes 294944 | tf_op jit(solution)/shard_map/ppermute | solution.py:100
  236.7 4.1 %collective-permute-done.49.got = bf16[4,96,384]{2,1,0:T(8,128)(2,1)S(1)} collective-permute-done((bf16[4,96,384]{2,1,0:T(8,128)(2,1)S(1)}, bf16[4,96,384]{2,1,0:T(8,128)(2,1)S(1)}, u32[]{:S(2)}, u32[]{:S(2)}) %collective-permute-start.49) | collective-permute-done | bytes 294944 | tf_op jit(solution)/shard_map/ppermute | solution.py:100
  241.3 1.6 collective-permute-start.52
  243.0 2.5 collective-permute-start.55
  245.6 1.8 shard_map.282
  247.4 2.1 shard_map.281
  250.1 2.5 collective-permute-start.54
  252.6 2.6 all-to-all-start.4
  255.4 1.7 collective-permute-start.57
  257.1 2.5 collective-permute-done.55
  259.5 2.9 %collective-permute-done.53 = bf16[1,96,384]{2,1,0:T(8,128)(2,1)S(1)} collective-permute-done((bf16[1,96,384]{2,1,0:T(8,128)(2,1)S(1)}, bf16[1,96,384]{2,1,0:T(8,128)(2,1)S(1)}, u32[]{:S(2)}, u32[]{:S(2)}) %collective-permute-start.53) | collective-permute-done | bytes 73760 | tf_op jit(solution)/shard_map/ppermute | solution.py:100
  263.6 1.4 shard_map.287
  (306 shorter events, 60.3 us)
Async XLA Ops:
  0.7 14.6 %collective-permute-start = (bf16[1,128,768]{2,1,0:T(8,128)(2,1)}, bf16[1,128,768]{2,1,0:T(8,128)(2,1)S(1)}, u32[]{:S(2)}, u32[]{:S(2)}) collective-permute-start(bf16[1,128,768]{2,1,0:T(8,128)(2,1)} %bitcast.66), channel_id=1, source_target_pairs={{0,16},{1,17},{2,18},{3,19},{4,20},{5,21},{6,22},{7,23},{8,24},{9,... | collective-permute-start | bytes 589832 | tf_op jit(solution)/shard_map/ppermute | solution.py:100
  8.2 12.2 %all-to-all-start = ((bf16[32,16,128]{2,1,0:T(8,128)(2,1)}), bf16[32,16,128]{2,1,0:T(8,128)(2,1)S(1)}, u32[]{:S(2)}, u32[]{:S(2)}) async-start(bf16[32,16,128]{2,1,0:T(8,128)(2,1)} %get-tuple-element.194), calls=%async_computation | async-start | bytes 262144 | tf_op jit(solution)/shard_map/all_to_all | solution.py:779
  13.3 20.7 %collective-permute-start.3 = (bf16[480,768]{1,0:T(8,128)(2,1)S(1)}, bf16[480,768]{1,0:T(8,128)(2,1)S(1)}, u32[]{:S(2)}, u32[]{:S(2)}) collective-permute-start(bf16[480,768]{1,0:T(8,128)(2,1)S(1)} %pad_maximum_fusion.6.own), channel_id=1, source_target_pairs={{0,4},{1,5},{2,6},{3,7},{4,0},{5,1},{6,2},{7,3},{8,12},{9,13},{10,... | collective-permute-start | bytes 2211848 | tf_op jit(solution)/shard_map/ppermute | solution.py:100
  15.3 9.9 %collective-permute-start.1 = (bf16[1,24,3072]{2,1,0:T(8,128)(2,1)S(1)}, bf16[1,24,3072]{2,1,0:T(8,128)(2,1)S(1)}, u32[]{:S(2)}, u32[]{:S(2)}) collective-permute-start(bf16[1,24,3072]{2,1,0:T(8,128)(2,1)S(1)} %maximum_bitcast_fusion), channel_id=1, source_target_pairs={{0,16},{1,17},{2,18},{3,19},{4,20},{5,21},{6,22},{7,23},{8,24},{9,... | collective-permute-start | bytes 442376 | tf_op jit(solution)/shard_map/ppermute | solution.py:100
  25.8 8.2 %collective-permute-start.2 = (bf16[2,24,3072]{2,1,0:T(8,128)(2,1)S(1)}, bf16[2,24,3072]{2,1,0:T(8,128)(2,1)S(1)}, u32[]{:S(2)}, u32[]{:S(2)}) collective-permute-start(bf16[2,24,3072]{2,1,0:T(8,128)(2,1)S(1)} %pad_maximum_fusion.13), channel_id=1, source_target_pairs={{0,8},{1,9},{2,10},{3,11},{4,12},{5,13},{6,14},{7,15},{8,0},{9,1},... | collective-permute-start | bytes 884744 | tf_op jit(solution)/shard_map/ppermute | solution.py:100
  34.1 8.3 %collective-permute-start.4 = (bf16[4,24,1536]{2,1,0:T(8,128)(2,1)S(1)}, bf16[4,24,1536]{2,1,0:T(8,128)(2,1)S(1)}, u32[]{:S(2)}, u32[]{:S(2)}) collective-permute-start(bf16[4,24,1536]{2,1,0:T(8,128)(2,1)S(1)} %get-tuple-element.400), channel_id=1, source_target_pairs={{0,4},{1,5},{2,6},{3,7},{4,0},{5,1},{6,2},{7,3},{8,12},{9,13},{10,... | collective-permute-start | bytes 884744 | tf_op jit(solution)/shard_map/ppermute | solution.py:100
  36.1 8.4 %collective-permute-start.6 = (bf16[4,24,1536]{2,1,0:T(8,128)(2,1)S(1)}, bf16[4,24,1536]{2,1,0:T(8,128)(2,1)S(1)}, u32[]{:S(2)}, u32[]{:S(2)}) collective-permute-start(bf16[4,24,1536]{2,1,0:T(8,128)(2,1)S(1)} %get-tuple-element.399), channel_id=1, source_target_pairs={{0,2},{1,3},{2,0},{3,1},{4,6},{5,7},{6,4},{7,5},{8,10},{9,11},{10,... | collective-permute-start | bytes 884744 | tf_op jit(solution)/shard_map/ppermute | solution.py:100
  37.5 29.9 %all-to-all-start.1 = ((bf16[32,64,128]{2,1,0:T(8,128)(2,1)}), bf16[32,64,128]{2,1,0:T(8,128)(2,1)S(1)}, u32[]{:S(2)}, u32[]{:S(2)}) async-start(bf16[32,64,128]{2,1,0:T(8,128)(2,1)} %get-tuple-element.197), calls=%async_computation.1 | async-start | bytes 1048576 | tf_op jit(solution)/shard_map/all_to_all | solution.py:799
  43.2 25.0 %collective-permute-start.5 = (bf16[8,24,1536]{2,1,0:T(8,128)(2,1)}, bf16[8,24,1536]{2,1,0:T(8,128)(2,1)}, u32[]{:S(2)}, u32[]{:S(2)}) collective-permute-start(bf16[8,24,1536]{2,1,0:T(8,128)(2,1)} %pad_maximum_fusion.7), channel_id=1, source_target_pairs={{0,2},{1,3},{2,0},{3,1},{4,6},{5,7},{6,4},{7,5},{8,10},{9,11},{10,... | collective-permute-start | bytes 1769480 | tf_op jit(solution)/shard_map/ppermute | solution.py:100
  45.5 22.7 %collective-permute-start.7 = (bf16[8,24,1536]{2,1,0:T(8,128)(2,1)}, bf16[8,24,1536]{2,1,0:T(8,128)(2,1)}, u32[]{:S(2)}, u32[]{:S(2)}) collective-permute-start(bf16[8,24,1536]{2,1,0:T(8,128)(2,1)} %pad_maximum_fusion.8), channel_id=1, source_target_pairs={{0,4},{1,5},{2,6},{3,7},{4,0},{5,1},{6,2},{7,3},{8,12},{9,13},{10,... | collective-permute-start | bytes 1769480 | tf_op jit(solution)/shard_map/ppermute | solution.py:100
  47.3 20.1 %collective-permute-start.8 = (bf16[2,128,768]{2,1,0:T(8,128)(2,1)S(1)}, bf16[2,128,768]{2,1,0:T(8,128)(2,1)S(1)}, u32[]{:S(2)}, u32[]{:S(2)}) collective-permute-start(bf16[2,128,768]{2,1,0:T(8,128)(2,1)S(1)} %pad_maximum_fusion.10), channel_id=1, source_target_pairs={{0,8},{1,9},{2,10},{3,11},{4,12},{5,13},{6,14},{7,15},{8,0},{9,1},... | collective-permute-start | bytes 1179656 | tf_op jit(solution)/shard_map/ppermute | solution.py:100
  49.3 19.0 %collective-permute-start.9 = (bf16[2,96,768]{2,1,0:T(8,128)(2,1)S(1)}, bf16[2,96,768]{2,1,0:T(8,128)(2,1)}, u32[]{:S(2)}, u32[]{:S(2)}) collective-permute-start(bf16[2,96,768]{2,1,0:T(8,128)(2,1)S(1)} %get-tuple-element.205), channel_id=1, source_target_pairs={{0,16},{1,17},{2,18},{3,19},{4,20},{5,21},{6,22},{7,23},{8,24},{9,... | collective-permute-start | bytes 884744 | tf_op jit(solution)/shard_map/ppermute | solution.py:100
  69.5 7.1 %collective-permute-start.10 = (bf16[16,24,1536]{2,1,0:T(8,128)(2,1)S(1)}, bf16[16,24,1536]{2,1,0:T(8,128)(2,1)S(1)}, u32[]{:S(2)}, u32[]{:S(2)}) collective-permute-start(bf16[16,24,1536]{2,1,0:T(8,128)(2,1)S(1)} %pad_maximum_fusion.1), channel_id=1, source_target_pairs={{0,1},{1,0},{2,3},{3,2},{4,5},{5,4},{6,7},{7,6},{8,9},{9,8},{10,11... | collective-permute-start | bytes 3538952 | tf_op jit(solution)/shard_map/ppermute | solution.py:100
  71.0 5.6 %collective-permute-start.11 = (bf16[16,24,1536]{2,1,0:T(8,128)(2,1)S(1)}, bf16[16,24,1536]{2,1,0:T(8,128)(2,1)S(1)}, u32[]{:S(2)}, u32[]{:S(2)}) collective-permute-start(bf16[16,24,1536]{2,1,0:T(8,128)(2,1)S(1)} %pad_maximum_fusion.2), channel_id=1, source_target_pairs={{0,1},{1,0},{2,3},{3,2},{4,5},{5,4},{6,7},{7,6},{8,9},{9,8},{10,11... | collective-permute-start | bytes 3538952 | tf_op jit(solution)/shard_map/ppermute | solution.py:100
  72.6 12.2 %collective-permute-start.14 = (bf16[2,96,768]{2,1,0:T(8,128)(2,1)S(1)}, bf16[2,96,768]{2,1,0:T(8,128)(2,1)S(1)}, u32[]{:S(2)}, u32[]{:S(2)}) collective-permute-start(bf16[2,96,768]{2,1,0:T(8,128)(2,1)S(1)} %pad_maximum_fusion.14), channel_id=1, source_target_pairs={{0,8},{1,9},{2,10},{3,11},{4,12},{5,13},{6,14},{7,15},{8,0},{9,1},... | collective-permute-start | bytes 884744 | tf_op jit(solution)/shard_map/ppermute | solution.py:100
  75.1 9.8 %collective-permute-start.15 = (bf16[768,128]{1,0:T(8,128)(2,1)S(1)}, bf16[768,128]{1,0:T(8,128)(2,1)S(1)}, u32[]{:S(2)}, u32[]{:S(2)}) collective-permute-start(bf16[768,128]{1,0:T(8,128)(2,1)S(1)} %get-tuple-element.214.shared), channel_id=1, source_target_pairs={{0,4},{1,5},{2,6},{3,7},{4,0},{5,1},{6,2},{7,3},{8,12},{9,13},{10,... | collective-permute-start | bytes 589832 | tf_op jit(solution)/shard_map/ppermute | solution.py:100
  80.6 7.1 %collective-permute-start.12 = (bf16[1,128,384]{2,1,0:T(8,128)(2,1)S(1)}, bf16[1,128,384]{2,1,0:T(8,128)(2,1)S(1)}, u32[]{:S(2)}, u32[]{:S(2)}) collective-permute-start(bf16[1,128,384]{2,1,0:T(8,128)(2,1)S(1)} %bitcast.81), channel_id=1, source_target_pairs={{0,16},{1,17},{2,18},{3,19},{4,20},{5,21},{6,22},{7,23},{8,24},{9,... | collective-permute-start | bytes 294920 | tf_op jit(solution)/shard_map/ppermute | solution.py:100
  81.8 5.9 %collective-permute-start.13 = (bf16[1,128,384]{2,1,0:T(8,128)(2,1)S(1)}, bf16[1,128,384]{2,1,0:T(8,128)(2,1)S(1)}, u32[]{:S(2)}, u32[]{:S(2)}) collective-permute-start(bf16[1,128,384]{2,1,0:T(8,128)(2,1)S(1)} %bitcast.77), channel_id=1, source_target_pairs={{0,2},{1,3},{2,0},{3,1},{4,6},{5,7},{6,4},{7,5},{8,10},{9,11},{10,... | collective-permute-start | bytes 294920 | tf_op jit(solution)/shard_map/ppermute | solution.py:100
  84.3 22.5 %collective-permute-start.19 = (bf16[4,128,768]{2,1,0:T(8,128)(2,1)}, bf16[4,128,768]{2,1,0:T(8,128)(2,1)}, u32[]{:S(2)}, u32[]{:S(2)}) collective-permute-start(bf16[4,128,768]{2,1,0:T(8,128)(2,1)} %pad_maximum_fusion.3), channel_id=1, source_target_pairs={{0,2},{1,3},{2,0},{3,1},{4,6},{5,7},{6,4},{7,5},{8,10},{9,11},{10,... | collective-permute-start | bytes 2359304 | tf_op jit(solution)/shard_map/ppermute | solution.py:100
  88.7 22.2 %collective-permute-start.18 = (bf16[4,96,768]{2,1,0:T(8,128)(2,1)}, bf16[4,96,768]{2,1,0:T(8,128)(2,1)}, u32[]{:S(2)}, u32[]{:S(2)}) collective-permute-start(bf16[4,96,768]{2,1,0:T(8,128)(2,1)} %pad_maximum_fusion.9.own), channel_id=1, source_target_pairs={{0,4},{1,5},{2,6},{3,7},{4,0},{5,1},{6,2},{7,3},{8,12},{9,13},{10,... | collective-permute-start | bytes 1769480 | tf_op jit(solution)/shard_map/ppermute | solution.py:100
  89.4 17.3 %all-to-all-start.2 = ((f32[32,16,128]{2,1,0:T(8,128)}), f32[32,16,128]{2,1,0:T(8,128)}, u32[]{:S(2)}, u32[]{:S(2)}) async-start(f32[32,16,128]{2,1,0:T(8,128)} %copy-done.41), calls=%async_computation.2 | async-start | bytes 524288 | tf_op jit(solution)/shard_map/all_to_all | solution.py:862
  94.9 13.4 %collective-permute-start.16 = (bf16[2,128,384]{2,1,0:T(8,128)(2,1)}, bf16[2,128,384]{2,1,0:T(8,128)(2,1)}, u32[]{:S(2)}, u32[]{:S(2)}) collective-permute-start(bf16[2,128,384]{2,1,0:T(8,128)(2,1)} %pad_maximum_fusion.15), channel_id=1, source_target_pairs={{0,8},{1,9},{2,10},{3,11},{4,12},{5,13},{6,14},{7,15},{8,0},{9,1},... | collective-permute-start | bytes 589832 | tf_op jit(solution)/shard_map/ppermute | solution.py:100
  98.1 12.8 %collective-permute-start.17 = (bf16[2,128,384]{2,1,0:T(8,128)(2,1)}, bf16[2,128,384]{2,1,0:T(8,128)(2,1)}, u32[]{:S(2)}, u32[]{:S(2)}) collective-permute-start(bf16[2,128,384]{2,1,0:T(8,128)(2,1)} %pad_maximum_fusion.16), channel_id=1, source_target_pairs={{0,16},{1,17},{2,18},{3,19},{4,20},{5,21},{6,22},{7,23},{8,24},{9,... | collective-permute-start | bytes 589832 | tf_op jit(solution)/shard_map/ppermute | solution.py:100
  114.5 4.0 %collective-permute-start.22 = (bf16[8,128,768]{2,1,0:T(8,128)(2,1)S(1)}, bf16[8,128,768]{2,1,0:T(8,128)(2,1)S(1)}, u32[]{:S(2)}, u32[]{:S(2)}) collective-permute-start(bf16[8,128,768]{2,1,0:T(8,128)(2,1)S(1)} %pad_maximum_fusion), channel_id=1, source_target_pairs={{0,1},{1,0},{2,3},{3,2},{4,5},{5,4},{6,7},{7,6},{8,9},{9,8},{10,11... | collective-permute-start | bytes 4718600 | tf_op jit(solution)/shard_map/ppermute | solution.py:100
  114.6 11.5 %collective-permute-start.20 = (bf16[4,128,384]{2,1,0:T(8,128)(2,1)S(1)}, bf16[4,128,384]{2,1,0:T(8,128)(2,1)S(1)}, u32[]{:S(2)}, u32[]{:S(2)}) collective-permute-start(bf16[4,128,384]{2,1,0:T(8,128)(2,1)S(1)} %pad_maximum_fusion.11), channel_id=1, source_target_pairs={{0,2},{1,3},{2,0},{3,1},{4,6},{5,7},{6,4},{7,5},{8,10},{9,11},{10,... | collective-permute-start | bytes 1179656 | tf_op jit(solution)/shard_map/ppermute | solution.py:100
  116.1 11.2 %collective-permute-start.21 = (bf16[4,128,384]{2,1,0:T(8,128)(2,1)S(1)}, bf16[4,128,384]{2,1,0:T(8,128)(2,1)S(1)}, u32[]{:S(2)}, u32[]{:S(2)}) collective-permute-start(bf16[4,128,384]{2,1,0:T(8,128)(2,1)S(1)} %pad_maximum_fusion.12), channel_id=1, source_target_pairs={{0,8},{1,9},{2,10},{3,11},{4,12},{5,13},{6,14},{7,15},{8,0},{9,1},... | collective-permute-start | bytes 1179656 | tf_op jit(solution)/shard_map/ppermute | solution.py:100
  129.5 2.4 collective-permute-start.23
  129.5 3.4 %collective-permute-start.24 = (bf16[8,128,384]{2,1,0:T(8,128)(2,1)S(1)}, bf16[8,128,384]{2,1,0:T(8,128)(2,1)S(1)}, u32[]{:S(2)}, u32[]{:S(2)}) collective-permute-start(bf16[8,128,384]{2,1,0:T(8,128)(2,1)S(1)} %pad_maximum_fusion.5), channel_id=1, source_target_pairs={{0,1},{1,0},{2,3},{3,2},{4,5},{5,4},{6,7},{7,6},{8,9},{9,8},{10,11... | collective-permute-start | bytes 2359304 | tf_op jit(solution)/shard_map/ppermute | solution.py:100
  132.9 17.4 %collective-permute-start.25 = (bf16[128,1536]{1,0:T(8,128)(2,1)S(1)}, bf16[128,1536]{1,0:T(8,128)(2,1)S(1)}, u32[]{:S(2)}, u32[]{:S(2)}) collective-permute-start(bf16[128,1536]{1,0:T(8,128)(2,1)S(1)} %copy-done.28), channel_id=1, source_target_pairs={{0,1},{1,0},{2,3},{3,2},{4,5},{5,4},{6,7},{7,6},{8,9},{9,8},{10,11... | collective-permute-start | bytes 1179656 | tf_op jit(solution)/shard_map/ppermute | solution.py:100
  133.1 17.2 %collective-permute-start.26 = (bf16[128,1536]{1,0:T(8,128)(2,1)S(1)}, bf16[128,1536]{1,0:T(8,128)(2,1)S(1)}, u32[]{:S(2)}, u32[]{:S(2)}) collective-permute-start(bf16[128,1536]{1,0:T(8,128)(2,1)S(1)} %copy-done.28), channel_id=1, source_target_pairs={{0,2},{1,3},{2,0},{3,1},{4,6},{5,7},{6,4},{7,5},{8,10},{9,11},{10,... | collective-permute-start | bytes 1179656 | tf_op jit(solution)/shard_map/ppermute | solution.py:100
  133.6 18.7 %collective-permute-start.27 = (bf16[128,1536]{1,0:T(8,128)(2,1)S(1)}, bf16[128,1536]{1,0:T(8,128)(2,1)S(1)}, u32[]{:S(2)}, u32[]{:S(2)}) collective-permute-start(bf16[128,1536]{1,0:T(8,128)(2,1)S(1)} %copy-done.28), channel_id=1, source_target_pairs={{0,3},{1,2},{2,1},{3,0},{4,7},{5,6},{6,5},{7,4},{8,11},{9,10},{10,... | collective-permute-start | bytes 1179656 | tf_op jit(solution)/shard_map/ppermute | solution.py:100
  152.3 19.5 %collective-permute-start.32 = (bf16[8,144,768]{2,1,0:T(8,128)(2,1)S(1)}, bf16[8,144,768]{2,1,0:T(8,128)(2,1)S(1)}, u32[]{:S(2)}, u32[]{:S(2)}) collective-permute-start(bf16[8,144,768]{2,1,0:T(8,128)(2,1)S(1)} %bitcast.98), channel_id=1, source_target_pairs={{0,1},{1,0},{2,3},{3,2},{4,5},{5,4},{6,7},{7,6},{8,9},{9,8},{10,11... | collective-permute-start | bytes 5308424 | tf_op jit(solution)/shard_map/ppermute | solution.py:100
  152.7 6.1 %collective-permute-start.28 = (bf16[8,144,384]{2,1,0:T(8,128)(2,1)S(1)}, bf16[8,144,384]{2,1,0:T(8,128)(2,1)S(1)}, u32[]{:S(2)}, u32[]{:S(2)}) collective-permute-start(bf16[8,144,384]{2,1,0:T(8,128)(2,1)S(1)} %bitcast.100), channel_id=1, source_target_pairs={{0,1},{1,0},{2,3},{3,2},{4,5},{5,4},{6,7},{7,6},{8,9},{9,8},{10,11... | collective-permute-start | bytes 2654216 | tf_op jit(solution)/shard_map/ppermute | solution.py:100
  152.8 6.0 %collective-permute-start.29 = (bf16[8,144,384]{2,1,0:T(8,128)(2,1)S(1)}, bf16[8,144,384]{2,1,0:T(8,128)(2,1)S(1)}, u32[]{:S(2)}, u32[]{:S(2)}) collective-permute-start(bf16[8,144,384]{2,1,0:T(8,128)(2,1)S(1)} %bitcast.99), channel_id=1, source_target_pairs={{0,1},{1,0},{2,3},{3,2},{4,5},{5,4},{6,7},{7,6},{8,9},{9,8},{10,11... | collective-permute-start | bytes 2654216 | tf_op jit(solution)/shard_map/ppermute | solution.py:100
  159.0 12.3 %collective-permute-start.30 = (bf16[4,144,384]{2,1,0:T(8,128)(2,1)S(1)}, bf16[4,144,384]{2,1,0:T(8,128)(2,1)S(1)}, u32[]{:S(2)}, u32[]{:S(2)}) collective-permute-start(bf16[4,144,384]{2,1,0:T(8,128)(2,1)S(1)} %get-tuple-element.250), channel_id=1, source_target_pairs={{0,2},{1,3},{2,0},{3,1},{4,6},{5,7},{6,4},{7,5},{8,10},{9,11},{10,... | collective-permute-start | bytes 1327112 | tf_op jit(solution)/shard_map/ppermute | solution.py:100
  159.9 12.0 %collective-permute-start.31 = (bf16[4,144,384]{2,1,0:T(8,128)(2,1)S(1)}, bf16[4,144,384]{2,1,0:T(8,128)(2,1)S(1)}, u32[]{:S(2)}, u32[]{:S(2)}) collective-permute-start(bf16[4,144,384]{2,1,0:T(8,128)(2,1)S(1)} %get-tuple-element.253), channel_id=1, source_target_pairs={{0,8},{1,9},{2,10},{3,11},{4,12},{5,13},{6,14},{7,15},{8,0},{9,1},... | collective-permute-start | bytes 1327112 | tf_op jit(solution)/shard_map/ppermute | solution.py:100
  160.2 15.1 %collective-permute-start.33 = (bf16[2,96,960]{2,1,0:T(8,128)(2,1)S(1)}, bf16[2,96,960]{2,1,0:T(8,128)(2,1)S(1)}, u32[]{:S(2)}, u32[]{:S(2)}) collective-permute-start(bf16[2,96,960]{2,1,0:T(8,128)(2,1)S(1)} %get-tuple-element.264), channel_id=1, source_target_pairs={{0,4},{1,5},{2,6},{3,7},{4,0},{5,1},{6,2},{7,3},{8,12},{9,13},{10,... | collective-permute-start | bytes 1105928 | tf_op jit(solution)/shard_map/ppermute | solution.py:100
  172.3 14.9 %collective-permute-start.36 = (bf16[2,144,768]{2,1,0:T(8,128)(2,1)S(1)}, bf16[2,144,768]{2,1,0:T(8,128)(2,1)S(1)}, u32[]{:S(2)}, u32[]{:S(2)}) collective-permute-start(bf16[2,144,768]{2,1,0:T(8,128)(2,1)S(1)} %get-tuple-element.270), channel_id=1, source_target_pairs={{0,2},{1,3},{2,0},{3,1},{4,6},{5,7},{6,4},{7,5},{8,10},{9,11},{10,... | collective-permute-start | bytes 1327112 | tf_op jit(solution)/shard_map/ppermute | solution.py:100
  173.8 9.7 %collective-permute-start.37 = (bf16[2,96,960]{2,1,0:T(8,128)(2,1)S(1)}, bf16[2,96,960]{2,1,0:T(8,128)(2,1)S(1)}, u32[]{:S(2)}, u32[]{:S(2)}) collective-permute-start(bf16[2,96,960]{2,1,0:T(8,128)(2,1)S(1)} %get-tuple-element.271), channel_id=1, source_target_pairs={{0,4},{1,5},{2,6},{3,7},{4,0},{5,1},{6,2},{7,3},{8,12},{9,13},{10,... | collective-permute-start | bytes 1105928 | tf_op jit(solution)/shard_map/ppermute | solution.py:100
  175.4 9.3 %collective-permute-start.34 = (bf16[2,144,384]{2,1,0:T(8,128)(2,1)S(1)}, bf16[2,144,384]{2,1,0:T(8,128)(2,1)S(1)}, u32[]{:S(2)}, u32[]{:S(2)}) collective-permute-start(bf16[2,144,384]{2,1,0:T(8,128)(2,1)S(1)} %get-tuple-element.266), channel_id=1, source_target_pairs={{0,8},{1,9},{2,10},{3,11},{4,12},{5,13},{6,14},{7,15},{8,0},{9,1},... | collective-permute-start | bytes 663560 | tf_op jit(solution)/shard_map/ppermute | solution.py:100
  175.9 11.3 %collective-permute-start.35 = (bf16[2,144,384]{2,1,0:T(8,128)(2,1)S(1)}, bf16[2,144,384]{2,1,0:T(8,128)(2,1)S(1)}, u32[]{:S(2)}, u32[]{:S(2)}) collective-permute-start(bf16[2,144,384]{2,1,0:T(8,128)(2,1)S(1)} %get-tuple-element.269), channel_id=1, source_target_pairs={{0,16},{1,17},{2,18},{3,19},{4,20},{5,21},{6,22},{7,23},{8,24},{9,... | collective-permute-start | bytes 663560 | tf_op jit(solution)/shard_map/ppermute | solution.py:100
  187.2 28.2 %collective-permute-start.42 = (bf16[480,768]{1,0:T(8,128)(2,1)S(1)}, bf16[480,768]{1,0:T(8,128)(2,1)S(1)}, u32[]{:S(2)}, u32[]{:S(2)}) collective-permute-start(bf16[480,768]{1,0:T(8,128)(2,1)S(1)} %get-tuple-element.307), channel_id=1, source_target_pairs={{0,4},{1,5},{2,6},{3,7},{4,0},{5,1},{6,2},{7,3},{8,12},{9,13},{10,... | collective-permute-start | bytes 2211848 | tf_op jit(solution)/shard_map/ppermute | solution.py:100
  187.7 21.7 %collective-permute-start.41 = (bf16[2,144,768]{2,1,0:T(8,128)(2,1)S(1)}, bf16[2,144,768]{2,1,0:T(8,128)(2,1)S(1)}, u32[]{:S(2)}, u32[]{:S(2)}) collective-permute-start(bf16[2,144,768]{2,1,0:T(8,128)(2,1)S(1)} %get-tuple-element.302), channel_id=1, source_target_pairs={{0,2},{1,3},{2,0},{3,1},{4,6},{5,7},{6,4},{7,5},{8,10},{9,11},{10,... | collective-permute-start | bytes 1327112 | tf_op jit(solution)/shard_map/ppermute | solution.py:100
  188.4 5.7 %collective-permute-start.38 = (bf16[1,144,384]{2,1,0:T(8,128)(2,1)S(1)}, bf16[1,144,384]{2,1,0:T(8,128)(2,1)S(1)}, u32[]{:S(2)}, u32[]{:S(2)}) collective-permute-start(bf16[1,144,384]{2,1,0:T(8,128)(2,1)S(1)} %get-tuple-element.279), channel_id=1, source_target_pairs={{0,16},{1,17},{2,18},{3,19},{4,20},{5,21},{6,22},{7,23},{8,24},{9,... | collective-permute-start | bytes 331784 | tf_op jit(solution)/shard_map/ppermute | solution.py:100
  188.5 9.1 %collective-permute-start.39 = (bf16[1,144,384]{2,1,0:T(8,128)(2,1)S(1)}, bf16[1,144,384]{2,1,0:T(8,128)(2,1)S(1)}, u32[]{:S(2)}, u32[]{:S(2)}) collective-permute-start(bf16[1,144,384]{2,1,0:T(8,128)(2,1)S(1)} %get-tuple-element.282), channel_id=1, source_target_pairs={{0,2},{1,3},{2,0},{3,1},{4,6},{5,7},{6,4},{7,5},{8,10},{9,11},{10,... | collective-permute-start | bytes 331784 | tf_op jit(solution)/shard_map/ppermute | solution.py:100
  197.6 13.0 %collective-permute-start.40 = (bf16[96,960]{1,0:T(8,128)(2,1)S(1)}, bf16[96,960]{1,0:T(8,128)(2,1)S(1)}, u32[]{:S(2)}, u32[]{:S(2)}) collective-permute-start(bf16[96,960]{1,0:T(8,128)(2,1)S(1)} %get-tuple-element.301), channel_id=1, source_target_pairs={{0,16},{1,17},{2,18},{3,19},{4,20},{5,21},{6,22},{7,23},{8,24},{9,... | collective-permute-start | bytes 552968 | tf_op jit(solution)/shard_map/ppermute | solution.py:100
  199.1 13.4 %collective-permute-start.44 = (bf16[96,960]{1,0:T(8,128)(2,1)S(1)}, bf16[96,960]{1,0:T(8,128)(2,1)S(1)}, u32[]{:S(2)}, u32[]{:S(2)}) collective-permute-start(bf16[96,960]{1,0:T(8,128)(2,1)S(1)} %get-tuple-element.309), channel_id=1, source_target_pairs={{0,24},{1,25},{2,26},{3,27},{4,28},{5,29},{6,30},{7,31},{8,16},{9,... | collective-permute-start | bytes 552968 | tf_op jit(solution)/shard_map/ppermute | solution.py:100
  210.6 3.7 %collective-permute-start.43 = (bf16[128,768]{1,0:T(8,128)(2,1)S(1)}, bf16[128,768]{1,0:T(8,128)(2,1)S(1)}, u32[]{:S(2)}, u32[]{:S(2)}) collective-permute-start(bf16[128,768]{1,0:T(8,128)(2,1)S(1)} %get-tuple-element.308), channel_id=1, source_target_pairs={{0,1},{1,0},{2,3},{3,2},{4,5},{5,4},{6,7},{7,6},{8,9},{9,8},{10,11... | collective-permute-start | bytes 589832 | tf_op jit(solution)/shard_map/ppermute | solution.py:100
  210.6 10.5 %collective-permute-start.46 = (bf16[128,768]{1,0:T(8,128)(2,1)}, bf16[128,768]{1,0:T(8,128)(2,1)S(1)}, u32[]{:S(2)}, u32[]{:S(2)}) collective-permute-start(bf16[128,768]{1,0:T(8,128)(2,1)} %get-tuple-element.320), channel_id=1, source_target_pairs={{0,2},{1,3},{2,0},{3,1},{4,6},{5,7},{6,4},{7,5},{8,10},{9,11},{10,... | collective-permute-start | bytes 589832 | tf_op jit(solution)/shard_map/ppermute | solution.py:100
  211.5 10.4 %collective-permute-start.47 = (bf16[128,768]{1,0:T(8,128)(2,1)}, bf16[128,768]{1,0:T(8,128)(2,1)S(1)}, u32[]{:S(2)}, u32[]{:S(2)}) collective-permute-start(bf16[128,768]{1,0:T(8,128)(2,1)} %get-tuple-element.321), channel_id=1, source_target_pairs={{0,3},{1,2},{2,1},{3,0},{4,7},{5,6},{6,5},{7,4},{8,11},{9,10},{10,... | collective-permute-start | bytes 589832 | tf_op jit(solution)/shard_map/ppermute | solution.py:100
  212.4 7.9 %collective-permute-start.45 = (bf16[96,960]{1,0:T(8,128)(2,1)}, bf16[96,960]{1,0:T(8,128)(2,1)S(1)}, u32[]{:S(2)}, u32[]{:S(2)}) collective-permute-start(bf16[96,960]{1,0:T(8,128)(2,1)} %get-tuple-element.313), channel_id=1, source_target_pairs={{0,8},{1,9},{2,10},{3,11},{4,12},{5,13},{6,14},{7,15},{8,0},{9,1},... | collective-permute-start | bytes 552968 | tf_op jit(solution)/shard_map/ppermute | solution.py:100
  214.3 18.3 %collective-permute-start.50 = (bf16[2,144,768]{2,1,0:T(8,128)(2,1)}, bf16[2,144,768]{2,1,0:T(8,128)(2,1)S(1)}, u32[]{:S(2)}, u32[]{:S(2)}) collective-permute-start(bf16[2,144,768]{2,1,0:T(8,128)(2,1)} %get-tuple-element.324), channel_id=1, source_target_pairs={{0,8},{1,9},{2,10},{3,11},{4,12},{5,13},{6,14},{7,15},{8,0},{9,1},... | collective-permute-start | bytes 1327112 | tf_op jit(solution)/shard_map/ppermute | solution.py:100
  216.7 30.7 %all-to-all-start.3 = ((bf16[32,36,128]{2,1,0:T(8,128)(2,1)}), bf16[32,36,128]{2,1,0:T(8,128)(2,1)S(1)}, u32[]{:S(2)}, u32[]{:S(2)}) async-start(bf16[32,36,128]{2,1,0:T(8,128)(2,1)} %copy-done.38), calls=%async_computation.3 | async-start | bytes 655360 | tf_op jit(solution)/shard_map/all_to_all | solution.py:1060
  225.6 11.1 %collective-permute-start.48 = (bf16[4,96,384]{2,1,0:T(8,128)(2,1)S(1)}, bf16[4,96,384]{2,1,0:T(8,128)(2,1)S(1)}, u32[]{:S(2)}, u32[]{:S(2)}) collective-permute-start(bf16[4,96,384]{2,1,0:T(8,128)(2,1)S(1)} %get-tuple-element.322), channel_id=1, source_target_pairs={{0,4},{1,5},{2,6},{3,7},{4,0},{5,1},{6,2},{7,3},{8,12},{9,13},{10,... | collective-permute-start | bytes 884744 | tf_op jit(solution)/shard_map/ppermute | solution.py:100
  227.2 13.6 %collective-permute-start.49 = (bf16[4,96,384]{2,1,0:T(8,128)(2,1)S(1)}, bf16[4,96,384]{2,1,0:T(8,128)(2,1)S(1)}, u32[]{:S(2)}, u32[]{:S(2)}) collective-permute-start(bf16[4,96,384]{2,1,0:T(8,128)(2,1)S(1)} %get-tuple-element.323), channel_id=1, source_target_pairs={{0,8},{1,9},{2,10},{3,11},{4,12},{5,13},{6,14},{7,15},{8,0},{9,1},... | collective-permute-start | bytes 884744 | tf_op jit(solution)/shard_map/ppermute | solution.py:100
  240.9 8.6 %collective-permute-start.51 = (bf16[2,96,384]{2,1,0:T(8,128)(2,1)S(1)}, bf16[2,96,384]{2,1,0:T(8,128)(2,1)S(1)}, u32[]{:S(2)}, u32[]{:S(2)}) collective-permute-start(bf16[2,96,384]{2,1,0:T(8,128)(2,1)S(1)} %get-tuple-element.330), channel_id=1, source_target_pairs={{0,8},{1,9},{2,10},{3,11},{4,12},{5,13},{6,14},{7,15},{8,0},{9,1},... | collective-permute-start | bytes 442376 | tf_op jit(solution)/shard_map/ppermute | solution.py:100
  241.3 8.1 %collective-permute-start.52 = (bf16[2,96,384]{2,1,0:T(8,128)(2,1)S(1)}, bf16[2,96,384]{2,1,0:T(8,128)(2,1)S(1)}, u32[]{:S(2)}, u32[]{:S(2)}) collective-permute-start(bf16[2,96,384]{2,1,0:T(8,128)(2,1)S(1)} %get-tuple-element.333), channel_id=1, source_target_pairs={{0,4},{1,5},{2,6},{3,7},{4,0},{5,1},{6,2},{7,3},{8,12},{9,13},{10,... | collective-permute-start | bytes 442376 | tf_op jit(solution)/shard_map/ppermute | solution.py:100
  243.0 16.5 %collective-permute-start.55 = (bf16[1,144,768]{2,1,0:T(8,128)(2,1)S(1)}, bf16[1,144,768]{2,1,0:T(8,128)(2,1)S(1)}, u32[]{:S(2)}, u32[]{:S(2)}) collective-permute-start(bf16[1,144,768]{2,1,0:T(8,128)(2,1)S(1)} %get-tuple-element.349), channel_id=1, source_target_pairs={{0,16},{1,17},{2,18},{3,19},{4,20},{5,21},{6,22},{7,23},{8,24},{9,... | collective-permute-start | bytes 663560 | tf_op jit(solution)/shard_map/ppermute | solution.py:100
  249.5 13.0 %collective-permute-start.53 = (bf16[1,96,384]{2,1,0:T(8,128)(2,1)S(1)}, bf16[1,96,384]{2,1,0:T(8,128)(2,1)S(1)}, u32[]{:S(2)}, u32[]{:S(2)}) collective-permute-start(bf16[1,96,384]{2,1,0:T(8,128)(2,1)S(1)} %get-tuple-element.345), channel_id=1, source_target_pairs={{0,16},{1,17},{2,18},{3,19},{4,20},{5,21},{6,22},{7,23},{8,24},{9,... | collective-permute-start | bytes 221192 | tf_op jit(solution)/shard_map/ppermute | solution.py:100
  250.1 13.4 %collective-permute-start.54 = (bf16[1,96,384]{2,1,0:T(8,128)(2,1)S(1)}, bf16[1,96,384]{2,1,0:T(8,128)(2,1)S(1)}, u32[]{:S(2)}, u32[]{:S(2)}) collective-permute-start(bf16[1,96,384]{2,1,0:T(8,128)(2,1)S(1)} %get-tuple-element.348), channel_id=1, source_target_pairs={{0,16},{1,17},{2,18},{3,19},{4,20},{5,21},{6,22},{7,23},{8,24},{9,... | collective-permute-start | bytes 221192 | tf_op jit(solution)/shard_map/ppermute | solution.py:100
  252.6 14.9 %all-to-all-start.4 = ((f32[32,8,128]{2,1,0:T(8,128)}), f32[32,8,128]{2,1,0:T(8,128)S(1)}, u32[]{:S(2)}, u32[]{:S(2)}) async-start(f32[32,8,128]{2,1,0:T(8,128)} %get-tuple-element.354), calls=%async_computation.4 | async-start | bytes 262144 | tf_op jit(solution)/shard_map/all_to_all | solution.py:1173
  255.2 8.3 %collective-permute-start.56 = (bf16[96,384]{1,0:T(8,128)(2,1)S(1)}, bf16[96,384]{1,0:T(8,128)(2,1)S(1)}, u32[]{:S(2)}, u32[]{:S(2)}) collective-permute-start(bf16[96,384]{1,0:T(8,128)(2,1)S(1)} %get-tuple-element.403), channel_id=1, source_target_pairs={{0,1},{1,0},{2,3},{3,2},{4,5},{5,4},{6,7},{7,6},{8,9},{9,8},{10,11... | collective-permute-start | bytes 221192 | tf_op jit(solution)/shard_map/ppermute | solution.py:100
  255.4 8.1 %collective-permute-start.57 = (bf16[96,384]{1,0:T(8,128)(2,1)S(1)}, bf16[96,384]{1,0:T(8,128)(2,1)S(1)}, u32[]{:S(2)}, u32[]{:S(2)}) collective-permute-start(bf16[96,384]{1,0:T(8,128)(2,1)S(1)} %get-tuple-element.402), channel_id=1, source_target_pairs={{0,2},{1,3},{2,0},{3,1},{4,6},{5,7},{6,4},{7,5},{8,10},{9,11},{10,... | collective-permute-start | bytes 221192 | tf_op jit(solution)/shard_map/ppermute | solution.py:100
  259.5 4.0 %collective-permute-start.58 = (bf16[96,384]{1,0:T(8,128)(2,1)S(1)}, bf16[96,384]{1,0:T(8,128)(2,1)S(1)}, u32[]{:S(2)}, u32[]{:S(2)}) collective-permute-start(bf16[96,384]{1,0:T(8,128)(2,1)S(1)} %get-tuple-element.401), channel_id=1, source_target_pairs={{0,3},{1,2},{2,1},{3,0},{4,7},{5,6},{6,5},{7,4},{8,11},{9,10},{10,... | collective-permute-start | bytes 221192 | tf_op jit(solution)/shard_map/ppermute | solution.py:100
  (89 other events, 855.3 us)
